TPU v7x, 32 devices: a whole 2x2x4 slice. The times are simulated.
32 devices in a mesh: mem: 8 (over z, core), row: 4 (over y, x).
Axes of the slice: x: 2, y: 2, z: 4, core: 2. Of those that a mesh axis runs over, the one named last changes fastest.
Arguments:
- members: bfloat16 [16, 5, 64, 4096], P('mem', None, 'row'), may hold values from -6 to 6
- enc_first: bfloat16 [64, 5, 3, 3], replicated, may hold values from -0.875 to 0.875
- enc_second: bfloat16 [64, 64, 3, 3], replicated, may hold values from -0.25 to 0.25
- enc_third: bfloat16 [16, 64, 3, 3], replicated, may hold values from -0.25 to 0.25
- mix_weight: bfloat16 [32, 256], replicated, may hold values from -0.375 to 0.375
- dec_first: bfloat16 [32, 32, 4, 4], replicated, may hold values from -0.5 to 0.5
- dec_second: bfloat16 [16, 32, 4, 4], replicated, may hold values from -0.5 to 0.5
Outputs:
- output_field: bfloat16 [16, 64, 4096], P(None, 'row', 'mem')
All inputs are finite; a program needn't handle non-finite values.
Results may differ from a plain program's by a relative error of at most 0.029.
Values may be sent and summed in bfloat16 or wider, within the bound.
No kernel may reach another device: no remote copies, remote signals or barrier semaphores. Data moves between devices by JAX's collectives and lax.ppermute only.
A program may use at most 128 MiB of HBM per device.

v0:
```python
import functools

import jax
import jax.numpy as jnp
import numpy as np
from jax import lax
from jax.experimental import pallas as pl
from jax.experimental.pallas import tpu as pltpu
from jax.sharding import PartitionSpec as P

BF = jnp.bfloat16
F32 = jnp.float32
CH_BOT = 16
UP = 5
DOWN = 2
TRANSPOSED = [(p, i, 2 * i - p) for p in range(2) for i in range(3) if 0 <= 2 * i - p < 4]


def dot(a, b):
    return lax.dot_general(a, b, (((1,), (0,)), ((), ())), preferred_element_type=F32)


def dot_t(a, b):
    return lax.dot_general(a, b, (((0,), (0,)), ((), ())), preferred_element_type=F32)


def silu_of_half(y):
    return y + y * jnp.tanh(y)


def spread(step, tile):
    one = np.zeros((step * tile, step * tile), np.float32)
    for q in range(step):
        for c in range(tile):
            one[step * c + q, q * tile + c] = 1
    return one


def padded(n, to):
    return -(-n // to) * to


def first_selectors(members, channels, rows):
    half = rows // 2
    own = np.zeros((3, 2, 48, 5 * channels * rows), np.float32)
    per = [padded(members * channels * n, 8) for n in (UP, DOWN)]
    total = [padded(5 * n, 16) for n in per]
    down = np.zeros((members, 3, 2, 48, total[0]), np.float32)
    up = np.zeros((members, 2, 48, total[1]), np.float32)
    for pc in range(2):
        for c in range(channels):
            for dr in range(3):
                for dc in range(3):
                    tap = (c * 3 + dr) * 3 + dc
                    ph = 2 * pc + dc
                    for kind, h in enumerate((1, 0, half)):
                        row = 2 * h + dr - 1
                        if 0 <= row < rows:
                            own[kind, pc, tap, (ph * channels + c) * rows + row] = 1
                    for m in range(members):
                        for kind, h in enumerate((-2, -1, 0)):
                            row = 2 * h + dr - 1
                            if row < 0:
                                down[m, kind, pc, tap, ph * per[0] + (m * channels + c) * UP + row + UP] = 1
                        row = 2 * half + dr - 1
                        if row >= rows:
                            up[m, pc, tap, ph * per[1] + (m * channels + c) * DOWN + row - rows] = 1
    return own, down, up, per, total


def shift_right(v):
    return jnp.concatenate([jnp.zeros_like(v[:, :1]), v[:, :-1]], axis=1)


def shift_left(v):
    return jnp.concatenate([v[:, 1:], jnp.zeros_like(v[:, :1])], axis=1)


def put_hidden(ref, m, at, value):
    v = value.astype(BF)
    even, odd = v[0:64], v[64:128]
    ref[m, at, 64:128, :] = even
    ref[m, at, 128:192, :] = odd
    ref[m, at, 0:64, :] = shift_right(odd)
    ref[m, at, 192:256, :] = shift_left(even)


def slab(ref, m, first, count):
    return ref[m, first : first + count].reshape(count * 256, ref.shape[3])


def place_halo(source, spreader, y_ref, count, per):
    tile = spreader.shape[0] // 4
    z = dot(source, spreader)
    y_ref[...] = jnp.zeros_like(y_ref)
    for t in range(y_ref.shape[1] // tile):
        for q in range(4):
            y_ref[(q + 1) * per : (q + 1) * per + count, t * tile : (t + 1) * tile] = z[
                t * count : (t + 1) * count, q * tile : (q + 1) * tile
            ]
    y_ref[0:per, :] = shift_right(y_ref[4 * per : 5 * per, :])
    return y_ref[...].astype(BF)


def pack_kernel(members, channels, rows, x_ref, down_ref, up_ref, d_scr, u_scr):
    wide = x_ref.shape[1]
    lanes = down_ref.shape[1]
    nd, nu = members * channels * UP, members * channels * DOWN
    for t in range(wide // lanes):
        for g in range(members * channels):
            block = x_ref[g * rows : (g + 1) * rows, t * lanes : (t + 1) * lanes].astype(F32)
            d_scr[t * nd + g * UP : t * nd + (g + 1) * UP, :] = block[rows - UP : rows]
            u_scr[t * nu + g * DOWN : t * nu + (g + 1) * DOWN, :] = block[0:DOWN]
    down_ref[...] = d_scr[...].astype(BF)
    up_ref[...] = u_scr[...].astype(BF)


def inner_kernel(
    members, channels, rows,
    x_ref, w1_ref, w2_ref, w3_ref, mix_ref, own_ref, down_ref, up_ref, p_ref, d1_ref, d2_ref,
    top_pre, low_pre, top_h1, low_h1, top_v, low_v, mixed_ref, w2_big, w3_big, w1_down, w1_up, wd1, wd2,
    y_ref, w1_own, h1_ref,
):
    half = rows // 2
    wide = x_ref.shape[1]
    tile = p_ref.shape[0] // 4
    cr = channels * rows
    spreader = p_ref[...]
    for t in range(wide // (4 * tile)):
        z = dot(x_ref[:, 4 * tile * t : 4 * tile * (t + 1)], spreader).astype(BF)
        for q in range(4):
            for m in range(members):
                y_ref[m, (q + 1) * cr : (q + 2) * cr, t * tile : (t + 1) * tile] = z[
                    m * cr : (m + 1) * cr, q * tile : (q + 1) * tile
                ]
    for m in range(members):
        y_ref[m, 0:cr, :] = shift_right(y_ref[m, 4 * cr : 5 * cr, :])

    w1 = w1_ref[...]
    for pc in range(2):
        lanes = slice(pc * 64, (pc + 1) * 64)
        for kind in range(3):
            w1_own[kind, lanes, :] = (0.5 * dot_t(w1, own_ref[kind, pc])).astype(BF)
        for m in range(members):
            for kind in range(3):
                w1_down[m, kind * 128 + pc * 64 : kind * 128 + (pc + 1) * 64, :] = (
                    0.5 * dot_t(w1, down_ref[m, kind, pc])
                ).astype(BF)
            w1_up[m, lanes, :] = (0.5 * dot_t(w1, up_ref[m, pc])).astype(BF)
    w2_big[...] = jnp.zeros_like(w2_big)
    for orow in range(2):
        for ocol in range(2):
            for dr in range(3):
                for dc in range(3):
                    w2_big[
                        (orow * 2 + ocol) * 64 : (orow * 2 + ocol + 1) * 64,
                        (orow + dr) * 256 + (ocol + dc) * 64 : (orow + dr) * 256 + (ocol + dc + 1) * 64,
                    ] = (0.5 * w2_ref[dr * 3 + dc].astype(F32)).astype(BF)
    w3_big[...] = jnp.zeros_like(w3_big)
    for dr, place, base in ((1, 0, 0), (2, 0, 128), (0, 2, 128)):
        for dc, shifted_out, at in ((1, 0, 0), (2, 0, 64), (0, 1, 64)):
            w3_big[(place + shifted_out) * 16 : (place + shifted_out + 1) * 16, base + at : base + at + 64] = (
                0.5 * w3_ref[dr * 3 + dc].astype(F32)
            ).astype(BF)
    wd1[...] = jnp.zeros_like(wd1)
    wd2[...] = jnp.zeros_like(wd2)
    for pr, rr, tr in TRANSPOSED:
        for pc, cc, tc in TRANSPOSED:
            wd1[(pr * 2 + pc) * 32 : (pr * 2 + pc + 1) * 32, (rr * 3 + cc) * 32 : (rr * 3 + cc + 1) * 32] = (
                0.5 * d1_ref[tr * 4 + tc].astype(F32)
            ).astype(BF)
            for q in range(2):
                at = pr * 4 + 2 * q + pc
                to = rr * 4 + q + cc
                wd2[at * 16 : (at + 1) * 16, to * 32 : (to + 1) * 32] = d2_ref[tr * 4 + tc]

    for m in range(members):
        base = w1_own[0]
        for h in range(1, half):
            w = base if h == 1 else pltpu.roll(base.astype(F32), 2 * (h - 1), 1).astype(BF)
            put_hidden(h1_ref, m, h - 1, silu_of_half(dot(w, y_ref[m])))
        top_pre[m] = dot(w1_own[1], y_ref[m])
        low_pre[m] = dot(w1_own[2], y_ref[m])
        top_h1[m] = h1_ref[m, 0:2]
        low_h1[m] = h1_ref[m, half - 4 : half - 1]

    mids = []
    for m in range(members):
        carry = None
        for a in range(2, half - 2, 2):
            h2 = silu_of_half(dot(w2_big[...], slab(h1_ref, m, a - 2, 4))).astype(BF)
            v = dot(w3_big[...], h2)
            if a == 2:
                top_v[m] = v[0:32]
            else:
                w = v[0:32] + carry
                mids.append((a // 2, m, silu_of_half(w[0:16] + shift_right(w[16:32])).astype(BF)))
            carry = v[32:64]
        low_v[m] = carry
    for r in range(2, half // 2 - 1):
        mixed_ref[r - 2] = dot(mix_ref[...], jnp.concatenate([b for s, _, b in mids if s == r], axis=0))


def low_kernel(
    members, channels, half, per,
    got_ref, p_ref, w1_ref, pre_ref, h1_in, w2_big, w3_big, v_ref, mix_ref, mixed_ref, y_ref, h1_ref,
):
    below = jnp.where(lax.axis_index("row") == lax.axis_size("row") - 1, 0.0, 1.0).astype(F32)
    y = place_halo(got_ref[...], p_ref[...], y_ref, members * channels * DOWN, per)
    parts = []
    for m in range(members):
        h1_ref[m, 0:3] = h1_in[m]
        put_hidden(h1_ref, m, 3, silu_of_half((dot(w1_ref[m], y) + pre_ref[m]) * below))
        h2 = silu_of_half(dot(w2_big[...], slab(h1_ref, m, 0, 4))).astype(BF)
        w = dot(w3_big[0:32], h2) + v_ref[m]
        parts.append(silu_of_half(w[0:16] + shift_right(w[16:32])).astype(BF))
    mixed_ref[...] = dot(mix_ref[...], jnp.concatenate(parts, axis=0))


def top_kernel(
    members, channels, half, per, nb,
    got_ref, p_ref, w1_ref, pre_ref, h1_in, w2_big, w3_big, v_ref, mix_ref, mid_ref, low_ref,
    keep_ref, send_ref, y_ref, h1_ref, mixed_ref,
):
    above = jnp.where(lax.axis_index("row") == 0, 0.0, 1.0).astype(F32)
    y = place_halo(got_ref[...], p_ref[...], y_ref, members * channels * UP, per)
    first, second = [], []
    for m in range(members):
        h1_ref[m, 3:5] = h1_in[m]
        fresh = dot(w1_ref[m], y)
        put_hidden(h1_ref, m, 0, silu_of_half(fresh[0:128]))
        put_hidden(h1_ref, m, 1, silu_of_half(fresh[128:256]))
        put_hidden(h1_ref, m, 2, silu_of_half(fresh[256:384] + pre_ref[m]))
        h2 = silu_of_half(dot(w2_big[0:128, 0:768], slab(h1_ref, m, 0, 3)) * above).astype(BF)
        carry = dot(w3_big[32:64, 128:256], h2)
        h2 = silu_of_half(dot(w2_big[...], slab(h1_ref, m, 1, 4))).astype(BF)
        v = dot(w3_big[...], h2)
        w = v[0:32] + carry
        first.append(silu_of_half(w[0:16] + shift_right(w[16:32])).astype(BF))
        w = v[32:64] + v_ref[m]
        second.append(silu_of_half(w[0:16] + shift_right(w[16:32])).astype(BF))
    cols = y_ref.shape[1]
    quarter = half // 2
    margin = jnp.zeros((quarter * 32, 128), F32)
    mixed_ref[:, 0:128] = margin
    mixed_ref[:, 128 + cols : 256 + cols] = margin
    mixed_ref[0:32, 128 : 128 + cols] = dot(mix_ref[...], jnp.concatenate(first, axis=0))
    mixed_ref[32:64, 128 : 128 + cols] = dot(mix_ref[...], jnp.concatenate(second, axis=0))
    for r in range(2, quarter - 1):
        mixed_ref[r * 32 : (r + 1) * 32, 128 : 128 + cols] = mid_ref[r - 2]
    mixed_ref[(quarter - 1) * 32 : quarter * 32, 128 : 128 + cols] = low_ref[...]

    me = lax.axis_index("mem")
    slots = lax.axis_size("mem") // 2
    tall = quarter * 32
    def lanes_from(lane):
        base = pl.multiple_of(lane // 128 * 128, 128)
        v = mixed_ref[:, pl.ds(base, 128)]
        return v if nb % 128 == 0 else pltpu.roll(v, (128 - lane % 128) % 128, 1)

    lane_at = lax.broadcasted_iota(jnp.int32, (tall, 128), 1)
    edges = jnp.zeros((tall, 128), F32)
    for side, ref in enumerate((keep_ref, send_ref)):
        for k in range(slots):
            block = me ^ (2 * k + side)
            start = 128 + block * nb
            ref[k, 0:tall, :] = lanes_from(start).astype(BF)
            if nb % 128 == 0:
                left = mixed_ref[:, pl.ds(pl.multiple_of(start - 128, 128), 128)][:, 127:128]
            else:
                left = lanes_from(start - 1)[:, 0:1]
            right = lanes_from(start + nb)[:, 0:1]
            at = 2 * (side * slots + k)
            edges = jnp.where(lane_at == at, left, edges)
            edges = jnp.where(lane_at == at + 1, right, edges)
    turned = edges.T
    for side, ref in enumerate((keep_ref, send_ref)):
        for k in range(slots):
            at = 2 * (side * slots + k)
            ref[k, tall : tall + 16, :] = jnp.concatenate(
                [turned[at : at + 2], jnp.zeros((14, 128), F32)], axis=0
            ).astype(BF)


def pair_kernel(keep_ref, got_ref, own_ref, *out_refs):
    own_ref[...] = keep_ref[0].astype(F32) + got_ref[0].astype(F32)
    for k, ref in enumerate(out_refs):
        ref[...] = (keep_ref[k + 1].astype(F32) + got_ref[k + 1].astype(F32)).astype(BF)


def latent_kernel(nb, quarter, own_ref, *refs):
    ext_ref, top_ref, low_ref = refs[-3:]
    total = own_ref[...]
    for ref in refs[:-3]:
        total = total + ref[...].astype(F32)
    latent = silu_of_half(0.5 * total)
    tall = quarter * 32
    turned = jnp.concatenate([latent[tall : tall + 16], jnp.zeros((112, 128), F32)], axis=0).T
    ext = ext_ref.shape[2]
    for r in range(quarter):
        rows = slice(r * 32, (r + 1) * 32)
        line = jnp.concatenate(
            [
                latent[rows, 0:nb],
                turned[rows, 1:2],
                jnp.zeros((32, ext - nb - 2), F32),
                turned[rows, 0:1],
            ],
            axis=1,
        )
        put_latent(ext_ref, r, line)
        if r == 0:
            top_ref[...] = line.astype(BF)
        if r == quarter - 1:
            low_ref[...] = line.astype(BF)


def put_latent(ref, at, line):
    ext = line.shape[1]
    ref[at, 0:32, :] = pltpu.roll(line, 1, 1).astype(BF)
    ref[at, 32:64, :] = line.astype(BF)
    ref[at, 64:96, :] = pltpu.roll(line, ext - 1, 1).astype(BF)


def decoder_kernel(nb, ext_ref, above_ref, below_ref, w1_ref, w2_ref, p_ref, r_ref, out_ref, l_ref, u_ref, g_ref):
    row_at, mem_at = lax.axis_index("row"), lax.axis_index("mem")
    row_last, mem_last = lax.axis_size("row") - 1, lax.axis_size("mem") - 1
    rows, _, wide = ext_ref.shape
    l_ref[0] = jnp.zeros_like(l_ref[0])
    l_ref[rows + 3] = jnp.zeros_like(l_ref[0])
    put_latent(l_ref, 1, above_ref[...].astype(F32))
    l_ref[2 : rows + 2] = ext_ref[...]
    put_latent(l_ref, rows + 2, below_ref[...].astype(F32))
    w1, w2 = w1_ref[...], w2_ref[...]
    lane = lax.broadcasted_iota(jnp.int32, (32, wide), 1)
    keep_odd = jnp.where((lane == wide - 1) & (mem_at == 0), 0.0, 1.0).astype(F32)
    keep_even = jnp.where((lane == nb) & (mem_at == mem_last), 0.0, 1.0).astype(F32)
    keep_first = jnp.where(row_at == 0, 0.0, 1.0).astype(F32)
    keep_last = jnp.where(row_at == row_last, 0.0, 1.0).astype(F32)
    for a in range(-1, rows + 1):
        v = silu_of_half(dot(w1, l_ref[a + 1 : a + 4].reshape(288, wide)))
        for pr in range(2):
            row = 2 * a + pr
            if not -1 <= row <= 2 * rows:
                continue
            even = v[pr * 64 : pr * 64 + 32] * keep_even
            odd = v[pr * 64 + 32 : pr * 64 + 64] * keep_odd
            if row == -1:
                even, odd = even * keep_first, odd * keep_first
            if row == 2 * rows:
                even, odd = even * keep_last, odd * keep_last
            at = (row + 1) * 128
            u_ref[at : at + 32, :] = pltpu.roll(odd, 1, 1)[:, 0:nb].astype(BF)
            u_ref[at + 32 : at + 64, :] = even[:, 0:nb].astype(BF)
            u_ref[at + 64 : at + 96, :] = odd[:, 0:nb].astype(BF)
            u_ref[at + 96 : at + 128, :] = pltpu.roll(even, wide - 1, 1)[:, 0:nb].astype(BF)
    for a in range(2 * rows):
        v = dot(w2, u_ref[a * 128 : (a + 3) * 128, :]).astype(BF)
        for pr in range(2):
            for ph in range(4):
                g_ref[(2 * a + pr) * 16 : (2 * a + pr + 1) * 16, ph * nb : (ph + 1) * nb] = v[
                    (pr * 4 + ph) * 16 : (pr * 4 + ph + 1) * 16
                ]
    g = dot(r_ref[...], g_ref[...]).astype(BF)
    out_ref[...] = dot(g, p_ref[...]).astype(BF).reshape(out_ref.shape)


def shifted(value, axis, by):
    peers = lax.axis_size(axis)
    return lax.ppermute(value, axis, [(i, i + by) for i in range(peers) if 0 <= i + by < peers])


def swapped(value, by):
    return lax.ppermute(value, "mem", [(i, i ^ by) for i in range(lax.axis_size("mem"))])


VMEM = pl.BlockSpec(memory_space=pltpu.VMEM)
PARAMS = pltpu.CompilerParams(vmem_limit_bytes=56 * 2**20)


def call(kernel, outs, scratch, *operands):
    return pl.pallas_call(
        kernel,
        out_shape=[jax.ShapeDtypeStruct(*o) for o in outs],
        in_specs=[VMEM] * len(operands),
        out_specs=[VMEM] * len(outs),
        scratch_shapes=[pltpu.VMEM(*s) for s in scratch],
        compiler_params=PARAMS,
    )(*operands)


def per_device(members, enc_first, enc_second, enc_third, mix_weight, dec_first, dec_second):
    count, channels, rows, wide = members.shape
    own, sel_down, sel_up, per, total = first_selectors(count, channels, rows)
    half, quarter = rows // 2, rows // 4
    cols = wide // 4
    peers = lax.axis_size("mem")
    nb = cols // peers
    tile = 128
    lanes = 4 * tile
    chunks = wide // lanes
    x = members.reshape(count * channels * rows, wide)
    nd, nu = count * channels * UP, count * channels * DOWN
    pack = functools.partial(pack_kernel, count, channels, rows)
    sizes = [(nd * chunks, lanes), (nu * chunks, lanes)]
    down, up = call(pack, [(s, BF) for s in sizes], [(s, F32) for s in sizes], x)
    up = shifted(up, "row", -1)
    down = shifted(down, "row", 1)

    w1 = jnp.pad(enc_first.transpose(1, 2, 3, 0).reshape(channels * 9, 64), ((0, 3), (0, 0)))
    w2 = enc_second.transpose(2, 3, 0, 1).reshape(9, 64, 64)
    w3 = enc_third.transpose(2, 3, 0, 1).reshape(9, 16, 64)
    d1 = dec_first.transpose(2, 3, 0, 1).reshape(16, 32, 32)
    d2 = dec_second.transpose(2, 3, 0, 1).reshape(16, 16, 32)
    mix = lax.dynamic_slice_in_dim(mix_weight, lax.axis_index("mem") * (count * CH_BOT), count * CH_BOT, 1)
    apart = jnp.asarray(spread(4, tile), BF)
    top_pre, low_pre, top_h1, low_h1, top_v, low_v, mid, w2_big, w3_big, w1_down, w1_up, wd1, wd2 = call(
        functools.partial(inner_kernel, count, channels, rows),
        [
            ((count, 128, cols), F32),
            ((count, 128, cols), F32),
            ((count, 2, 256, cols), BF),
            ((count, 3, 256, cols), BF),
            ((count, 32, cols), F32),
            ((count, 32, cols), F32),
            ((quarter - 3, 32, cols), F32),
            ((256, 1024), BF),
            ((64, 256), BF),
            ((count, 384, total[0]), BF),
            ((count, 128, total[1]), BF),
            ((128, 288), BF),
            ((128, 384), BF),
        ],
        [
            ((count, 5 * channels * rows, cols), BF),
            ((3, 128, 5 * channels * rows), BF),
            ((count, half - 1, 256, cols), BF),
        ],
        x, w1, w2, w3, mix, jnp.asarray(own, BF), jnp.asarray(sel_down, BF), jnp.asarray(sel_up, BF), apart, d1, d2,
    )
    (low,) = call(
        functools.partial(low_kernel, count, channels, half, per[1]),
        [((32, cols), F32)],
        [((total[1], cols), F32), ((count, 4, 256, cols), BF)],
        up, apart, w1_up, low_pre, low_h1, w2_big, w3_big, low_v, mix,
    )
    slots = peers // 2
    chunk = (quarter * 32 + 16, 128)
    keep, send = call(
        functools.partial(top_kernel, count, channels, half, per[0], nb),
        [((slots,) + chunk, BF)] * 2,
        [((total[0], cols), F32), ((count, 5, 256, cols), BF), ((quarter * 32, cols + 256), F32)],
        down, apart, w1_down, top_pre, top_h1, w2_big, w3_big, top_v, mix, mid, low,
    )
    got = swapped(send, 1)
    mine, *others = call(pair_kernel, [(chunk, F32)] + [(chunk, BF)] * (slots - 1), [], keep, got)
    others = [swapped(o, 2 * (k + 1)) for k, o in enumerate(others)]
    ext = padded(nb + 2, 128)
    latent, top, low = call(
        functools.partial(latent_kernel, nb, quarter),
        [((quarter, 96, ext), BF), ((32, ext), BF), ((32, ext), BF)],
        [],
        mine, *others,
    )
    above = shifted(low, "row", 1)
    below = shifted(top, "row", -1)
    reorder = np.zeros((16 * rows, 16 * rows), np.float32)
    for r in range(rows):
        for level in range(16):
            reorder[level * rows + r, r * 16 + level] = 1
    (out,) = call(
        functools.partial(decoder_kernel, nb),
        [((16, rows, 4 * nb), BF)],
        [((quarter + 4, 96, ext), BF), ((128 * (half + 2), nb), BF), ((16 * rows, 4 * nb), BF)],
        latent, above, below, wd1, wd2, jnp.asarray(spread(4, nb).T, BF), jnp.asarray(reorder, BF),
    )
    return out


def solution(mesh):
    placed = (P("mem", None, "row", None), P(), P(), P(), P(), P(), P())
    return jax.shard_map(
        per_device, mesh=mesh, in_specs=placed, out_specs=P(None, "row", "mem"), check_vma=False
    )
```

profile of v0, /device:TPU:0, one launch (start us, length us, event | category | flops | bytes accessed | tf_op | source)
XLA Modules:
  0.0 71.7 jit_solution(10236019502322850861)
XLA Ops:
  0.0 0.0 copy-start
  0.0 2.4 %shard_map.127 = (bf16[400,512]{1,0:T(8,128)(2,1)}, bf16[160,512]{1,0:T(8,128)(2,1)}) custom-call(bf16[160,4096]{1,0:T(8,128)(2,1)} %bitcast.12), custom_call_target="tpu_custom_call" | custom-call | tf_op jit(solution)/shard_map/pallas_call | solution.py:382
  2.4 4.9 %collective-permute-start = (bf16[400,512]{1,0:T(8,128)(2,1)}, bf16[400,512]{1,0:T(8,128)(2,1)S(1)}, u32[]{:S(2)}, u32[]{:S(2)}) collective-permute-start(bf16[400,512]{1,0:T(8,128)(2,1)} %get-tuple-element.29), channel_id=1, source_target_pairs={{0,1},{1,2},{2,3},{4,5},{5,6},{6,7},{8,9},{9,10},{10,11},{12,13},{... | collective-permute-start | bytes 1228808 | tf_op jit(solution)/shard_map/ppermute | solution.py:370
  7.3 1.3 %collective-permute-start.1 = (bf16[160,512]{1,0:T(8,128)(2,1)}, bf16[160,512]{1,0:T(8,128)(2,1)S(1)}, u32[]{:S(2)}, u32[]{:S(2)}) collective-permute-start(bf16[160,512]{1,0:T(8,128)(2,1)} %get-tuple-element.37), channel_id=1, source_target_pairs={{1,0},{2,1},{3,2},{5,4},{6,5},{7,6},{9,8},{10,9},{11,10},{13,12},{... | collective-permute-start | bytes 491528 | tf_op jit(solution)/shard_map/ppermute | solution.py:370
  8.6 1.6 %copy.14 = bf16[4,4,32,32]{3,2,1,0:T(8,128)(2,1)} copy(bf16[4,4,32,32]{3,1,0,2:T(4,128)(2,1)} %bitcast.17) | data formatting | bytes 65536 | tf_op jit(solution)/shard_map/transpose | solution.py:413
  10.2 1.5 %copy.15 = bf16[4,4,16,32]{3,2,1,0:T(8,128)(2,1)} copy(bf16[4,4,16,32]{3,1,0,2:T(4,128)(2,1)} %bitcast.18) | data formatting | bytes 32768 | tf_op jit(solution)/shard_map/transpose | solution.py:414
  11.7 0.7 %reshape.19 = bf16[45,64]{1,0:T(8,128)(2,1)S(1)} reshape(bf16[5,3,3,64]{3,2,1,0:T(4,128)(2,1)} %bitcast.20) | data formatting | bytes 11520 | tf_op jit(solution)/shard_map/reshape | solution.py:410
  12.4 0.6 pad.4.w1_ref
  13.0 0.0 copy-done
  13.0 0.7 constant_dynamic-slice_fusion.mix_ref
  13.7 12.4 %shard_map.128 = (f32[2,128,1024]{2,1,0:T(8,128)}, f32[2,128,1024]{2,1,0:T(8,128)}, bf16[2,2,256,1024]{3,2,1,0:T(8,128)(2,1)}, bf16[2,3,256,1024]{3,2,1,0:T(8,12...) custom-call(bf16[160,4096]{1,0:T(8,128)(2,1)} %bitcast.13, ...), custom_call_target="tpu_custom_call" | custom-call | tf_op jit(solution)/shard_map/pallas_call | solution.py:382
  26.1 0.0 collective-permute-done.1.got_ref
  26.1 0.0 copy-start.2
  26.1 0.7 copy-done.2
  26.8 5.5 %shard_map.129.low_ref = f32[32,1024]{1,0:T(8,128)} custom-call(bf16[160,512]{1,0:T(8,128)(2,1)} %copy-done.2, bf16[512,512]{1,0:T(8,128)(2,1)} %constant.26.clone.p_ref, bf16[2,128,128]{2,1,0:T(8,128)(2,1)} %get-tuple-element.38.w1_ref, f32[2,128,1024]{2,1,0:T(8,128)} %get-tuple-element.39.pre_ref, bf16[2,3,256,1024]{3,2,1,0:T(8,128)(2,1)} %get-tuple-element.40.h1_in, ...), custom_call_target="tpu_custom_call" | custom-call | tf_op jit(solution)/shard_map/pallas_call | solution.py:382
  32.3 0.0 collective-permute-done.got_ref
  32.3 0.0 copy-start.1
  32.3 0.8 %copy-done.1 = bf16[400,512]{1,0:T(8,128)(2,1)} copy-done((bf16[400,512]{1,0:T(8,128)(2,1)}, bf16[400,512]{1,0:T(8,128)(2,1)S(1)}, u32[]{:S(2)}) %copy-start.1) | copy-done | bytes 409624
  33.1 7.7 %shard_map.130 = (bf16[4,144,128]{2,1,0:T(8,128)(2,1)}, bf16[4,144,128]{2,1,0:T(8,128)(2,1)}) custom-call(bf16[400,512]{1,0:T(8,128)(2,1)} %copy-done.1, bf16[512,512]{1,0:T(8,128)(2,1)} %constant.26.clone.p_ref, bf16[2,384,288]{2,1,0:T(8,128)(2,1)} %get-tuple-element.30.w1_ref, f32[2,128,1024]{2,1,0:T(8,128)} %get-tuple-element.31.pre_ref, ...), custom_call_target="tpu_custom_call" | custom-call | tf_op jit(solution)/shard_map/pallas_call | solution.py:382
  40.8 0.0 collective-permute-start.2
  40.8 1.6 %collective-permute-done.2.got_ref = bf16[4,144,128]{2,1,0:T(8,128)(2,1)S(1)} collective-permute-done((bf16[4,144,128]{2,1,0:T(8,128)(2,1)}, bf16[4,144,128]{2,1,0:T(8,128)(2,1)S(1)}, u32[]{:S(2)}, u32[]{:S(2)}) %collective-permute-start.2) | collective-permute-done | bytes 147488 | tf_op jit(solution)/shard_map/ppermute | solution.py:374
  42.3 0.0 copy-start.3
  42.3 0.7 copy-done.3
  43.0 1.7 %shard_map.131 = (f32[144,128]{1,0:T(8,128)}, bf16[144,128]{1,0:T(8,128)(2,1)}, bf16[144,128]{1,0:T(8,128)(2,1)}, bf16[144,128]{1,0:T(8,128)(2,1)}) custom-call(bf16[4,144,128]{2,1,0:T(8,128)(2,1)} %get-tuple-element.42.keep_ref, bf16[4,144,128]{2,1,0:T(8,128)(2,1)} %copy-done.3), custom_call_target="tpu_custom_call" | custom-call | tf_op jit(solution)/shard_map/pallas_call | solution.py:382
  44.7 1.6 %collective-permute-start.3 = (bf16[144,128]{1,0:T(8,128)(2,1)}, bf16[144,128]{1,0:T(8,128)(2,1)S(1)}, u32[]{:S(2)}, u32[]{:S(2)}) collective-permute-start(bf16[144,128]{1,0:T(8,128)(2,1)} %get-tuple-element.45), channel_id=1, source_target_pairs={{0,8},{4,12},{8,0},{12,4},{16,24},{20,28},{24,16},{28,20},{1,9},{5... | collective-permute-start | bytes 110600 | tf_op jit(solution)/shard_map/ppermute | solution.py:374
  46.3 2.6 %collective-permute-start.4 = (bf16[144,128]{1,0:T(8,128)(2,1)}, bf16[144,128]{1,0:T(8,128)(2,1)S(1)}, u32[]{:S(2)}, u32[]{:S(2)}) collective-permute-start(bf16[144,128]{1,0:T(8,128)(2,1)} %get-tuple-element.46), channel_id=1, source_target_pairs={{0,16},{4,20},{8,24},{12,28},{16,0},{20,4},{24,8},{28,12},{1,17},{... | collective-permute-start | bytes 110600 | tf_op jit(solution)/shard_map/ppermute | solution.py:374
  48.8 0.2 collective-permute-start.5
  49.1 0.0 collective-permute-done.3.refs_0_
  49.1 0.0 copy-start.4
  49.1 3.0 %collective-permute-done.4.refs_1_ = bf16[144,128]{1,0:T(8,128)(2,1)S(1)} collective-permute-done((bf16[144,128]{1,0:T(8,128)(2,1)}, bf16[144,128]{1,0:T(8,128)(2,1)S(1)}, u32[]{:S(2)}, u32[]{:S(2)}) %collective-permute-start.4) | collective-permute-done | bytes 36896 | tf_op jit(solution)/shard_map/ppermute | solution.py:374
  52.1 0.0 copy-start.5
  52.1 2.8 %collective-permute-done.5.refs_2_ = bf16[144,128]{1,0:T(8,128)(2,1)S(1)} collective-permute-done((bf16[144,128]{1,0:T(8,128)(2,1)}, bf16[144,128]{1,0:T(8,128)(2,1)S(1)}, u32[]{:S(2)}, u32[]{:S(2)}) %collective-permute-start.5) | collective-permute-done | bytes 36896 | tf_op jit(solution)/shard_map/ppermute | solution.py:374
  54.8 0.0 copy-start.6
  54.8 0.0 copy-done.4
  54.8 0.0 copy-done.5
  54.8 0.6 copy-done.6
  55.4 1.8 %shard_map.132 = (bf16[4,96,256]{2,1,0:T(8,128)(2,1)}, bf16[32,256]{1,0:T(8,128)(2,1)}, bf16[32,256]{1,0:T(8,128)(2,1)}) custom-call(f32[144,128]{1,0:T(8,128)} %get-tuple-element.44.own_ref, bf16[144,128]{1,0:T(8,128)(2,1)} %copy-done.4, bf16[144,128]{1,0:T(8,128)(2,1)} %copy-done.5, bf16[144,128]{1,0:T(8,128)(2,1)} %copy-done.6), custom_call_target="tpu_custom_call" | custom-call | tf_op jit(solution)/shard_map/pallas_call | solution.py:382
  57.3 4.5 %collective-permute-start.6 = (bf16[32,256]{1,0:T(8,128)(2,1)}, bf16[32,256]{1,0:T(8,128)(2,1)S(1)}, u32[]{:S(2)}, u32[]{:S(2)}) collective-permute-start(bf16[32,256]{1,0:T(8,128)(2,1)} %get-tuple-element.49), channel_id=1, source_target_pairs={{0,1},{1,2},{2,3},{4,5},{5,6},{6,7},{8,9},{9,10},{10,11},{12,13},{... | collective-permute-start | bytes 49160 | tf_op jit(solution)/shard_map/ppermute | solution.py:370
  61.8 1.3 %collective-permute-start.7 = (bf16[32,256]{1,0:T(8,128)(2,1)}, bf16[32,256]{1,0:T(8,128)(2,1)S(1)}, u32[]{:S(2)}, u32[]{:S(2)}) collective-permute-start(bf16[32,256]{1,0:T(8,128)(2,1)} %get-tuple-element.50), channel_id=1, source_target_pairs={{1,0},{2,1},{3,2},{5,4},{6,5},{7,6},{9,8},{10,9},{11,10},{13,12},{... | collective-permute-start | bytes 49160 | tf_op jit(solution)/shard_map/ppermute | solution.py:370
  63.1 0.3 collective-permute-done.6.above_ref
  63.4 0.0 copy-start.7
  63.4 4.6 %collective-permute-done.7.below_ref = bf16[32,256]{1,0:T(8,128)(2,1)S(1)} collective-permute-done((bf16[32,256]{1,0:T(8,128)(2,1)}, bf16[32,256]{1,0:T(8,128)(2,1)S(1)}, u32[]{:S(2)}, u32[]{:S(2)}) %collective-permute-start.7) | collective-permute-done | bytes 16416 | tf_op jit(solution)/shard_map/ppermute | solution.py:370
  68.0 0.0 copy-start.8
  68.0 0.0 copy-done.7
  68.0 0.6 copy-done.8
  68.6 3.1 %shard_map.133 = bf16[16,16,512]{2,1,0:T(8,128)(2,1)} custom-call(bf16[4,96,256]{2,1,0:T(8,128)(2,1)} %get-tuple-element.48.ext_ref, bf16[32,256]{1,0:T(8,128)(2,1)} %copy-done.7, bf16[32,256]{1,0:T(8,128)(2,1)} %copy-done.8, bf16[128,288]{1,0:T(8,128)(2,1)} %get-tuple-element.51.w1_ref, bf16[128,384]{1,0:T(8,128)(2,1)} %get-tuple-element.52.w2_ref, ...), custom_call_target="tpu_custom_call" | custom-call | tf_op jit(solution)/shard_map/pallas_call | solution.py:382
Async XLA Ops:
  0.0 13.0 %copy-start = (bf16[32,256]{1,0:T(8,128)(2,1)S(1)}, bf16[32,256]{1,0:T(8,128)(2,1)}, u32[]{:S(2)}) copy-start(bf16[32,256]{1,0:T(8,128)(2,1)} %param.17) | copy-start | bytes 49156
  2.4 29.9 %collective-permute-start = (bf16[400,512]{1,0:T(8,128)(2,1)}, bf16[400,512]{1,0:T(8,128)(2,1)S(1)}, u32[]{:S(2)}, u32[]{:S(2)}) collective-permute-start(bf16[400,512]{1,0:T(8,128)(2,1)} %get-tuple-element.29), channel_id=1, source_target_pairs={{0,1},{1,2},{2,3},{4,5},{5,6},{6,7},{8,9},{9,10},{10,11},{12,13},{... | collective-permute-start | bytes 1228808 | tf_op jit(solution)/shard_map/ppermute | solution.py:370
  7.3 18.8 %collective-permute-start.1 = (bf16[160,512]{1,0:T(8,128)(2,1)}, bf16[160,512]{1,0:T(8,128)(2,1)S(1)}, u32[]{:S(2)}, u32[]{:S(2)}) collective-permute-start(bf16[160,512]{1,0:T(8,128)(2,1)} %get-tuple-element.37), channel_id=1, source_target_pairs={{1,0},{2,1},{3,2},{5,4},{6,5},{7,6},{9,8},{10,9},{11,10},{13,12},{... | collective-permute-start | bytes 491528 | tf_op jit(solution)/shard_map/ppermute | solution.py:370
  26.1 0.7 copy-start.2
  32.3 0.8 %copy-start.1 = (bf16[400,512]{1,0:T(8,128)(2,1)}, bf16[400,512]{1,0:T(8,128)(2,1)S(1)}, u32[]{:S(2)}) copy-start(bf16[400,512]{1,0:T(8,128)(2,1)S(1)} %collective-permute-done.got_ref) | copy-start | bytes 1228804
  40.8 1.6 %collective-permute-start.2 = (bf16[4,144,128]{2,1,0:T(8,128)(2,1)}, bf16[4,144,128]{2,1,0:T(8,128)(2,1)S(1)}, u32[]{:S(2)}, u32[]{:S(2)}) collective-permute-start(bf16[4,144,128]{2,1,0:T(8,128)(2,1)} %get-tuple-element.43), channel_id=1, source_target_pairs={{0,4},{4,0},{8,12},{12,8},{16,20},{20,16},{24,28},{28,24},{1,5},{5... | collective-permute-start | bytes 442376 | tf_op jit(solution)/shard_map/ppermute | solution.py:374
  42.3 0.7 copy-start.3
  44.7 4.4 %collective-permute-start.3 = (bf16[144,128]{1,0:T(8,128)(2,1)}, bf16[144,128]{1,0:T(8,128)(2,1)S(1)}, u32[]{:S(2)}, u32[]{:S(2)}) collective-permute-start(bf16[144,128]{1,0:T(8,128)(2,1)} %get-tuple-element.45), channel_id=1, source_target_pairs={{0,8},{4,12},{8,0},{12,4},{16,24},{20,28},{24,16},{28,20},{1,9},{5... | collective-permute-start | bytes 110600 | tf_op jit(solution)/shard_map/ppermute | solution.py:374
  46.3 5.8 %collective-permute-start.4 = (bf16[144,128]{1,0:T(8,128)(2,1)}, bf16[144,128]{1,0:T(8,128)(2,1)S(1)}, u32[]{:S(2)}, u32[]{:S(2)}) collective-permute-start(bf16[144,128]{1,0:T(8,128)(2,1)} %get-tuple-element.46), channel_id=1, source_target_pairs={{0,16},{4,20},{8,24},{12,28},{16,0},{20,4},{24,8},{28,12},{1,17},{... | collective-permute-start | bytes 110600 | tf_op jit(solution)/shard_map/ppermute | solution.py:374
  48.8 6.0 %collective-permute-start.5 = (bf16[144,128]{1,0:T(8,128)(2,1)}, bf16[144,128]{1,0:T(8,128)(2,1)S(1)}, u32[]{:S(2)}, u32[]{:S(2)}) collective-permute-start(bf16[144,128]{1,0:T(8,128)(2,1)} %get-tuple-element.47), channel_id=1, source_target_pairs={{0,24},{4,28},{8,16},{12,20},{16,8},{20,12},{24,0},{28,4},{1,25},{... | collective-permute-start | bytes 110600 | tf_op jit(solution)/shard_map/ppermute | solution.py:374
  49.1 5.7 %copy-start.4 = (bf16[144,128]{1,0:T(8,128)(2,1)}, bf16[144,128]{1,0:T(8,128)(2,1)S(1)}, u32[]{:S(2)}) copy-start(bf16[144,128]{1,0:T(8,128)(2,1)S(1)} %collective-permute-done.3.refs_0_) | copy-start | bytes 110596
  52.1 2.8 %copy-start.5 = (bf16[144,128]{1,0:T(8,128)(2,1)}, bf16[144,128]{1,0:T(8,128)(2,1)S(1)}, u32[]{:S(2)}) copy-start(bf16[144,128]{1,0:T(8,128)(2,1)S(1)} %collective-permute-done.4.refs_1_) | copy-start | bytes 110596
  54.8 0.6 copy-start.6
  57.3 6.2 %collective-permute-start.6 = (bf16[32,256]{1,0:T(8,128)(2,1)}, bf16[32,256]{1,0:T(8,128)(2,1)S(1)}, u32[]{:S(2)}, u32[]{:S(2)}) collective-permute-start(bf16[32,256]{1,0:T(8,128)(2,1)} %get-tuple-element.49), channel_id=1, source_target_pairs={{0,1},{1,2},{2,3},{4,5},{5,6},{6,7},{8,9},{9,10},{10,11},{12,13},{... | collective-permute-start | bytes 49160 | tf_op jit(solution)/shard_map/ppermute | solution.py:370
  61.8 6.2 %collective-permute-start.7 = (bf16[32,256]{1,0:T(8,128)(2,1)}, bf16[32,256]{1,0:T(8,128)(2,1)S(1)}, u32[]{:S(2)}, u32[]{:S(2)}) collective-permute-start(bf16[32,256]{1,0:T(8,128)(2,1)} %get-tuple-element.50), channel_id=1, source_target_pairs={{1,0},{2,1},{3,2},{5,4},{6,5},{7,6},{9,8},{10,9},{11,10},{13,12},{... | collective-permute-start | bytes 49160 | tf_op jit(solution)/shard_map/ppermute | solution.py:370
  63.4 4.6 %copy-start.7 = (bf16[32,256]{1,0:T(8,128)(2,1)}, bf16[32,256]{1,0:T(8,128)(2,1)S(1)}, u32[]{:S(2)}) copy-start(bf16[32,256]{1,0:T(8,128)(2,1)S(1)} %collective-permute-done.6.above_ref) | copy-start | bytes 49156
  68.0 0.6 copy-start.8
where the time goes:
time: 72.2 us; the launch traced here: 71.7 us
  Pallas kernels  34.7 us (48%)
  starting transfers between devices  16.4 us (23%)
  waiting for transfers between devices  12.2 us (17%)
  local copies, waits for them, and re-layouts  8.37 us (12%)
    pallas_call x7, Pallas kernels, call(): pl.pallas_call(kernel, out_shape=[jax.ShapeDtypeStruct(*o) for o in outs]...  34.7 us
    ppermute x4, starting transfers between devices, shifted(): lax.ppermute(value, axis, [(i, i + by) for i in range(peers) if 0 <= i +...  12 us
    ppermute x4, waiting for transfers between devices, swapped(): lax.ppermute(value, 'mem', [(i, i ^ by) for i in range(lax.axis_size('mem...  7.31 us
    ppermute x4, waiting for transfers between devices, shifted(): lax.ppermute(value, axis, [(i, i + by) for i in range(peers) if 0 <= i +...  4.9 us
    ppermute x4, starting transfers between devices, swapped(): lax.ppermute(value, 'mem', [(i, i ^ by) for i in range(lax.axis_size('mem...  4.39 us
    unnamed x18, local copies, waits for them, and re-layouts  3.29 us
    transpose x1, local copies, waits for them, and re-layouts, per_device(): d1 = dec_first.transpose(2, 3, 0, 1).reshape(16, 32, 32)  1.59 us
    transpose x1, local copies, waits for them, and re-layouts, per_device(): d2 = dec_second.transpose(2, 3, 0, 1).reshape(16, 16, 32)  1.48 us
  transfers between devices with their start and end apart: 8, of which 5 were waited for; matrix products, arithmetic and copies ran while one was open for 7% of the time, Pallas kernels for 25%

commit v1 on v0

--- a/solution.py
+++ b/solution.py
@@ -375,17 +375,17 @@
 
 
 VMEM = pl.BlockSpec(memory_space=pltpu.VMEM)
-PARAMS = pltpu.CompilerParams(vmem_limit_bytes=56 * 2**20)
-
-
-def call(kernel, outs, scratch, *operands):
+def params(mb): return pltpu.CompilerParams(vmem_limit_bytes=mb * 2**20)
+
+
+def call(kernel, outs, scratch, *operands, mb=16):
     return pl.pallas_call(
         kernel,
         out_shape=[jax.ShapeDtypeStruct(*o) for o in outs],
         in_specs=[VMEM] * len(operands),
         out_specs=[VMEM] * len(outs),
         scratch_shapes=[pltpu.VMEM(*s) for s in scratch],
-        compiler_params=PARAMS,
+        compiler_params=params(mb),
     )(*operands)
 
 
@@ -436,13 +436,13 @@
             ((3, 128, 5 * channels * rows), BF),
             ((count, half - 1, 256, cols), BF),
         ],
-        x, w1, w2, w3, mix, jnp.asarray(own, BF), jnp.asarray(sel_down, BF), jnp.asarray(sel_up, BF), apart, d1, d2,
+        x, w1, w2, w3, mix, jnp.asarray(own, BF), jnp.asarray(sel_down, BF), jnp.asarray(sel_up, BF), apart, d1, d2, mb=32,
     )
     (low,) = call(
         functools.partial(low_kernel, count, channels, half, per[1]),
         [((32, cols), F32)],
         [((total[1], cols), F32), ((count, 4, 256, cols), BF)],
-        up, apart, w1_up, low_pre, low_h1, w2_big, w3_big, low_v, mix,
+        up, apart, w1_up, low_pre, low_h1, w2_big, w3_big, low_v, mix, mb=20,
     )
     slots = peers // 2
     chunk = (quarter * 32 + 16, 128)
@@ -450,7 +450,7 @@
         functools.partial(top_kernel, count, channels, half, per[0], nb),
         [((slots,) + chunk, BF)] * 2,
         [((total[0], cols), F32), ((count, 5, 256, cols), BF), ((quarter * 32, cols + 256), F32)],
-        down, apart, w1_down, top_pre, top_h1, w2_big, w3_big, top_v, mix, mid, low,
+        down, apart, w1_down, top_pre, top_h1, w2_big, w3_big, top_v, mix, mid, low, mb=20,
     )
     got = swapped(send, 1)
     mine, *others = call(pair_kernel, [(chunk, F32)] + [(chunk, BF)] * (slots - 1), [], keep, got)

time: 72.2 us -> 54 us (0.75)
  Pallas kernels: 34.7 us -> 16.6 us
    pallas_call x7, Pallas kernels: 34.7 us -> 16.6 us  [call(): pl.pallas_call(kernel, out_shape=[jax.ShapeDtypeStruct(*o) for o in outs]...]
    unnamed x18 -> x22, local copies, waits for them, and re-layouts: 3.29 us -> 5.83 us
  transfers between devices with their start and end apart: 8 -> 8, of which waited for: 5 -> 5; matrix products, arithmetic and copies ran while one was open for 7% -> 5% of each run, Pallas kernels for 25% -> 18%
where the time goes in v1:
time: 54 us; the launch traced here: 53.4 us
  Pallas kernels  16.6 us (31%)
  starting transfers between devices  16.6 us (31%)
  waiting for transfers between devices  11.6 us (21%)
  local copies, waits for them, and re-layouts  8.46 us (16%)
    pallas_call x7, Pallas kernels, call(): pl.pallas_call(kernel, out_shape=[jax.ShapeDtypeStruct(*o) for o in outs]...  16.6 us
    ppermute x4, starting transfers between devices, shifted(): lax.ppermute(value, axis, [(i, i + by) for i in range(peers) if 0 <= i +...  12.1 us
    ppermute x4, waiting for transfers between devices, swapped(): lax.ppermute(value, 'mem', [(i, i ^ by) for i in range(lax.axis_size('mem...  6.89 us
    unnamed x22, local copies, waits for them, and re-layouts  5.83 us
    ppermute x4, waiting for transfers between devices, shifted(): lax.ppermute(value, axis, [(i, i + by) for i in range(peers) if 0 <= i +...  4.7 us
    ppermute x4, starting transfers between devices, swapped(): lax.ppermute(value, 'mem', [(i, i ^ by) for i in range(lax.axis_size('mem...  4.49 us
  transfers between devices with their start and end apart: 8, of which 5 were waited for; matrix products, arithmetic and copies ran while one was open for 5% of the time, Pallas kernels for 18%

profile of v1, /device:TPU:0, one launch (start us, length us, event | category | flops | bytes accessed | tf_op | source)
XLA Modules:
  0.0 53.4 jit_solution(9393011202545592704)
XLA Ops:
  0.0 0.0 copy-start
  0.0 0.0 copy-start.1
  0.0 1.3 %copy-done.1 = bf16[2,5,16,4096]{3,2,1,0:T(8,128)(2,1)S(1)} copy-done((bf16[2,5,16,4096]{3,2,1,0:T(8,128)(2,1)S(1)}, bf16[2,5,16,4096]{3,2,1,0:T(8,128)(2,1)}, u32[]{:S(2)}) %copy-start.1) | copy-done | bytes 1310744
  1.3 0.0 copy-start.2
  1.3 0.0 copy-start.5
  1.3 0.3 shard_map.127
  1.6 5.0 %collective-permute-start = (bf16[400,512]{1,0:T(8,128)(2,1)S(1)}, bf16[400,512]{1,0:T(8,128)(2,1)S(1)}, u32[]{:S(2)}, u32[]{:S(2)}) collective-permute-start(bf16[400,512]{1,0:T(8,128)(2,1)S(1)} %get-tuple-element.29), channel_id=1, source_target_pairs={{0,1},{1,2},{2,3},{4,5},{5,6},{6,7},{8,9},{9,10},{10,11},{12,13},{... | collective-permute-start | bytes 1228808 | tf_op jit(solution)/shard_map/ppermute | solution.py:370
  6.6 1.3 %collective-permute-start.1 = (bf16[160,512]{1,0:T(8,128)(2,1)S(1)}, bf16[160,512]{1,0:T(8,128)(2,1)S(1)}, u32[]{:S(2)}, u32[]{:S(2)}) collective-permute-start(bf16[160,512]{1,0:T(8,128)(2,1)S(1)} %get-tuple-element.37), channel_id=1, source_target_pairs={{1,0},{2,1},{3,2},{5,4},{6,5},{7,6},{9,8},{10,9},{11,10},{13,12},{... | collective-permute-start | bytes 491528 | tf_op jit(solution)/shard_map/ppermute | solution.py:370
  7.9 0.9 %copy.14 = bf16[4,4,32,32]{3,2,1,0:T(8,128)(2,1)S(1)} copy(bf16[4,4,32,32]{3,1,0,2:T(4,128)(2,1)} %bitcast.18) | data formatting | bytes 65536 | tf_op jit(solution)/shard_map/transpose | solution.py:413
  8.9 0.9 %copy.15 = bf16[4,4,16,32]{3,2,1,0:T(8,128)(2,1)S(1)} copy(bf16[4,4,16,32]{3,1,0,2:T(4,128)(2,1)} %bitcast.19) | data formatting | bytes 32768 | tf_op jit(solution)/shard_map/transpose | solution.py:414
  9.7 0.7 %reshape.19 = bf16[45,64]{1,0:T(8,128)(2,1)S(1)} reshape(bf16[5,3,3,64]{3,2,1,0:T(4,128)(2,1)} %bitcast.20) | data formatting | bytes 11520 | tf_op jit(solution)/shard_map/reshape | solution.py:410
  10.5 0.0 copy-done
  10.5 0.1 constant_dynamic-slice_fusion.mix_ref
  10.6 0.0 copy-done.2
  10.6 0.0 copy-done.5
  10.6 0.0 copy-start.3
  10.6 1.0 %copy-done.3 = bf16[512,512]{1,0:T(8,128)(2,1)S(1)} copy-done((bf16[512,512]{1,0:T(8,128)(2,1)S(1)}, bf16[512,512]{1,0:T(8,128)(2,1)}, u32[]{:S(2)}) %copy-start.3) | copy-done | bytes 524312
  11.6 0.0 copy-start.6
  11.6 1.0 %copy-done.6 = bf16[3,2,48,400]{3,2,1,0:T(8,128)(2,1)S(1)} copy-done((bf16[3,2,48,400]{3,2,1,0:T(8,128)(2,1)S(1)}, bf16[3,2,48,400]{3,2,1,0:T(8,128)(2,1)}, u32[]{:S(2)}) %copy-start.6) | copy-done | bytes 230424
  12.6 0.0 copy-start.7
  12.6 0.9 %copy-done.7 = bf16[64,64,3,3]{1,0,3,2:T(8,128)(2,1)S(1)} copy-done((bf16[64,64,3,3]{1,0,3,2:T(8,128)(2,1)S(1)}, bf16[64,64,3,3]{1,0,3,2:T(8,128)(2,1)}, u32[]{:S(2)}) %copy-start.7) | copy-done | bytes 73752
  13.5 0.0 copy-start.9
  13.5 0.8 %copy-done.9 = bf16[2,2,48,128]{3,2,1,0:T(8,128)(2,1)S(1)} copy-done((bf16[2,2,48,128]{3,2,1,0:T(8,128)(2,1)S(1)}, bf16[2,2,48,128]{3,2,1,0:T(8,128)(2,1)}, u32[]{:S(2)}) %copy-start.9) | copy-done | bytes 49176
  14.3 0.0 copy-start.10
  14.3 0.8 %copy-done.10 = bf16[16,64,3,3]{1,0,3,2:T(8,128)(2,1)S(1)} copy-done((bf16[16,64,3,3]{1,0,3,2:T(8,128)(2,1)S(1)}, bf16[16,64,3,3]{1,0,3,2:T(8,128)(2,1)}, u32[]{:S(2)}) %copy-start.10) | copy-done | bytes 18456
  15.1 7.6 %shard_map.128 = (f32[2,128,1024]{2,1,0:T(8,128)S(1)}, f32[2,128,1024]{2,1,0:T(8,128)S(1)}, bf16[2,2,256,1024]{3,2,1,0:T(8,128)(2,1)S(1)}, bf16[2,3,256,1024]{3,...) custom-call(bf16[160,4096]{1,0:T(8,128)(2,1)S(1)} %bitcast.13, ...), custom_call_target="tpu_custom_call" | custom-call | tf_op jit(solution)/shard_map/pallas_call | solution.py:382
  22.7 0.0 collective-permute-done.1.got_ref
  22.7 2.2 %shard_map.129.low_ref = f32[32,1024]{1,0:T(8,128)S(1)} custom-call(bf16[160,512]{1,0:T(8,128)(2,1)S(1)} %collective-permute-done.1.got_ref, bf16[512,512]{1,0:T(8,128)(2,1)S(1)} %copy-done.3, bf16[2,128,128]{2,1,0:T(8,128)(2,1)S(1)} %get-tuple-element.38.w1_ref, f32[2,128,1024]{2,1,0:T(8,128)S(1)} %get-tuple-element.39.pre_ref, ...), custom_call_target="tpu_custom_call" | custom-call | tf_op jit(solution)/shard_map/pallas_call | solution.py:382
  25.0 0.0 collective-permute-done.got_ref
  25.0 0.0 copy-start.4
  25.0 0.0 copy-start.8
  25.0 4.3 %shard_map.130 = (bf16[4,144,128]{2,1,0:T(8,128)(2,1)S(1)}, bf16[4,144,128]{2,1,0:T(8,128)(2,1)S(1)}) custom-call(bf16[400,512]{1,0:T(8,128)(2,1)S(1)} %collective-permute-done.got_ref, bf16[512,512]{1,0:T(8,128)(2,1)S(1)} %copy-done.3, bf16[2,384,288]{2,1,0:T(8,128)(2,1)S(1)} %get-tuple-element.30.w1_ref, f32[2,128,1024]{2,1,0:T(8,128)S(1)} %get-tuple-element.31.pre_ref, ...), custom_call_target="tpu_custom_call" | custom-call | tf_op jit(solution)/shard_map/pallas_call | solution.py:382
  29.3 0.0 collective-permute-start.2
  29.3 1.4 %collective-permute-done.2.got_ref = bf16[4,144,128]{2,1,0:T(8,128)(2,1)S(1)} collective-permute-done((bf16[4,144,128]{2,1,0:T(8,128)(2,1)S(1)}, bf16[4,144,128]{2,1,0:T(8,128)(2,1)S(1)}, u32[]{:S(2)}, u32[]{:S(2)}) %collective-permute-start.2) | collective-permute-done | bytes 147488 | tf_op jit(solution)/shard_map/ppermute | solution.py:374
  30.7 1.6 %collective-permute-start.3 = (bf16[144,128]{1,0:T(8,128)(2,1)S(1)}, bf16[144,128]{1,0:T(8,128)(2,1)S(1)}, u32[]{:S(2)}, u32[]{:S(2)}) collective-permute-start(bf16[144,128]{1,0:T(8,128)(2,1)S(1)} %get-tuple-element.45), channel_id=1, source_target_pairs={{0,8},{4,12},{8,0},{12,4},{16,24},{20,28},{24,16},{28,20},{1,9},{5... | collective-permute-start | bytes 110600 | tf_op jit(solution)/shard_map/ppermute | solution.py:374
  32.4 2.6 %collective-permute-start.4 = (bf16[144,128]{1,0:T(8,128)(2,1)S(1)}, bf16[144,128]{1,0:T(8,128)(2,1)S(1)}, u32[]{:S(2)}, u32[]{:S(2)}) collective-permute-start(bf16[144,128]{1,0:T(8,128)(2,1)S(1)} %get-tuple-element.46), channel_id=1, source_target_pairs={{0,16},{4,20},{8,24},{12,28},{16,0},{20,4},{24,8},{28,12},{1,17},{... | collective-permute-start | bytes 110600 | tf_op jit(solution)/shard_map/ppermute | solution.py:374
  34.9 0.2 collective-permute-start.5
  35.2 0.0 collective-permute-done.3.refs_0_
  35.2 2.8 %collective-permute-done.4.refs_1_ = bf16[144,128]{1,0:T(8,128)(2,1)S(1)} collective-permute-done((bf16[144,128]{1,0:T(8,128)(2,1)S(1)}, bf16[144,128]{1,0:T(8,128)(2,1)S(1)}, u32[]{:S(2)}, u32[]{:S(2)}) %collective-permute-start.4) | collective-permute-done | bytes 36896 | tf_op jit(solution)/shard_map/ppermute | solution.py:374
  37.9 2.8 %collective-permute-done.5.refs_2_ = bf16[144,128]{1,0:T(8,128)(2,1)S(1)} collective-permute-done((bf16[144,128]{1,0:T(8,128)(2,1)S(1)}, bf16[144,128]{1,0:T(8,128)(2,1)S(1)}, u32[]{:S(2)}, u32[]{:S(2)}) %collective-permute-start.5) | collective-permute-done | bytes 36896 | tf_op jit(solution)/shard_map/ppermute | solution.py:374
  40.7 0.3 shard_map.132
  41.0 4.5 %collective-permute-start.6 = (bf16[32,256]{1,0:T(8,128)(2,1)S(1)}, bf16[32,256]{1,0:T(8,128)(2,1)S(1)}, u32[]{:S(2)}, u32[]{:S(2)}) collective-permute-start(bf16[32,256]{1,0:T(8,128)(2,1)S(1)} %get-tuple-element.49), channel_id=1, source_target_pairs={{0,1},{1,2},{2,3},{4,5},{5,6},{6,7},{8,9},{9,10},{10,11},{12,13},{... | collective-permute-start | bytes 49160 | tf_op jit(solution)/shard_map/ppermute | solution.py:370
  45.5 1.3 %collective-permute-start.7 = (bf16[32,256]{1,0:T(8,128)(2,1)S(1)}, bf16[32,256]{1,0:T(8,128)(2,1)S(1)}, u32[]{:S(2)}, u32[]{:S(2)}) collective-permute-start(bf16[32,256]{1,0:T(8,128)(2,1)S(1)} %get-tuple-element.50), channel_id=1, source_target_pairs={{1,0},{2,1},{3,2},{5,4},{6,5},{7,6},{9,8},{10,9},{11,10},{13,12},{... | collective-permute-start | bytes 49160 | tf_op jit(solution)/shard_map/ppermute | solution.py:370
  46.8 0.1 collective-permute-done.6.above_ref
  47.0 4.6 %collective-permute-done.7.below_ref = bf16[32,256]{1,0:T(8,128)(2,1)S(1)} collective-permute-done((bf16[32,256]{1,0:T(8,128)(2,1)S(1)}, bf16[32,256]{1,0:T(8,128)(2,1)S(1)}, u32[]{:S(2)}, u32[]{:S(2)}) %collective-permute-start.7) | collective-permute-done | bytes 16416 | tf_op jit(solution)/shard_map/ppermute | solution.py:370
  51.5 0.0 copy-done.4
  51.5 0.0 copy-done.8
  51.5 1.9 %shard_map.133 = bf16[16,16,512]{2,1,0:T(8,128)(2,1)} custom-call(bf16[4,96,256]{2,1,0:T(8,128)(2,1)S(1)} %get-tuple-element.48.ext_ref, bf16[32,256]{1,0:T(8,128)(2,1)S(1)} %collective-permute-done.6.above_ref, bf16[32,256]{1,0:T(8,128)(2,1)S(1)} %collective-permute-done.7.below_ref, bf16[128,288]{1,0:T(8,128)(2,1)S(1)} %get-tuple-element.51.w1_ref, ...), custom_call_target="tpu_custom_call" | custom-call | tf_op jit(solution)/shard_map/pallas_call | solution.py:382
  (2 shorter events, 0.0 us)
Async XLA Ops:
  0.0 10.5 %copy-start = (bf16[32,256]{1,0:T(8,128)(2,1)S(1)}, bf16[32,256]{1,0:T(8,128)(2,1)}, u32[]{:S(2)}) copy-start(bf16[32,256]{1,0:T(8,128)(2,1)} %param.17) | copy-start | bytes 49156
  0.0 1.3 %copy-start.1 = (bf16[2,5,16,4096]{3,2,1,0:T(8,128)(2,1)S(1)}, bf16[2,5,16,4096]{3,2,1,0:T(8,128)(2,1)}, u32[]{:S(2)}) copy-start(bf16[2,5,16,4096]{3,2,1,0:T(8,128)(2,1)} %param.13) | copy-start | bytes 3932164
  1.3 9.2 %copy-start.2 = (bf16[2,5,16,4096]{3,2,1,0:T(8,128)(2,1)S(1)}, bf16[2,5,16,4096]{3,2,1,0:T(8,128)(2,1)}, u32[]{:S(2)}) copy-start(bf16[2,5,16,4096]{3,2,1,0:T(8,128)(2,1)} %param.13) | copy-start | bytes 3932164
  1.3 9.2 %copy-start.5 = (bf16[2,3,2,48,288]{4,3,2,1,0:T(8,128)(2,1)S(1)}, bf16[2,3,2,48,288]{4,3,2,1,0:T(8,128)(2,1)}, u32[]{:S(2)}) copy-start(bf16[2,3,2,48,288]{4,3,2,1,0:T(8,128)(2,1)} %constant.28.clone.down_ref) | copy-start | bytes 995332
  1.6 23.4 %collective-permute-start = (bf16[400,512]{1,0:T(8,128)(2,1)S(1)}, bf16[400,512]{1,0:T(8,128)(2,1)S(1)}, u32[]{:S(2)}, u32[]{:S(2)}) collective-permute-start(bf16[400,512]{1,0:T(8,128)(2,1)S(1)} %get-tuple-element.29), channel_id=1, source_target_pairs={{0,1},{1,2},{2,3},{4,5},{5,6},{6,7},{8,9},{9,10},{10,11},{12,13},{... | collective-permute-start | bytes 1228808 | tf_op jit(solution)/shard_map/ppermute | solution.py:370
  6.6 16.1 %collective-permute-start.1 = (bf16[160,512]{1,0:T(8,128)(2,1)S(1)}, bf16[160,512]{1,0:T(8,128)(2,1)S(1)}, u32[]{:S(2)}, u32[]{:S(2)}) collective-permute-start(bf16[160,512]{1,0:T(8,128)(2,1)S(1)} %get-tuple-element.37), channel_id=1, source_target_pairs={{1,0},{2,1},{3,2},{5,4},{6,5},{7,6},{9,8},{10,9},{11,10},{13,12},{... | collective-permute-start | bytes 491528 | tf_op jit(solution)/shard_map/ppermute | solution.py:370
  10.6 1.0 %copy-start.3 = (bf16[512,512]{1,0:T(8,128)(2,1)S(1)}, bf16[512,512]{1,0:T(8,128)(2,1)}, u32[]{:S(2)}) copy-start(bf16[512,512]{1,0:T(8,128)(2,1)} %constant.26.clone.p_ref) | copy-start | bytes 1572868
  11.6 1.0 %copy-start.6 = (bf16[3,2,48,400]{3,2,1,0:T(8,128)(2,1)S(1)}, bf16[3,2,48,400]{3,2,1,0:T(8,128)(2,1)}, u32[]{:S(2)}) copy-start(bf16[3,2,48,400]{3,2,1,0:T(8,128)(2,1)} %constant.27.clone.own_ref) | copy-start | bytes 691204
  12.6 0.9 %copy-start.7 = (bf16[64,64,3,3]{1,0,3,2:T(8,128)(2,1)S(1)}, bf16[64,64,3,3]{1,0,3,2:T(8,128)(2,1)}, u32[]{:S(2)}) copy-start(bf16[64,64,3,3]{1,0,3,2:T(8,128)(2,1)} %param.15) | copy-start | bytes 221188
  13.5 0.8 %copy-start.9 = (bf16[2,2,48,128]{3,2,1,0:T(8,128)(2,1)S(1)}, bf16[2,2,48,128]{3,2,1,0:T(8,128)(2,1)}, u32[]{:S(2)}) copy-start(bf16[2,2,48,128]{3,2,1,0:T(8,128)(2,1)} %constant.29.clone.up_ref) | copy-start | bytes 147460
  14.3 0.8 %copy-start.10 = (bf16[16,64,3,3]{1,0,3,2:T(8,128)(2,1)S(1)}, bf16[16,64,3,3]{1,0,3,2:T(8,128)(2,1)}, u32[]{:S(2)}) copy-start(bf16[16,64,3,3]{1,0,3,2:T(8,128)(2,1)} %param.16) | copy-start | bytes 55300
  25.0 26.6 %copy-start.4 = (bf16[512,512]{1,0:T(8,128)(2,1)S(1)}, bf16[512,512]{1,0:T(8,128)(2,1)}, u32[]{:S(2)}) copy-start(bf16[512,512]{1,0:T(8,128)(2,1)} %constant.30.clone.p_ref) | copy-start | bytes 1572868
  25.0 26.5 %copy-start.8 = (bf16[256,256]{1,0:T(8,128)(2,1)S(1)}, bf16[256,256]{1,0:T(8,128)(2,1)}, u32[]{:S(2)}) copy-start(bf16[256,256]{1,0:T(8,128)(2,1)} %constant.31.clone.r_ref) | copy-start | bytes 393220
  29.3 1.4 %collective-permute-start.2 = (bf16[4,144,128]{2,1,0:T(8,128)(2,1)S(1)}, bf16[4,144,128]{2,1,0:T(8,128)(2,1)S(1)}, u32[]{:S(2)}, u32[]{:S(2)}) collective-permute-start(bf16[4,144,128]{2,1,0:T(8,128)(2,1)S(1)} %get-tuple-element.43), channel_id=1, source_target_pairs={{0,4},{4,0},{8,12},{12,8},{16,20},{20,16},{24,28},{28,24},{1,5},{5... | collective-permute-start | bytes 442376 | tf_op jit(solution)/shard_map/ppermute | solution.py:374
  30.7 4.5 %collective-permute-start.3 = (bf16[144,128]{1,0:T(8,128)(2,1)S(1)}, bf16[144,128]{1,0:T(8,128)(2,1)S(1)}, u32[]{:S(2)}, u32[]{:S(2)}) collective-permute-start(bf16[144,128]{1,0:T(8,128)(2,1)S(1)} %get-tuple-element.45), channel_id=1, source_target_pairs={{0,8},{4,12},{8,0},{12,4},{16,24},{20,28},{24,16},{28,20},{1,9},{5... | collective-permute-start | bytes 110600 | tf_op jit(solution)/shard_map/ppermute | solution.py:374
  32.4 5.6 %collective-permute-start.4 = (bf16[144,128]{1,0:T(8,128)(2,1)S(1)}, bf16[144,128]{1,0:T(8,128)(2,1)S(1)}, u32[]{:S(2)}, u32[]{:S(2)}) collective-permute-start(bf16[144,128]{1,0:T(8,128)(2,1)S(1)} %get-tuple-element.46), channel_id=1, source_target_pairs={{0,16},{4,20},{8,24},{12,28},{16,0},{20,4},{24,8},{28,12},{1,17},{... | collective-permute-start | bytes 110600 | tf_op jit(solution)/shard_map/ppermute | solution.py:374
  34.9 5.8 %collective-permute-start.5 = (bf16[144,128]{1,0:T(8,128)(2,1)S(1)}, bf16[144,128]{1,0:T(8,128)(2,1)S(1)}, u32[]{:S(2)}, u32[]{:S(2)}) collective-permute-start(bf16[144,128]{1,0:T(8,128)(2,1)S(1)} %get-tuple-element.47), channel_id=1, source_target_pairs={{0,24},{4,28},{8,16},{12,20},{16,8},{20,12},{24,0},{28,4},{1,25},{... | collective-permute-start | bytes 110600 | tf_op jit(solution)/shard_map/ppermute | solution.py:374
  41.0 6.0 %collective-permute-start.6 = (bf16[32,256]{1,0:T(8,128)(2,1)S(1)}, bf16[32,256]{1,0:T(8,128)(2,1)S(1)}, u32[]{:S(2)}, u32[]{:S(2)}) collective-permute-start(bf16[32,256]{1,0:T(8,128)(2,1)S(1)} %get-tuple-element.49), channel_id=1, source_target_pairs={{0,1},{1,2},{2,3},{4,5},{5,6},{6,7},{8,9},{9,10},{10,11},{12,13},{... | collective-permute-start | bytes 49160 | tf_op jit(solution)/shard_map/ppermute | solution.py:370
  45.5 6.0 %collective-permute-start.7 = (bf16[32,256]{1,0:T(8,128)(2,1)S(1)}, bf16[32,256]{1,0:T(8,128)(2,1)S(1)}, u32[]{:S(2)}, u32[]{:S(2)}) collective-permute-start(bf16[32,256]{1,0:T(8,128)(2,1)S(1)} %get-tuple-element.50), channel_id=1, source_target_pairs={{1,0},{2,1},{3,2},{5,4},{6,5},{7,6},{9,8},{10,9},{11,10},{13,12},{... | collective-permute-start | bytes 49160 | tf_op jit(solution)/shard_map/ppermute | solution.py:370

commit v2 on v1

v2 whole, which is shorter than its diff:
```python
import functools

import jax
import jax.numpy as jnp
import numpy as np
from jax import lax
from jax.experimental import pallas as pl
from jax.experimental.pallas import tpu as pltpu
from jax.sharding import PartitionSpec as P

BF = jnp.bfloat16
F32 = jnp.float32
CH_BOT = 16
UP = 3
DOWN = 2
TRANSPOSED = [(p, i, 2 * i - p) for p in range(2) for i in range(3) if 0 <= 2 * i - p < 4]


def dot(a, b):
    return lax.dot_general(a, b, (((1,), (0,)), ((), ())), preferred_element_type=F32)


def dot_t(a, b):
    return lax.dot_general(a, b, (((0,), (0,)), ((), ())), preferred_element_type=F32)


def silu_of_half(y):
    return y + y * jnp.tanh(y)


def padded(n, to):
    return -(-n // to) * to


def spread(step, tile):
    one = np.zeros((step * tile, step * tile), np.float32)
    for q in range(step):
        for c in range(tile):
            one[step * c + q, q * tile + c] = 1
    return one


def shift_right(v):
    return jnp.concatenate([jnp.zeros_like(v[:, :1]), v[:, :-1]], axis=1)


def shift_left(v):
    return jnp.concatenate([v[:, 1:], jnp.zeros_like(v[:, :1])], axis=1)


def is_row(at):
    return jnp.where(lax.axis_index("row") == at, 0.0, 1.0).astype(F32)


def put_hidden(ref, at, value):
    v = value.astype(BF)
    even, odd = v[0:64], v[64:128]
    ref[at * 256 + 64 : at * 256 + 128, :] = even
    ref[at * 256 + 128 : at * 256 + 192, :] = odd
    ref[at * 256 : at * 256 + 64, :] = shift_right(odd)
    ref[at * 256 + 192 : at * 256 + 256, :] = shift_left(even)


def apart(block, even_ref, odd_ref):
    first = dot(block[:, 0:256], even_ref)
    second = dot(block[:, 256:512], odd_ref)
    low = lax.broadcasted_iota(jnp.int32, (block.shape[0], 128), 1) < 64
    out = []
    for half in range(2):
        e, o = first[:, half * 128 : half * 128 + 128], second[:, half * 128 : half * 128 + 128]
        out.append(jnp.where(low, e, o))
        out.append(pltpu.roll(jnp.where(low, o, e), 64, 1))
    return out


def place_halo(source, spread_ref, y_ref, count, per):
    y_ref[...] = jnp.zeros_like(y_ref)
    for q, z in enumerate(apart(source, spread_ref[0], spread_ref[1])):
        for t in range(y_ref.shape[1] // 128):
            y_ref[(q + 1) * per : (q + 1) * per + count, t * 128 : (t + 1) * 128] = z[t * count : (t + 1) * count]
    y_ref[0:per, :] = shift_right(y_ref[4 * per : 5 * per, :])
    return y_ref[...].astype(BF)


def pack_kernel(members, channels, rows, x_ref, down_ref, up_ref, d_scr, u_scr):
    wide = x_ref.shape[1]
    lanes = down_ref.shape[1]
    nd, nu = members * channels * UP, members * channels * DOWN
    for t in range(wide // lanes):
        for g in range(members * channels):
            block = x_ref[g * rows : (g + 1) * rows, t * lanes : (t + 1) * lanes].astype(F32)
            d_scr[t * nd + g * UP : t * nd + (g + 1) * UP, :] = block[rows - UP : rows]
            u_scr[t * nu + g * DOWN : t * nu + (g + 1) * DOWN, :] = block[0:DOWN]
    down_ref[...] = d_scr[...].astype(BF)
    up_ref[...] = u_scr[...].astype(BF)


def inner_kernel(
    members, channels, rows, per,
    x_ref, w1_ref, w2_ref, w3_ref, mix_ref,
    h_first, h_last, a_first, a_second, a_last, v_second, v_last, mixed_ref,
    w2_big, w3_big, w1_down, w1_up, spread_ref, mix_own,
    w1_flat, w1_own, y_ref, out1_ref, h1_ref, h2_ref,
):
    half, groups = rows // 2, rows // 8
    wide = x_ref.shape[1]
    cols = wide // 4

    row_of = lax.broadcasted_iota(jnp.int32, (256, 256), 0)
    lane_of = lax.broadcasted_iota(jnp.int32, (256, 256), 1)
    place = lane_of // 64
    for odd in range(2):
        q = place ^ odd
        spread_ref[odd] = jnp.where(row_of == 4 * (lane_of - 64 * place) + q, 1.0, 0.0).astype(BF)

    w1_flat[...] = jnp.zeros_like(w1_flat)
    for c in range(channels):
        for dr in range(3):
            at = (c * 3 + dr) * 3
            w1_flat[at : at + 3, :] = 0.5 * w1_ref[c, dr].astype(F32)
    w1 = w1_flat[...].astype(BF)
    taps = w1.shape[0]

    def taps_at(lanes, target):
        tap = lax.broadcasted_iota(jnp.int32, (taps, lanes), 0)
        c = sum(((tap >= 9 * k).astype(jnp.int32) for k in range(1, channels)), jnp.zeros_like(tap))
        rest = tap - 9 * c
        dr = (rest >= 3).astype(jnp.int32) + (rest >= 6).astype(jnp.int32)
        dc = rest - 3 * dr
        to, valid = target(c, dr, dc)
        at = lax.broadcasted_iota(jnp.int32, (taps, lanes), 1)
        return dot_t(w1, jnp.where((at == to) & valid, 1.0, 0.0).astype(BF)).astype(BF)

    for pc in range(2):
        for j in range(5):
            def own(c, dr, dc):
                row = 2 * j + dr - 1
                return ((2 * pc + dc) * channels + c) * 8 + row, (row >= 0) & (row < 8)
            w1_own[j * 128 + pc * 64 : j * 128 + pc * 64 + 64, :] = taps_at(w1_own.shape[1], own)
        for m in range(members):
            for kind in range(2):
                def above(c, dr, dc):
                    slot = dr if kind == 0 else dr + 2
                    return (2 * pc + dc) * per[0] + (m * channels + c) * UP + slot, slot < UP
                w1_down[m, kind * 128 + pc * 64 : kind * 128 + pc * 64 + 64, :] = taps_at(w1_down.shape[2], above)
            def below(c, dr, dc):
                return (2 * pc + dc) * per[1] + (m * channels + c) * DOWN + dr - 1, dr >= 1
            w1_up[m, pc * 64 : pc * 64 + 64, :] = taps_at(w1_up.shape[2], below)

    w2_big[...] = jnp.zeros_like(w2_big)
    for ocol in range(2):
        for dr in range(3):
            for dc in range(3):
                at = dr * 256 + (ocol + dc) * 64
                w2_big[ocol * 64 : ocol * 64 + 64, at : at + 64] = (0.5 * w2_ref[dr * 3 + dc].astype(F32)).astype(BF)
    w3_big[...] = jnp.zeros_like(w3_big)
    for dr, to, base in ((1, 0, 0), (2, 0, 128), (0, 2, 128)):
        for dc, moved, at in ((1, 0, 0), (2, 0, 64), (0, 1, 64)):
            w3_big[(to + moved) * 16 : (to + moved + 1) * 16, base + at : base + at + 64] = (
                0.5 * w3_ref[dr * 3 + dc].astype(F32)
            ).astype(BF)
    own_lanes = members * CH_BOT
    total = mix_ref.shape[1]
    start = lax.axis_index("mem") * own_lanes
    mix = pltpu.roll(mix_ref[...].astype(F32), lax.rem(total - start, total), 1)[:, 0:own_lanes].astype(BF)
    mix_own[...] = mix

    for t in range(wide // 512):
        for q, z in enumerate(apart(x_ref[:, 512 * t : 512 * (t + 1)], spread_ref[0], spread_ref[1])):
            for m in range(members):
                for c in range(channels):
                    for g in range(groups):
                        at = ((q + 1) * channels + c) * 8
                        frm = (m * channels + c) * rows + g * 8
                        y_ref[m, g, at : at + 8, t * 128 : (t + 1) * 128] = z[frm : frm + 8]
    c8 = channels * 8
    for m in range(members):
        for g in range(groups):
            y_ref[m, g, 0:c8, :] = shift_right(y_ref[m, g, 4 * c8 : 5 * c8, :])

    mids = []
    for m in range(members):
        for g in range(groups):
            out1_ref[g] = dot(w1_own[...], y_ref[m, g].astype(BF))
        h_first[m] = out1_ref[0, 0:128]
        h_last[m] = out1_ref[groups - 1, 512:640]
        for h in range(1, half):
            g, j = h // 4, h % 4
            v = out1_ref[g, j * 128 : j * 128 + 128]
            if j == 0:
                v = v + out1_ref[g - 1, 512:640]
            put_hidden(h1_ref, h - 1, silu_of_half(v))
        a_first[m] = dot(w2_big[:, 512:768], h1_ref[0:256, :])
        a_second[m] = dot(w2_big[:, 256:768], h1_ref[0:512, :])
        a_last[m] = dot(w2_big[:, 0:512], h1_ref[(half - 3) * 256 : (half - 1) * 256, :])
        carry = None
        for o in range(2, half - 1):
            h2_ref[(o % 2) * 128 : (o % 2) * 128 + 128, :] = silu_of_half(
                dot(w2_big[...], h1_ref[(o - 2) * 256 : (o + 1) * 256, :])
            ).astype(BF)
            if o % 2:
                v = dot(w3_big[...], h2_ref[...])
                if o == 3:
                    v_second[m] = v[0:32]
                else:
                    w = v[0:32] + carry
                    mids.append((o // 2, silu_of_half(w[0:16] + shift_right(w[16:32])).astype(BF)))
                carry = v[32:64]
        v_last[m] = carry + dot(w3_big[0:32, 0:128], h2_ref[0:128, :])
    for r in range(2, half // 2 - 1):
        mixed_ref[r - 2] = dot(mix, jnp.concatenate([b for s, b in mids if s == r], axis=0))


def low_kernel(
    members, channels, per,
    got_ref, spread_ref, w1_ref, h_ref, w2_ref, a_ref, w3_ref, v_ref, mix_ref,
    mixed_ref, carry_ref, y_ref, h1_ref,
):
    below = is_row(lax.axis_size("row") - 1)
    y = place_halo(got_ref[...], spread_ref, y_ref, members * channels * DOWN, per)
    parts = []
    for m in range(members):
        put_hidden(h1_ref, m, silu_of_half((dot(w1_ref[m], y) + h_ref[m]) * below))
        h2 = silu_of_half(dot(w2_ref[:, 512:768], h1_ref[m * 256 : m * 256 + 256, :]) + a_ref[m]).astype(BF)
        v = dot(w3_ref[:, 128:256], h2)
        carry_ref[m * 16 : m * 16 + 16, :] = (v[32:48] + shift_right(v[48:64])).astype(BF)
        w = v[0:32] + v_ref[m]
        parts.append(silu_of_half(w[0:16] + shift_right(w[16:32])).astype(BF))
    mixed_ref[...] = dot(mix_ref[...], jnp.concatenate(parts, axis=0))


def top_kernel(
    members, channels, per,
    got_ref, spread_ref, w1_ref, h_ref, w2_ref, a_first, a_second, w3_ref, v_ref, mix_ref, mid_ref, low_ref,
    pre_ref, tail_ref, y_ref, h1_ref, h2_ref,
):
    source = (got_ref[...].astype(F32) * is_row(0)).astype(BF)
    y = place_halo(source, spread_ref, y_ref, members * channels * UP, per)
    second = []
    for m in range(members):
        fresh = dot(w1_ref[m], y)
        put_hidden(h1_ref, 2 * m, silu_of_half(fresh[0:128]))
        put_hidden(h1_ref, 2 * m + 1, silu_of_half(fresh[128:256] + h_ref[m]))
        both = h1_ref[m * 512 : m * 512 + 512, :]
        h2_ref[0:128, :] = silu_of_half(dot(w2_ref[:, 0:512], both) + a_first[m]).astype(BF)
        h2_ref[128:256, :] = silu_of_half(dot(w2_ref[:, 0:256], both[256:512]) + a_second[m]).astype(BF)
        v = dot(w3_ref[...], h2_ref[...])
        pre_ref[m] = v[0:16] + shift_right(v[16:32])
        w = v[32:64] + v_ref[m]
        second.append(silu_of_half(w[0:16] + shift_right(w[16:32])).astype(BF))
    cols = y_ref.shape[1]
    tall = tail_ref.shape[0]
    tail_ref[:, 0:128] = jnp.zeros((tall, 128), F32)
    tail_ref[:, 128 + cols : 256 + cols] = jnp.zeros((tall, 128), F32)
    inside = slice(128, 128 + cols)
    tail_ref[0:32, inside] = dot(mix_ref[...], jnp.concatenate(second, axis=0))
    for r in range(mid_ref.shape[0]):
        tail_ref[(r + 1) * 32 : (r + 2) * 32, inside] = mid_ref[r]
    tail_ref[tall - 32 : tall, inside] = low_ref[...]


def chunk_kernel(nb, pre_ref, carry_ref, mix_ref, tail_ref, keep_ref, send_ref, head_ref):
    members, _, cols = pre_ref.shape
    carry = carry_ref[...].astype(F32) * is_row(0)
    first = [
        silu_of_half(pre_ref[m] + carry[m * 16 : m * 16 + 16]).astype(BF) for m in range(members)
    ]
    head_ref[:, 0:128] = jnp.zeros((32, 128), F32)
    head_ref[:, 128 + cols : 256 + cols] = jnp.zeros((32, 128), F32)
    head_ref[:, 128 : 128 + cols] = dot(mix_ref[...], jnp.concatenate(first, axis=0))

    me = lax.axis_index("mem")
    slots = lax.axis_size("mem") // 2
    tall = 32 + tail_ref.shape[0]

    def tile_at(base):
        at = pl.ds(pl.multiple_of(base, 128), 128)
        return jnp.concatenate([head_ref[:, at], tail_ref[:, at]], axis=0)

    def lanes_from(lane):
        v = tile_at(lane // 128 * 128)
        return v if nb % 128 == 0 else pltpu.roll(v, (128 - lane % 128) % 128, 1)

    lane_at = lax.broadcasted_iota(jnp.int32, (tall, 128), 1)
    edges = jnp.zeros((tall, 128), F32)
    for side, ref in enumerate((keep_ref, send_ref)):
        for k in range(slots):
            start = 128 + (me ^ (2 * k + side)) * nb
            ref[k, 0:tall, :] = lanes_from(start).astype(BF)
            if nb % 128 == 0:
                left = tile_at(start - 128)[:, 127:128]
            else:
                left = lanes_from(start - 1)[:, 0:1]
            right = lanes_from(start + nb)[:, 0:1]
            at = 2 * (side * slots + k)
            edges = jnp.where(lane_at == at, left, edges)
            edges = jnp.where(lane_at == at + 1, right, edges)
    turned = edges.T
    for side, ref in enumerate((keep_ref, send_ref)):
        for k in range(slots):
            at = 2 * (side * slots + k)
            ref[k, tall : tall + 16, :] = jnp.concatenate(
                [turned[at : at + 2], jnp.zeros((14, 128), F32)], axis=0
            ).astype(BF)


def pair_kernel(keep_ref, got_ref, own_ref, *out_refs):
    own_ref[...] = keep_ref[0].astype(F32) + got_ref[0].astype(F32)
    for k, ref in enumerate(out_refs):
        ref[...] = (keep_ref[k + 1].astype(F32) + got_ref[k + 1].astype(F32)).astype(BF)


def put_latent(ref, at, line):
    ext = line.shape[1]
    ref[at, 0:32, :] = pltpu.roll(line, 1, 1).astype(BF)
    ref[at, 32:64, :] = line.astype(BF)
    ref[at, 64:96, :] = pltpu.roll(line, ext - 1, 1).astype(BF)


def latent_kernel(nb, quarter, own_ref, *refs):
    ext_ref, first_ref, second_ref = refs[-3:]
    total = own_ref[...]
    for ref in refs[:-3]:
        total = total + ref[...].astype(F32)
    latent = silu_of_half(0.5 * total)
    tall = quarter * 32
    turned = jnp.concatenate([latent[tall : tall + 16], jnp.zeros((112, 128), F32)], axis=0).T
    ext = ext_ref.shape[2]
    lines = []
    for r in range(quarter):
        rows = slice(r * 32, (r + 1) * 32)
        line = [latent[rows, 0:nb], turned[rows, 1:2], jnp.zeros((32, ext - nb - 2), F32), turned[rows, 0:1]]
        lines.append(jnp.concatenate(line, axis=1))
        put_latent(ext_ref, r, lines[-1])
    odd = lax.rem(lax.axis_index("row"), 2) == 1
    first_ref[...] = jnp.where(odd, lines[0], lines[-1]).astype(BF)
    second_ref[...] = jnp.where(odd, lines[-1], lines[0]).astype(BF)


def weight_kernel(d1_ref, d2_ref, wd1, wd2):
    wd1[...] = jnp.zeros_like(wd1)
    wd2[...] = jnp.zeros_like(wd2)
    for pr, rr, tr in TRANSPOSED:
        for pc, cc, tc in TRANSPOSED:
            wd1[(pr * 2 + pc) * 32 : (pr * 2 + pc + 1) * 32, (rr * 3 + cc) * 32 : (rr * 3 + cc + 1) * 32] = (
                0.5 * d1_ref[tr * 4 + tc].astype(F32)
            ).astype(BF)
            for q in range(2):
                at = pr * 4 + 2 * q + pc
                to = rr * 4 + q + cc
                wd2[at * 16 : (at + 1) * 16, to * 32 : (to + 1) * 32] = d2_ref[tr * 4 + tc]


def decoder_kernel(nb, ext_ref, first_ref, second_ref, w1_ref, w2_ref, p_ref, r_ref, out_ref, l_ref, u_ref, g_ref):
    mem_at, mem_last = lax.axis_index("mem"), lax.axis_size("mem") - 1
    odd_row = lax.rem(lax.axis_index("row"), 2) == 1
    keep_first, keep_last = is_row(0), is_row(lax.axis_size("row") - 1)
    rows, _, wide = ext_ref.shape
    first, second = first_ref[...].astype(F32), second_ref[...].astype(F32)
    l_ref[0] = jnp.zeros_like(l_ref[0])
    l_ref[rows + 3] = jnp.zeros_like(l_ref[0])
    put_latent(l_ref, 1, jnp.where(odd_row, first, second) * keep_first)
    l_ref[2 : rows + 2] = ext_ref[...]
    put_latent(l_ref, rows + 2, jnp.where(odd_row, second, first) * keep_last)
    w1, w2 = w1_ref[...], w2_ref[...]
    lane = lax.broadcasted_iota(jnp.int32, (32, wide), 1)
    keep_odd = jnp.where((lane == wide - 1) & (mem_at == 0), 0.0, 1.0).astype(F32)
    keep_even = jnp.where((lane == nb) & (mem_at == mem_last), 0.0, 1.0).astype(F32)
    for a in range(-1, rows + 1):
        v = silu_of_half(dot(w1, l_ref[a + 1 : a + 4].reshape(288, wide)))
        for pr in range(2):
            row = 2 * a + pr
            if not -1 <= row <= 2 * rows:
                continue
            even = v[pr * 64 : pr * 64 + 32] * keep_even
            odd = v[pr * 64 + 32 : pr * 64 + 64] * keep_odd
            if row == -1:
                even, odd = even * keep_first, odd * keep_first
            if row == 2 * rows:
                even, odd = even * keep_last, odd * keep_last
            at = (row + 1) * 128
            u_ref[at : at + 32, :] = pltpu.roll(odd, 1, 1)[:, 0:nb].astype(BF)
            u_ref[at + 32 : at + 64, :] = even[:, 0:nb].astype(BF)
            u_ref[at + 64 : at + 96, :] = odd[:, 0:nb].astype(BF)
            u_ref[at + 96 : at + 128, :] = pltpu.roll(even, wide - 1, 1)[:, 0:nb].astype(BF)
    for a in range(2 * rows):
        v = dot(w2, u_ref[a * 128 : (a + 3) * 128, :]).astype(BF)
        for pr in range(2):
            for ph in range(4):
                g_ref[(2 * a + pr) * 16 : (2 * a + pr + 1) * 16, ph * nb : (ph + 1) * nb] = v[
                    (pr * 4 + ph) * 16 : (pr * 4 + ph + 1) * 16
                ]
    g = dot(r_ref[...], g_ref[...]).astype(BF)
    out_ref[...] = dot(g, p_ref[...]).astype(BF).reshape(out_ref.shape)


def shifted(value, by):
    peers = lax.axis_size("row")
    return lax.ppermute(value, "row", [(i, (i + by) % peers) for i in range(peers)])


def swapped(value, by):
    return lax.ppermute(value, "mem", [(i, i ^ by) for i in range(lax.axis_size("mem"))])


VMEM = pl.BlockSpec(memory_space=pltpu.VMEM)


def call(kernel, outs, scratch, *operands, mb=8):
    return pl.pallas_call(
        kernel,
        out_shape=[jax.ShapeDtypeStruct(*o) for o in outs],
        in_specs=[VMEM] * len(operands),
        out_specs=[VMEM] * len(outs),
        scratch_shapes=[pltpu.VMEM(*s) for s in scratch],
        compiler_params=pltpu.CompilerParams(vmem_limit_bytes=mb * 2**20),
    )(*operands)


def per_device(members, enc_first, enc_second, enc_third, mix_weight, dec_first, dec_second):
    count, channels, rows, wide = members.shape
    half, quarter = rows // 2, rows // 4
    cols = wide // 4
    peers, lines = lax.axis_size("mem"), lax.axis_size("row")
    nb = cols // peers
    lanes = 512
    chunks = wide // lanes
    x = members.reshape(count * channels * rows, wide)
    nd, nu = count * channels * UP, count * channels * DOWN
    per = padded(nd, 8), padded(nu, 8)
    total = padded(5 * per[0], 16), padded(5 * per[1], 16)
    pack = functools.partial(pack_kernel, count, channels, rows)
    sizes = [(nd * chunks, lanes), (nu * chunks, lanes)]
    down, up = call(pack, [(s, BF) for s in sizes], [(s, F32) for s in sizes], x, mb=16)
    up = shifted(up, -1)
    down = shifted(down, 1)

    w1 = enc_first.transpose(1, 2, 3, 0)
    w2 = enc_second.transpose(2, 3, 0, 1).reshape(9, 64, 64)
    w3 = enc_third.transpose(2, 3, 0, 1).reshape(9, 16, 64)
    row_f32 = ((count, 128, cols), F32)
    third_f32 = ((count, 32, cols), F32)
    (
        h_first, h_last, a_first, a_second, a_last, v_second, v_last, mid,
        w2_big, w3_big, w1_down, w1_up, spreads, mix,
    ) = call(
        functools.partial(inner_kernel, count, channels, rows, per),
        [row_f32] * 5
        + [third_f32] * 2
        + [
            ((quarter - 3, 32, cols), F32),
            ((128, 768), BF),
            ((64, 256), BF),
            ((count, 256, total[0]), BF),
            ((count, 128, total[1]), BF),
            ((2, 256, 256), BF),
            ((32, count * CH_BOT), BF),
        ],
        [
            ((48, 64), F32),
            ((640, 5 * channels * 8), BF),
            ((count, rows // 8, 5 * channels * 8, cols), F32),
            ((rows // 8, 640, cols), F32),
            ((256 * (half - 1), cols), BF),
            ((256, cols), BF),
        ],
        x, w1, w2, w3, mix_weight, mb=28,
    )
    low, carry = call(
        functools.partial(low_kernel, count, channels, per[1]),
        [((32, cols), F32), ((count * CH_BOT, cols), BF)],
        [((total[1], cols), F32), ((count * 256, cols), BF)],
        up, spreads, w1_up, h_last, w2_big, a_last, w3_big, v_last, mix, mb=16,
    )
    carry = shifted(carry, 1)
    pre, tail = call(
        functools.partial(top_kernel, count, channels, per[0]),
        [((count, CH_BOT, cols), F32), ((quarter * 32 - 32, cols + 256), F32)],
        [((total[0], cols), F32), ((count * 512, cols), BF), ((256, cols), BF)],
        down, spreads, w1_down, h_first, w2_big, a_first, a_second, w3_big, v_second, mix, mid, low, mb=16,
    )
    slots = peers // 2
    chunk = (quarter * 32 + 16, 128)
    keep, send = call(
        functools.partial(chunk_kernel, nb),
        [((slots,) + chunk, BF)] * 2,
        [((32, cols + 256), F32)],
        pre, carry, mix, tail,
    )
    got = swapped(send, 1)
    mine, *others = call(pair_kernel, [(chunk, F32)] + [(chunk, BF)] * (slots - 1), [], keep, got)
    order = sorted(range(slots - 1), key=lambda k: (k == 0, k))
    moved = {k: swapped(others[k], 2 * (k + 1)) for k in order}
    ext = padded(nb + 2, 128)
    latent, first, second = call(
        functools.partial(latent_kernel, nb, quarter),
        [((quarter, 96, ext), BF), ((32, ext), BF), ((32, ext), BF)],
        [],
        mine, *[moved[k] for k in range(slots - 1)],
    )
    first = lax.ppermute(first, "row", [(i, i ^ 1) for i in range(lines)])
    second = lax.ppermute(second, "row", [(i, (i + 1 if i % 2 else i - 1) % lines) for i in range(lines)])

    d1, d2, _ = lax.optimization_barrier((dec_first, dec_second, others[0]))
    d1 = d1.transpose(2, 3, 0, 1).reshape(16, 32, 32)
    d2 = d2.transpose(2, 3, 0, 1).reshape(16, 16, 32)
    wd1, wd2 = call(weight_kernel, [((128, 288), BF), ((128, 384), BF)], [], d1, d2)
    reorder = np.zeros((16 * rows, 16 * rows), np.float32)
    for r in range(rows):
        for level in range(16):
            reorder[level * rows + r, r * 16 + level] = 1
    (out,) = call(
        functools.partial(decoder_kernel, nb),
        [((16, rows, 4 * nb), BF)],
        [((quarter + 4, 96, ext), BF), ((128 * (half + 2), nb), BF), ((16 * rows, 4 * nb), BF)],
        latent, first, second, wd1, wd2, jnp.asarray(spread(4, nb).T, BF), jnp.asarray(reorder, BF),
    )
    return out


def solution(mesh):
    placed = (P("mem", None, "row", None), P(), P(), P(), P(), P(), P())
    return jax.shard_map(
        per_device, mesh=mesh, in_specs=placed, out_specs=P(None, "row", "mem"), check_vma=False
    )
```

time: 54 us -> 40.2 us (0.74)
  local copies, waits for them, and re-layouts: 8.46 us -> 4.5 us
  Pallas kernels: 16.6 us -> 13.2 us
  starting transfers between devices: 16.6 us -> 13.3 us
  waiting for transfers between devices: 11.6 us -> 8.76 us
    ppermute x4 -> x5, starting transfers between devices: 12.1 us -> 8.58 us  [the longest x3 5.55 us: shifted(): lax.ppermute(value, 'row', [(i, (i + by) % peers) for i in range(peers)])]
    pallas_call x7 -> x9, Pallas kernels: 16.6 us -> 13.2 us  [call(): pl.pallas_call(kernel, out_shape=[jax.ShapeDtypeStruct(*o) for o in outs]...]
    transpose x2, local copies, waits for them, and re-layouts: 1.8 us -> 0.05 us  [the longest x1 0.04 us: per_device(): d1 = d1.transpose(2, 3, 0, 1).reshape(16, 32, 32)]
    ppermute x4 -> x5, waiting for transfers between devices: 4.7 us -> 3.22 us  [the longest x3 1.59 us: shifted(): lax.ppermute(value, 'row', [(i, (i + by) % peers) for i in range(peers)])]
    unnamed x22 -> x20, local copies, waits for them, and re-layouts: 5.83 us -> 4.45 us
    ppermute x4, waiting for transfers between devices: 6.89 us -> 5.54 us  [swapped(): lax.ppermute(value, 'mem', [(i, i ^ by) for i in range(lax.axis_size('mem...]
    reshape x1 -> x0, local copies, waits for them, and re-layouts: 0.74 us -> none  [per_device(): enc_first.transpose(1, 2, 3, 0).reshape(channels * 9, 64)]
  transfers between devices with their start and end apart: 8 -> 9, of which waited for: 5 -> 6; matrix products, arithmetic and copies ran while one was open for 5% -> 0% of each run, Pallas kernels for 18% -> 26%
where the time goes in v2:
time: 40.2 us; the launch traced here: 39.8 us
  starting transfers between devices  13.3 us (33%)
  Pallas kernels  13.2 us (33%)
  waiting for transfers between devices  8.76 us (22%)
  local copies, waits for them, and re-layouts  4.5 us (11%)
    pallas_call x9, Pallas kernels, call(): pl.pallas_call(kernel, out_shape=[jax.ShapeDtypeStruct(*o) for o in outs]...  13.2 us
    ppermute x3, starting transfers between devices, shifted(): lax.ppermute(value, 'row', [(i, (i + by) % peers) for i in range(peers)])  5.55 us
    ppermute x4, waiting for transfers between devices, swapped(): lax.ppermute(value, 'mem', [(i, i ^ by) for i in range(lax.axis_size('mem...  5.54 us
    ppermute x4, starting transfers between devices, swapped(): lax.ppermute(value, 'mem', [(i, i ^ by) for i in range(lax.axis_size('mem...  4.69 us
    unnamed x20, local copies, waits for them, and re-layouts  4.45 us
    ppermute x1, starting transfers between devices, per_device(): lax.ppermute(second, 'row', [(i, (i + 1 if i % 2 else i - 1) % lines) for...  2.79 us
    ppermute x3, waiting for transfers between devices, shifted(): lax.ppermute(value, 'row', [(i, (i + by) % peers) for i in range(peers)])  1.59 us
    ppermute x1, waiting for transfers between devices, per_device(): lax.ppermute(second, 'row', [(i, (i + 1 if i % 2 else i - 1) % lines) for...  1.12 us
  transfers between devices with their start and end apart: 9, of which 6 were waited for; matrix products, arithmetic and copies ran while one was open for 0% of the time, Pallas kernels for 26%

profile of v2, /device:TPU:0, one launch (start us, length us, event | category | flops | bytes accessed | tf_op | source)
XLA Modules:
  0.0 39.8 jit_solution(7391773057447713748)
XLA Ops:
  0.0 0.0 copy-start
  0.0 1.3 %copy-done = bf16[2,5,16,4096]{3,2,1,0:T(8,128)(2,1)S(1)} copy-done((bf16[2,5,16,4096]{3,2,1,0:T(8,128)(2,1)S(1)}, bf16[2,5,16,4096]{3,2,1,0:T(8,128)(2,1)}, u32[]{:S(2)}) %copy-start) | copy-done | bytes 1310744
  1.3 0.0 copy-start.1
  1.3 0.2 shard_map.91
  1.6 3.0 %collective-permute-start = (bf16[240,512]{1,0:T(8,128)(2,1)S(1)}, bf16[240,512]{1,0:T(8,128)(2,1)S(1)}, u32[]{:S(2)}, u32[]{:S(2)}) collective-permute-start(bf16[240,512]{1,0:T(8,128)(2,1)S(1)} %get-tuple-element.38), channel_id=1, source_target_pairs={{0,1},{1,2},{2,3},{3,0},{4,5},{5,6},{6,7},{7,4},{8,9},{9,10},{10,1... | collective-permute-start | bytes 737288 | tf_op jit(solution)/shard_map/ppermute | solution.py:399
  4.5 1.0 %collective-permute-start.1 = (bf16[160,512]{1,0:T(8,128)(2,1)S(1)}, bf16[160,512]{1,0:T(8,128)(2,1)S(1)}, u32[]{:S(2)}, u32[]{:S(2)}) collective-permute-start(bf16[160,512]{1,0:T(8,128)(2,1)S(1)} %get-tuple-element.49), channel_id=1, source_target_pairs={{0,3},{1,0},{2,1},{3,2},{4,7},{5,4},{6,5},{7,6},{8,11},{9,8},{10,9... | collective-permute-start | bytes 491528 | tf_op jit(solution)/shard_map/ppermute | solution.py:399
  5.6 0.0 copy-done.1
  5.6 0.0 copy-start.3
  5.6 0.9 %copy-done.3 = bf16[64,64,3,3]{1,0,3,2:T(8,128)(2,1)S(1)} copy-done((bf16[64,64,3,3]{1,0,3,2:T(8,128)(2,1)S(1)}, bf16[64,64,3,3]{1,0,3,2:T(8,128)(2,1)}, u32[]{:S(2)}) %copy-start.3) | copy-done | bytes 73752
  6.5 0.0 copy-start.5
  6.5 0.8 %copy-done.5 = bf16[16,64,3,3]{1,0,3,2:T(8,128)(2,1)S(1)} copy-done((bf16[16,64,3,3]{1,0,3,2:T(8,128)(2,1)S(1)}, bf16[16,64,3,3]{1,0,3,2:T(8,128)(2,1)}, u32[]{:S(2)}) %copy-start.5) | copy-done | bytes 18456
  7.3 0.0 copy-start.6
  7.3 0.7 %copy-done.6 = bf16[32,256]{1,0:T(8,128)(2,1)S(1)} copy-done((bf16[32,256]{1,0:T(8,128)(2,1)S(1)}, bf16[32,256]{1,0:T(8,128)(2,1)}, u32[]{:S(2)}) %copy-start.6) | copy-done | bytes 16408
  8.0 0.0 copy-start.7
  8.0 0.7 %copy-done.7 = bf16[64,5,3,3]{0,3,2,1:T(4,128)(2,1)S(1)} copy-done((bf16[64,5,3,3]{0,3,2,1:T(4,128)(2,1)S(1)}, bf16[64,5,3,3]{0,3,2,1:T(4,128)(2,1)}, u32[]{:S(2)}) %copy-start.7) | copy-done | bytes 5784
  8.7 6.5 %shard_map.92 = (f32[2,128,1024]{2,1,0:T(8,128)S(1)}, f32[2,128,1024]{2,1,0:T(8,128)S(1)}, f32[2,128,1024]{2,1,0:T(8,128)S(1)}, f32[2,128,1024]{2,1,0:T(8,128)S(...) custom-call(bf16[160,4096]{1,0:T(8,128)(2,1)S(1)} %bitcast.13, ...), custom_call_target="tpu_custom_call" | custom-call | tf_op jit(solution)/shard_map/pallas_call | solution.py:410
  15.2 0.0 collective-permute-done.1.got_ref
  15.2 1.7 %shard_map.93 = (f32[32,1024]{1,0:T(8,128)S(1)}, bf16[32,1024]{1,0:T(8,128)(2,1)S(1)}) custom-call(bf16[160,512]{1,0:T(8,128)(2,1)S(1)} %collective-permute-done.1.got_ref, bf16[2,256,256]{2,1,0:T(8,128)(2,1)S(1)} %get-tuple-element.39.spread_ref, bf16[2,128,128]{2,1,0:T(8,128)(2,1)S(1)} %get-tuple-element.50.w1_ref, ...), custom_call_target="tpu_custom_call" | custom-call | tf_op jit(solution)/shard_map/pallas_call | solution.py:410
  16.9 1.5 %collective-permute-start.2 = (bf16[32,1024]{1,0:T(8,128)(2,1)S(1)}, bf16[32,1024]{1,0:T(8,128)(2,1)S(1)}, u32[]{:S(2)}, u32[]{:S(2)}) collective-permute-start(bf16[32,1024]{1,0:T(8,128)(2,1)S(1)} %get-tuple-element.56), channel_id=1, source_target_pairs={{0,1},{1,2},{2,3},{3,0},{4,5},{5,6},{6,7},{7,4},{8,9},{9,10},{10,1... | collective-permute-start | bytes 196616 | tf_op jit(solution)/shard_map/ppermute | solution.py:399
  18.5 0.0 collective-permute-done.got_ref
  18.5 0.0 copy-start.9
  18.5 2.1 %shard_map.94 = (f32[2,16,1024]{2,1,0:T(8,128)S(1)}, f32[96,1280]{1,0:T(8,128)S(1)}) custom-call(bf16[240,512]{1,0:T(8,128)(2,1)S(1)} %collective-permute-done.got_ref, bf16[2,256,256]{2,1,0:T(8,128)(2,1)S(1)} %get-tuple-element.39.spread_ref, bf16[2,256,160]{2,1,0:T(8,128)(2,1)S(1)} %get-tuple-element.40.w1_ref, ...), custom_call_target="tpu_custom_call" | custom-call | tf_op jit(solution)/shard_map/pallas_call | solution.py:410
  20.6 0.0 copy-start.8
  20.6 0.0 copy-start.2
  20.6 0.0 copy-start.4
  20.6 1.5 %collective-permute-done.2.carry_ref = bf16[32,1024]{1,0:T(8,128)(2,1)S(1)} collective-permute-done((bf16[32,1024]{1,0:T(8,128)(2,1)S(1)}, bf16[32,1024]{1,0:T(8,128)(2,1)S(1)}, u32[]{:S(2)}, u32[]{:S(2)}) %collective-permute-start.2) | collective-permute-done | bytes 65568 | tf_op jit(solution)/shard_map/ppermute | solution.py:399
  22.1 0.4 shard_map.95
  22.5 0.0 collective-permute-start.3
  22.6 1.4 %collective-permute-done.3.got_ref = bf16[4,144,128]{2,1,0:T(8,128)(2,1)S(1)} collective-permute-done((bf16[4,144,128]{2,1,0:T(8,128)(2,1)S(1)}, bf16[4,144,128]{2,1,0:T(8,128)(2,1)S(1)}, u32[]{:S(2)}, u32[]{:S(2)}) %collective-permute-start.3) | collective-permute-done | bytes 147488 | tf_op jit(solution)/shard_map/ppermute | solution.py:403
  24.0 3.1 %collective-permute-start.5 = (bf16[144,128]{1,0:T(8,128)(2,1)S(1)}, bf16[144,128]{1,0:T(8,128)(2,1)S(1)}, u32[]{:S(2)}, u32[]{:S(2)}) collective-permute-start(bf16[144,128]{1,0:T(8,128)(2,1)S(1)} %get-tuple-element.62), channel_id=1, source_target_pairs={{0,16},{4,20},{8,24},{12,28},{16,0},{20,4},{24,8},{28,12},{1,17},{... | collective-permute-start | bytes 110600 | tf_op jit(solution)/shard_map/ppermute | solution.py:403
  27.0 1.3 %collective-permute-start.6 = (bf16[144,128]{1,0:T(8,128)(2,1)S(1)}, bf16[144,128]{1,0:T(8,128)(2,1)S(1)}, u32[]{:S(2)}, u32[]{:S(2)}) collective-permute-start(bf16[144,128]{1,0:T(8,128)(2,1)S(1)} %get-tuple-element.63), channel_id=1, source_target_pairs={{0,24},{4,28},{8,16},{12,20},{16,8},{20,12},{24,0},{28,4},{1,25},{... | collective-permute-start | bytes 110600 | tf_op jit(solution)/shard_map/ppermute | solution.py:403
  28.4 0.2 collective-permute-start.4
  28.6 0.4 collective-permute-done.5.refs_1_
  29.0 3.8 %collective-permute-done.6.refs_2_ = bf16[144,128]{1,0:T(8,128)(2,1)S(1)} collective-permute-done((bf16[144,128]{1,0:T(8,128)(2,1)S(1)}, bf16[144,128]{1,0:T(8,128)(2,1)S(1)}, u32[]{:S(2)}, u32[]{:S(2)}) %collective-permute-start.6) | collective-permute-done | bytes 36896 | tf_op jit(solution)/shard_map/ppermute | solution.py:403
  32.8 0.0 collective-permute-done.4.refs_0_
  32.8 0.3 shard_map.97
  33.0 0.3 collective-permute-start.7
  33.3 2.8 %collective-permute-start.8 = (bf16[32,256]{1,0:T(8,128)(2,1)S(1)}, bf16[32,256]{1,0:T(8,128)(2,1)S(1)}, u32[]{:S(2)}, u32[]{:S(2)}) collective-permute-start(bf16[32,256]{1,0:T(8,128)(2,1)S(1)} %get-tuple-element.66), channel_id=1, source_target_pairs={{0,3},{1,2},{2,1},{3,0},{4,7},{5,6},{6,5},{7,4},{8,11},{9,10},{10,... | collective-permute-start | bytes 49160 | tf_op jit(solution)/shard_map/ppermute | solution.py:502
  36.1 0.0 copy-done.9
  36.1 0.0 copy-done.8
  36.2 0.2 shard_map.98
  36.3 0.5 %collective-permute-done.7.first_ref = bf16[32,256]{1,0:T(8,128)(2,1)S(1)} collective-permute-done((bf16[32,256]{1,0:T(8,128)(2,1)S(1)}, bf16[32,256]{1,0:T(8,128)(2,1)S(1)}, u32[]{:S(2)}, u32[]{:S(2)}) %collective-permute-start.7) | collective-permute-done | bytes 16416 | tf_op jit(solution)/shard_map/ppermute | solution.py:501
  36.8 1.1 %collective-permute-done.8.second_ref = bf16[32,256]{1,0:T(8,128)(2,1)S(1)} collective-permute-done((bf16[32,256]{1,0:T(8,128)(2,1)S(1)}, bf16[32,256]{1,0:T(8,128)(2,1)S(1)}, u32[]{:S(2)}, u32[]{:S(2)}) %collective-permute-start.8) | collective-permute-done | bytes 16416 | tf_op jit(solution)/shard_map/ppermute | solution.py:502
  38.0 0.0 copy-done.2
  38.0 0.0 copy-done.4
  38.0 1.9 %shard_map.99 = bf16[16,16,512]{2,1,0:T(8,128)(2,1)} custom-call(bf16[4,96,256]{2,1,0:T(8,128)(2,1)S(1)} %get-tuple-element.64.ext_ref, bf16[32,256]{1,0:T(8,128)(2,1)S(1)} %collective-permute-done.7.first_ref, bf16[32,256]{1,0:T(8,128)(2,1)S(1)} %collective-permute-done.8.second_ref, bf16[128,288]{1,0:T(8,128)(2,1)S(1)} %get-tuple-element.69.w1_ref, ...), custom_call_target="tpu_custom_call" | custom-call | tf_op jit(solution)/shard_map/pallas_call | solution.py:410
  (3 shorter events, 0.1 us)
Async XLA Ops:
  0.0 1.3 %copy-start = (bf16[2,5,16,4096]{3,2,1,0:T(8,128)(2,1)S(1)}, bf16[2,5,16,4096]{3,2,1,0:T(8,128)(2,1)}, u32[]{:S(2)}) copy-start(bf16[2,5,16,4096]{3,2,1,0:T(8,128)(2,1)} %param.9) | copy-start | bytes 3932164
  1.3 4.3 %copy-start.1 = (bf16[2,5,16,4096]{3,2,1,0:T(8,128)(2,1)S(1)}, bf16[2,5,16,4096]{3,2,1,0:T(8,128)(2,1)}, u32[]{:S(2)}) copy-start(bf16[2,5,16,4096]{3,2,1,0:T(8,128)(2,1)} %param.9) | copy-start | bytes 3932164
  1.6 16.9 %collective-permute-start = (bf16[240,512]{1,0:T(8,128)(2,1)S(1)}, bf16[240,512]{1,0:T(8,128)(2,1)S(1)}, u32[]{:S(2)}, u32[]{:S(2)}) collective-permute-start(bf16[240,512]{1,0:T(8,128)(2,1)S(1)} %get-tuple-element.38), channel_id=1, source_target_pairs={{0,1},{1,2},{2,3},{3,0},{4,5},{5,6},{6,7},{7,4},{8,9},{9,10},{10,1... | collective-permute-start | bytes 737288 | tf_op jit(solution)/shard_map/ppermute | solution.py:399
  4.5 10.7 %collective-permute-start.1 = (bf16[160,512]{1,0:T(8,128)(2,1)S(1)}, bf16[160,512]{1,0:T(8,128)(2,1)S(1)}, u32[]{:S(2)}, u32[]{:S(2)}) collective-permute-start(bf16[160,512]{1,0:T(8,128)(2,1)S(1)} %get-tuple-element.49), channel_id=1, source_target_pairs={{0,3},{1,0},{2,1},{3,2},{4,7},{5,4},{6,5},{7,6},{8,11},{9,8},{10,9... | collective-permute-start | bytes 491528 | tf_op jit(solution)/shard_map/ppermute | solution.py:399
  5.6 0.9 %copy-start.3 = (bf16[64,64,3,3]{1,0,3,2:T(8,128)(2,1)S(1)}, bf16[64,64,3,3]{1,0,3,2:T(8,128)(2,1)}, u32[]{:S(2)}) copy-start(bf16[64,64,3,3]{1,0,3,2:T(8,128)(2,1)} %param.11) | copy-start | bytes 221188
  6.5 0.8 %copy-start.5 = (bf16[16,64,3,3]{1,0,3,2:T(8,128)(2,1)S(1)}, bf16[16,64,3,3]{1,0,3,2:T(8,128)(2,1)}, u32[]{:S(2)}) copy-start(bf16[16,64,3,3]{1,0,3,2:T(8,128)(2,1)} %param.12) | copy-start | bytes 55300
  7.3 0.7 %copy-start.6 = (bf16[32,256]{1,0:T(8,128)(2,1)S(1)}, bf16[32,256]{1,0:T(8,128)(2,1)}, u32[]{:S(2)}) copy-start(bf16[32,256]{1,0:T(8,128)(2,1)} %mix_ref.1) | copy-start | bytes 49156
  8.0 0.7 %copy-start.7 = (bf16[64,5,3,3]{0,3,2,1:T(4,128)(2,1)S(1)}, bf16[64,5,3,3]{0,3,2,1:T(4,128)(2,1)}, u32[]{:S(2)}) copy-start(bf16[64,5,3,3]{0,3,2,1:T(4,128)(2,1)} %param.10) | copy-start | bytes 17284
  16.9 5.2 %collective-permute-start.2 = (bf16[32,1024]{1,0:T(8,128)(2,1)S(1)}, bf16[32,1024]{1,0:T(8,128)(2,1)S(1)}, u32[]{:S(2)}, u32[]{:S(2)}) collective-permute-start(bf16[32,1024]{1,0:T(8,128)(2,1)S(1)} %get-tuple-element.56), channel_id=1, source_target_pairs={{0,1},{1,2},{2,3},{3,0},{4,5},{5,6},{6,7},{7,4},{8,9},{9,10},{10,1... | collective-permute-start | bytes 196616 | tf_op jit(solution)/shard_map/ppermute | solution.py:399
  18.5 17.6 %copy-start.9 = (bf16[16,32,4,4]{1,3,2,0:T(4,128)(2,1)S(1)}, bf16[16,32,4,4]{1,3,2,0:T(4,128)(2,1)}, u32[]{:S(2)}) copy-start(bf16[16,32,4,4]{1,3,2,0:T(4,128)(2,1)} %param.15) | copy-start | bytes 49156
  20.6 15.5 %copy-start.8 = (bf16[32,32,4,4]{1,3,2,0:T(4,128)(2,1)S(1)}, bf16[32,32,4,4]{1,3,2,0:T(4,128)(2,1)}, u32[]{:S(2)}) copy-start(bf16[32,32,4,4]{1,3,2,0:T(4,128)(2,1)} %param.14) | copy-start | bytes 98308
  20.6 17.4 %copy-start.2 = (bf16[512,512]{1,0:T(8,128)(2,1)S(1)}, bf16[512,512]{1,0:T(8,128)(2,1)}, u32[]{:S(2)}) copy-start(bf16[512,512]{1,0:T(8,128)(2,1)} %constant.4.clone.p_ref) | copy-start | bytes 1572868
  20.6 17.4 %copy-start.4 = (bf16[256,256]{1,0:T(8,128)(2,1)S(1)}, bf16[256,256]{1,0:T(8,128)(2,1)}, u32[]{:S(2)}) copy-start(bf16[256,256]{1,0:T(8,128)(2,1)} %constant.5.clone.r_ref) | copy-start | bytes 393220
  22.5 1.4 %collective-permute-start.3 = (bf16[4,144,128]{2,1,0:T(8,128)(2,1)S(1)}, bf16[4,144,128]{2,1,0:T(8,128)(2,1)S(1)}, u32[]{:S(2)}, u32[]{:S(2)}) collective-permute-start(bf16[4,144,128]{2,1,0:T(8,128)(2,1)S(1)} %get-tuple-element.59), channel_id=1, source_target_pairs={{0,4},{4,0},{8,12},{12,8},{16,20},{20,16},{24,28},{28,24},{1,5},{5... | collective-permute-start | bytes 442376 | tf_op jit(solution)/shard_map/ppermute | solution.py:403
  24.0 5.0 %collective-permute-start.5 = (bf16[144,128]{1,0:T(8,128)(2,1)S(1)}, bf16[144,128]{1,0:T(8,128)(2,1)S(1)}, u32[]{:S(2)}, u32[]{:S(2)}) collective-permute-start(bf16[144,128]{1,0:T(8,128)(2,1)S(1)} %get-tuple-element.62), channel_id=1, source_target_pairs={{0,16},{4,20},{8,24},{12,28},{16,0},{20,4},{24,8},{28,12},{1,17},{... | collective-permute-start | bytes 110600 | tf_op jit(solution)/shard_map/ppermute | solution.py:403
  27.0 5.8 %collective-permute-start.6 = (bf16[144,128]{1,0:T(8,128)(2,1)S(1)}, bf16[144,128]{1,0:T(8,128)(2,1)S(1)}, u32[]{:S(2)}, u32[]{:S(2)}) collective-permute-start(bf16[144,128]{1,0:T(8,128)(2,1)S(1)} %get-tuple-element.63), channel_id=1, source_target_pairs={{0,24},{4,28},{8,16},{12,20},{16,8},{20,12},{24,0},{28,4},{1,25},{... | collective-permute-start | bytes 110600 | tf_op jit(solution)/shard_map/ppermute | solution.py:403
  28.4 4.4 %collective-permute-start.4 = (bf16[144,128]{1,0:T(8,128)(2,1)S(1)}, bf16[144,128]{1,0:T(8,128)(2,1)S(1)}, u32[]{:S(2)}, u32[]{:S(2)}) collective-permute-start(bf16[144,128]{1,0:T(8,128)(2,1)S(1)} %get-tuple-element.61), channel_id=1, source_target_pairs={{0,8},{4,12},{8,0},{12,4},{16,24},{20,28},{24,16},{28,20},{1,9},{5... | collective-permute-start | bytes 110600 | tf_op jit(solution)/shard_map/ppermute | solution.py:403
  33.0 3.8 %collective-permute-start.7 = (bf16[32,256]{1,0:T(8,128)(2,1)S(1)}, bf16[32,256]{1,0:T(8,128)(2,1)S(1)}, u32[]{:S(2)}, u32[]{:S(2)}) collective-permute-start(bf16[32,256]{1,0:T(8,128)(2,1)S(1)} %get-tuple-element.65), channel_id=1, source_target_pairs={{0,1},{1,0},{2,3},{3,2},{4,5},{5,4},{6,7},{7,6},{8,9},{9,8},{10,11... | collective-permute-start | bytes 49160 | tf_op jit(solution)/shard_map/ppermute | solution.py:501
  33.3 4.7 %collective-permute-start.8 = (bf16[32,256]{1,0:T(8,128)(2,1)S(1)}, bf16[32,256]{1,0:T(8,128)(2,1)S(1)}, u32[]{:S(2)}, u32[]{:S(2)}) collective-permute-start(bf16[32,256]{1,0:T(8,128)(2,1)S(1)} %get-tuple-element.66), channel_id=1, source_target_pairs={{0,3},{1,2},{2,1},{3,0},{4,7},{5,6},{6,5},{7,4},{8,11},{9,10},{10,... | collective-permute-start | bytes 49160 | tf_op jit(solution)/shard_map/ppermute | solution.py:502

commit v3 on v2

--- a/solution.py
+++ b/solution.py
@@ -98,9 +98,9 @@
 def inner_kernel(
     members, channels, rows, per,
     x_ref, w1_ref, w2_ref, w3_ref, mix_ref,
-    h_first, h_last, a_first, a_second, a_last, v_second, v_last, mixed_ref,
+    h1_ref, h_first, h_last, a_last, v_second, v_third,
     w2_big, w3_big, w1_down, w1_up, spread_ref, mix_own,
-    w1_flat, w1_own, y_ref, out1_ref, h1_ref, h2_ref,
+    w1_flat, w1_own, y_ref, out1_ref, h2_ref,
 ):
     half, groups = rows // 2, rows // 8
     wide = x_ref.shape[1]
@@ -178,60 +178,71 @@
         for g in range(groups):
             y_ref[m, g, 0:c8, :] = shift_right(y_ref[m, g, 4 * c8 : 5 * c8, :])
 
-    mids = []
     for m in range(members):
         for g in range(groups):
             out1_ref[g] = dot(w1_own[...], y_ref[m, g].astype(BF))
         h_first[m] = out1_ref[0, 0:128]
         h_last[m] = out1_ref[groups - 1, 512:640]
+        rows_of = h1_ref.at[m]
         for h in range(1, half):
             g, j = h // 4, h % 4
             v = out1_ref[g, j * 128 : j * 128 + 128]
             if j == 0:
                 v = v + out1_ref[g - 1, 512:640]
-            put_hidden(h1_ref, h - 1, silu_of_half(v))
-        a_first[m] = dot(w2_big[:, 512:768], h1_ref[0:256, :])
-        a_second[m] = dot(w2_big[:, 256:768], h1_ref[0:512, :])
-        a_last[m] = dot(w2_big[:, 0:512], h1_ref[(half - 3) * 256 : (half - 1) * 256, :])
-        carry = None
-        for o in range(2, half - 1):
-            h2_ref[(o % 2) * 128 : (o % 2) * 128 + 128, :] = silu_of_half(
-                dot(w2_big[...], h1_ref[(o - 2) * 256 : (o + 1) * 256, :])
+            put_hidden(rows_of, h - 1, silu_of_half(v))
+        a_last[m] = dot(w2_big[:, 0:512], h1_ref[m, (half - 3) * 256 : (half - 1) * 256, :])
+        for o in range(2):
+            h2_ref[o * 128 : o * 128 + 128, :] = silu_of_half(
+                dot(w2_big[...], h1_ref[m, o * 256 : (o + 3) * 256, :])
             ).astype(BF)
-            if o % 2:
-                v = dot(w3_big[...], h2_ref[...])
-                if o == 3:
-                    v_second[m] = v[0:32]
-                else:
-                    w = v[0:32] + carry
-                    mids.append((o // 2, silu_of_half(w[0:16] + shift_right(w[16:32])).astype(BF)))
-                carry = v[32:64]
-        v_last[m] = carry + dot(w3_big[0:32, 0:128], h2_ref[0:128, :])
-    for r in range(2, half // 2 - 1):
-        mixed_ref[r - 2] = dot(mix, jnp.concatenate([b for s, b in mids if s == r], axis=0))
+        v = dot(w3_big[...], h2_ref[...])
+        v_second[m] = v[0:32]
+        v_third[m] = v[32:64]
 
 
 def low_kernel(
     members, channels, per,
-    got_ref, spread_ref, w1_ref, h_ref, w2_ref, a_ref, w3_ref, v_ref, mix_ref,
-    mixed_ref, carry_ref, y_ref, h1_ref,
+    got_ref, spread_ref, w1_ref, h_ref, w2_ref, a_ref, w3_ref,
+    h2_ref, carry_ref, y_ref, h1_ref,
 ):
     below = is_row(lax.axis_size("row") - 1)
     y = place_halo(got_ref[...], spread_ref, y_ref, members * channels * DOWN, per)
-    parts = []
     for m in range(members):
         put_hidden(h1_ref, m, silu_of_half((dot(w1_ref[m], y) + h_ref[m]) * below))
         h2 = silu_of_half(dot(w2_ref[:, 512:768], h1_ref[m * 256 : m * 256 + 256, :]) + a_ref[m]).astype(BF)
-        v = dot(w3_ref[:, 128:256], h2)
-        carry_ref[m * 16 : m * 16 + 16, :] = (v[32:48] + shift_right(v[48:64])).astype(BF)
-        w = v[0:32] + v_ref[m]
-        parts.append(silu_of_half(w[0:16] + shift_right(w[16:32])).astype(BF))
-    mixed_ref[...] = dot(mix_ref[...], jnp.concatenate(parts, axis=0))
+        h2_ref[m] = h2
+        v = dot(w3_ref[32:64, 128:256], h2)
+        carry_ref[m * 16 : m * 16 + 16, :] = (v[0:16] + shift_right(v[16:32])).astype(BF)
+
+
+def middle_kernel(
+    members, half,
+    h1_ref, h2_low, w2_ref, w3_ref, v_ref, mix_ref,
+    a_first, a_second, mixed_ref, h2_ref,
+):
+    parts = {}
+    for m in range(members):
+        a_first[m] = dot(w2_ref[:, 512:768], h1_ref[m, 0:256, :])
+        a_second[m] = dot(w2_ref[:, 256:768], h1_ref[m, 0:512, :])
+        carry = v_ref[m]
+        for a in range(4, half, 2):
+            for o in (a, a + 1):
+                at = slice((o - a) * 128, (o - a) * 128 + 128)
+                if o == half - 1:
+                    h2_ref[at, :] = h2_low[m]
+                else:
+                    h2_ref[at, :] = silu_of_half(dot(w2_ref[...], h1_ref[m, (o - 2) * 256 : (o + 1) * 256, :])).astype(BF)
+            v = dot(w3_ref[...], h2_ref[...])
+            w = v[0:32] + carry
+            carry = v[32:64]
+            parts[a // 2, m] = silu_of_half(w[0:16] + shift_right(w[16:32])).astype(BF)
+    for r in range(2, half // 2):
+        mixed_ref[r - 2] = dot(mix_ref[...], jnp.concatenate([parts[r, m] for m in range(members)], axis=0))
 
 
 def top_kernel(
     members, channels, per,
-    got_ref, spread_ref, w1_ref, h_ref, w2_ref, a_first, a_second, w3_ref, v_ref, mix_ref, mid_ref, low_ref,
+    got_ref, spread_ref, w1_ref, h_ref, w2_ref, a_first, a_second, w3_ref, v_ref, mix_ref, mid_ref,
     pre_ref, tail_ref, y_ref, h1_ref, h2_ref,
 ):
     source = (got_ref[...].astype(F32) * is_row(0)).astype(BF)
@@ -256,7 +267,6 @@
     tail_ref[0:32, inside] = dot(mix_ref[...], jnp.concatenate(second, axis=0))
     for r in range(mid_ref.shape[0]):
         tail_ref[(r + 1) * 32 : (r + 2) * 32, inside] = mid_ref[r]
-    tail_ref[tall - 32 : tall, inside] = low_ref[...]
 
 
 def chunk_kernel(nb, pre_ref, carry_ref, mix_ref, tail_ref, keep_ref, send_ref, head_ref):
@@ -337,7 +347,62 @@
     second_ref[...] = jnp.where(odd, lines[-1], lines[0]).astype(BF)
 
 
-def weight_kernel(d1_ref, d2_ref, wd1, wd2):
+def upsample_row(w1, l_ref, a, keep_even, keep_odd, rows, u_ref, wanted, keeps):
+    wide = l_ref.shape[2]
+    nb = u_ref.shape[1]
+    v = silu_of_half(dot(w1, l_ref[a + 1 : a + 4].reshape(288, wide)))
+    for pr in range(2):
+        row = 2 * a + pr
+        if row not in wanted:
+            continue
+        even = v[pr * 64 : pr * 64 + 32] * keep_even
+        odd = v[pr * 64 + 32 : pr * 64 + 64] * keep_odd
+        if row in keeps:
+            even, odd = even * keeps[row], odd * keeps[row]
+        at = (row + 1) * 128
+        u_ref[at : at + 32, :] = pltpu.roll(odd, 1, 1)[:, 0:nb].astype(BF)
+        u_ref[at + 32 : at + 64, :] = even[:, 0:nb].astype(BF)
+        u_ref[at + 64 : at + 96, :] = odd[:, 0:nb].astype(BF)
+        u_ref[at + 96 : at + 128, :] = pltpu.roll(even, wide - 1, 1)[:, 0:nb].astype(BF)
+
+
+def column_keeps(nb, wide):
+    mem_at, mem_last = lax.axis_index("mem"), lax.axis_size("mem") - 1
+    lane = lax.broadcasted_iota(jnp.int32, (32, wide), 1)
+    keep_odd = jnp.where((lane == wide - 1) & (mem_at == 0), 0.0, 1.0).astype(F32)
+    keep_even = jnp.where((lane == nb) & (mem_at == mem_last), 0.0, 1.0).astype(F32)
+    return keep_even, keep_odd
+
+
+def field_rows(w2, u_ref, g_ref, which):
+    nb = u_ref.shape[1]
+    for n, a in enumerate(which):
+        v = dot(w2, u_ref[a * 128 : (a + 3) * 128, :]).astype(BF)
+        for pr in range(2):
+            for ph in range(4):
+                g_ref[(2 * n + pr) * 16 : (2 * n + pr + 1) * 16, ph * nb : (ph + 1) * nb] = v[
+                    (pr * 4 + ph) * 16 : (pr * 4 + ph + 1) * 16
+                ]
+
+
+def level_first(rows, which):
+    count = 32 * len(which)
+    to = lax.broadcasted_iota(jnp.int32, (16 * rows, count), 0)
+    frm = lax.broadcasted_iota(jnp.int32, (16 * rows, count), 1)
+    level, row = to // rows, lax.rem(to, rows)
+    hit = jnp.zeros(to.shape, jnp.bool_)
+    for n, a in enumerate(which):
+        for pr in range(2):
+            hit = hit | ((row == 2 * a + pr) & (frm == (2 * n + pr) * 16 + level))
+    return jnp.where(hit, 1.0, 0.0).astype(BF)
+
+
+def split_rows(rows):
+    inside = [a for a in range(2, 2 * rows - 2)]
+    return inside, [a for a in range(2 * rows) if a not in inside]
+
+
+def decoder_inner(nb, ext_ref, d1_ref, d2_ref, wd1, wd2, u_ref, join_ref, turn_ref, part_ref, l_ref, g_ref):
     wd1[...] = jnp.zeros_like(wd1)
     wd2[...] = jnp.zeros_like(wd2)
     for pr, rr, tr in TRANSPOSED:
@@ -349,10 +414,30 @@
                 at = pr * 4 + 2 * q + pc
                 to = rr * 4 + q + cc
                 wd2[at * 16 : (at + 1) * 16, to * 32 : (to + 1) * 32] = d2_ref[tr * 4 + tc]
-
-
-def decoder_kernel(nb, ext_ref, first_ref, second_ref, w1_ref, w2_ref, p_ref, r_ref, out_ref, l_ref, u_ref, g_ref):
-    mem_at, mem_last = lax.axis_index("mem"), lax.axis_size("mem") - 1
+    rows, _, wide = ext_ref.shape
+    frm = lax.broadcasted_iota(jnp.int32, join_ref.shape, 0)
+    to = lax.broadcasted_iota(jnp.int32, join_ref.shape, 1)
+    place = frm // nb
+    join_ref[...] = jnp.where(to == 4 * (frm - nb * place) + place, 1.0, 0.0).astype(BF)
+    inside, outside = split_rows(rows)
+    turn_ref[...] = level_first(4 * rows, outside)
+    l_ref[0] = jnp.zeros_like(l_ref[0])
+    l_ref[1] = jnp.zeros_like(l_ref[0])
+    l_ref[2 : rows + 2] = ext_ref[...]
+    l_ref[rows + 2] = jnp.zeros_like(l_ref[0])
+    u_ref[...] = jnp.zeros_like(u_ref)
+    keep_even, keep_odd = column_keeps(nb, wide)
+    for a in range(rows):
+        upsample_row(wd1[...], l_ref, a, keep_even, keep_odd, rows, u_ref, range(1, 2 * rows - 1), {})
+    field_rows(wd2[...], u_ref, g_ref, inside)
+    g = dot(level_first(4 * rows, inside), g_ref[...]).astype(BF)
+    part_ref[...] = dot(g, join_ref[...])
+
+
+def decoder_kernel(
+    nb, ext_ref, first_ref, second_ref, w1_ref, w2_ref, u_in, join_ref, turn_ref, part_ref,
+    out_ref, l_ref, u_ref, g_ref,
+):
     odd_row = lax.rem(lax.axis_index("row"), 2) == 1
     keep_first, keep_last = is_row(0), is_row(lax.axis_size("row") - 1)
     rows, _, wide = ext_ref.shape
@@ -362,36 +447,16 @@
     put_latent(l_ref, 1, jnp.where(odd_row, first, second) * keep_first)
     l_ref[2 : rows + 2] = ext_ref[...]
     put_latent(l_ref, rows + 2, jnp.where(odd_row, second, first) * keep_last)
-    w1, w2 = w1_ref[...], w2_ref[...]
-    lane = lax.broadcasted_iota(jnp.int32, (32, wide), 1)
-    keep_odd = jnp.where((lane == wide - 1) & (mem_at == 0), 0.0, 1.0).astype(F32)
-    keep_even = jnp.where((lane == nb) & (mem_at == mem_last), 0.0, 1.0).astype(F32)
-    for a in range(-1, rows + 1):
-        v = silu_of_half(dot(w1, l_ref[a + 1 : a + 4].reshape(288, wide)))
-        for pr in range(2):
-            row = 2 * a + pr
-            if not -1 <= row <= 2 * rows:
-                continue
-            even = v[pr * 64 : pr * 64 + 32] * keep_even
-            odd = v[pr * 64 + 32 : pr * 64 + 64] * keep_odd
-            if row == -1:
-                even, odd = even * keep_first, odd * keep_first
-            if row == 2 * rows:
-                even, odd = even * keep_last, odd * keep_last
-            at = (row + 1) * 128
-            u_ref[at : at + 32, :] = pltpu.roll(odd, 1, 1)[:, 0:nb].astype(BF)
-            u_ref[at + 32 : at + 64, :] = even[:, 0:nb].astype(BF)
-            u_ref[at + 64 : at + 96, :] = odd[:, 0:nb].astype(BF)
-            u_ref[at + 96 : at + 128, :] = pltpu.roll(even, wide - 1, 1)[:, 0:nb].astype(BF)
-    for a in range(2 * rows):
-        v = dot(w2, u_ref[a * 128 : (a + 3) * 128, :]).astype(BF)
-        for pr in range(2):
-            for ph in range(4):
-                g_ref[(2 * a + pr) * 16 : (2 * a + pr + 1) * 16, ph * nb : (ph + 1) * nb] = v[
-                    (pr * 4 + ph) * 16 : (pr * 4 + ph + 1) * 16
-                ]
-    g = dot(r_ref[...], g_ref[...]).astype(BF)
-    out_ref[...] = dot(g, p_ref[...]).astype(BF).reshape(out_ref.shape)
+    u_ref[...] = u_in[...]
+    keep_even, keep_odd = column_keeps(nb, wide)
+    keeps = {-1: keep_first, 2 * rows: keep_last}
+    for a in (-1, 0, rows - 1, rows):
+        upsample_row(
+            w1_ref[...], l_ref, a, keep_even, keep_odd, rows, u_ref, (-1, 0, 2 * rows - 1, 2 * rows), keeps
+        )
+    field_rows(w2_ref[...], u_ref, g_ref, split_rows(rows)[1])
+    g = dot(g_ref[...], join_ref[...]).astype(BF)
+    out_ref[...] = (dot(turn_ref[...], g) + part_ref[...]).astype(BF).reshape(out_ref.shape)
 
 
 def shifted(value, by):
@@ -406,7 +471,7 @@
 VMEM = pl.BlockSpec(memory_space=pltpu.VMEM)
 
 
-def call(kernel, outs, scratch, *operands, mb=8):
+def call(kernel, outs, scratch, *operands, mb=8, us=1):
     return pl.pallas_call(
         kernel,
         out_shape=[jax.ShapeDtypeStruct(*o) for o in outs],
@@ -414,6 +479,7 @@
         out_specs=[VMEM] * len(outs),
         scratch_shapes=[pltpu.VMEM(*s) for s in scratch],
         compiler_params=pltpu.CompilerParams(vmem_limit_bytes=mb * 2**20),
+        cost_estimate=pl.CostEstimate(flops=us * 10**9, bytes_accessed=us * 3 * 10**6, transcendentals=0),
     )(*operands)
 
 
@@ -431,7 +497,7 @@
     total = padded(5 * per[0], 16), padded(5 * per[1], 16)
     pack = functools.partial(pack_kernel, count, channels, rows)
     sizes = [(nd * chunks, lanes), (nu * chunks, lanes)]
-    down, up = call(pack, [(s, BF) for s in sizes], [(s, F32) for s in sizes], x, mb=16)
+    down, up = call(pack, [(s, BF) for s in sizes], [(s, F32) for s in sizes], x, mb=16, us=20)
     up = shifted(up, -1)
     down = shifted(down, 1)
 
@@ -441,14 +507,14 @@
     row_f32 = ((count, 128, cols), F32)
     third_f32 = ((count, 32, cols), F32)
     (
-        h_first, h_last, a_first, a_second, a_last, v_second, v_last, mid,
+        h1, h_first, h_last, a_last, v_second, v_third,
         w2_big, w3_big, w1_down, w1_up, spreads, mix,
     ) = call(
         functools.partial(inner_kernel, count, channels, rows, per),
-        [row_f32] * 5
+        [((count, 256 * (half - 1), cols), BF)]
+        + [row_f32] * 3
         + [third_f32] * 2
         + [
-            ((quarter - 3, 32, cols), F32),
             ((128, 768), BF),
             ((64, 256), BF),
             ((count, 256, total[0]), BF),
@@ -461,23 +527,28 @@
             ((640, 5 * channels * 8), BF),
             ((count, rows // 8, 5 * channels * 8, cols), F32),
             ((rows // 8, 640, cols), F32),
-            ((256 * (half - 1), cols), BF),
             ((256, cols), BF),
         ],
-        x, w1, w2, w3, mix_weight, mb=28,
-    )
-    low, carry = call(
+        x, w1, w2, w3, mix_weight, mb=24,
+    )
+    h2_low, carry = call(
         functools.partial(low_kernel, count, channels, per[1]),
-        [((32, cols), F32), ((count * CH_BOT, cols), BF)],
+        [((count, 128, cols), BF), ((count * CH_BOT, cols), BF)],
         [((total[1], cols), F32), ((count * 256, cols), BF)],
-        up, spreads, w1_up, h_last, w2_big, a_last, w3_big, v_last, mix, mb=16,
+        up, spreads, w1_up, h_last, w2_big, a_last, w3_big, mb=12,
     )
     carry = shifted(carry, 1)
+    a_first, a_second, mid = call(
+        functools.partial(middle_kernel, count, half),
+        [row_f32, row_f32, ((quarter - 2, 32, cols), F32)],
+        [((256, cols), BF)],
+        h1, h2_low, w2_big, w3_big, v_third, mix, mb=12,
+    )
     pre, tail = call(
         functools.partial(top_kernel, count, channels, per[0]),
         [((count, CH_BOT, cols), F32), ((quarter * 32 - 32, cols + 256), F32)],
         [((total[0], cols), F32), ((count * 512, cols), BF), ((256, cols), BF)],
-        down, spreads, w1_down, h_first, w2_big, a_first, a_second, w3_big, v_second, mix, mid, low, mb=16,
+        down, spreads, w1_down, h_first, w2_big, a_first, a_second, w3_big, v_second, mix, mid, mb=12,
     )
     slots = peers // 2
     chunk = (quarter * 32 + 16, 128)
@@ -504,16 +575,25 @@
     d1, d2, _ = lax.optimization_barrier((dec_first, dec_second, others[0]))
     d1 = d1.transpose(2, 3, 0, 1).reshape(16, 32, 32)
     d2 = d2.transpose(2, 3, 0, 1).reshape(16, 16, 32)
-    wd1, wd2 = call(weight_kernel, [((128, 288), BF), ((128, 384), BF)], [], d1, d2)
-    reorder = np.zeros((16 * rows, 16 * rows), np.float32)
-    for r in range(rows):
-        for level in range(16):
-            reorder[level * rows + r, r * 16 + level] = 1
+    inside, outside = split_rows(quarter)
+    wd1, wd2, u, join, turn, part = call(
+        functools.partial(decoder_inner, nb),
+        [
+            ((128, 288), BF),
+            ((128, 384), BF),
+            ((128 * (half + 2), nb), BF),
+            ((4 * nb, 4 * nb), BF),
+            ((16 * rows, 32 * len(outside)), BF),
+            ((16 * rows, 4 * nb), F32),
+        ],
+        [((quarter + 3, 96, ext), BF), ((32 * len(inside), 4 * nb), BF)],
+        latent, d1, d2,
+    )
     (out,) = call(
         functools.partial(decoder_kernel, nb),
         [((16, rows, 4 * nb), BF)],
-        [((quarter + 4, 96, ext), BF), ((128 * (half + 2), nb), BF), ((16 * rows, 4 * nb), BF)],
-        latent, first, second, wd1, wd2, jnp.asarray(spread(4, nb).T, BF), jnp.asarray(reorder, BF),
+        [((quarter + 4, 96, ext), BF), ((128 * (half + 2), nb), BF), ((32 * len(outside), 4 * nb), BF)],
+        latent, first, second, wd1, wd2, u, join, turn, part,
     )
     return out
 

time: 40.2 us -> 37 us (0.920)
  local copies, waits for them, and re-layouts: 4.5 us -> 1.41 us
  waiting for transfers between devices: 8.76 us -> 6.69 us
  Pallas kernels: 13.2 us -> 14.7 us
  starting transfers between devices: 13.3 us -> 13.9 us
    unnamed x20 -> x16, local copies, waits for them, and re-layouts: 4.45 us -> 1.36 us
    pallas_call x9 -> x10, Pallas kernels: 13.2 us -> 14.7 us  [call(): pl.pallas_call(kernel, out_shape=[jax.ShapeDtypeStruct(*o) for o in outs]...]
    ppermute x3, waiting for transfers between devices: 1.59 us -> 0.21 us  [shifted(): lax.ppermute(value, 'row', [(i, (i + by) % peers) for i in range(peers)])]
    ppermute x3, starting transfers between devices: 5.55 us -> 6.61 us  [shifted(): lax.ppermute(value, 'row', [(i, (i + by) % peers) for i in range(peers)])]
    ppermute x1, waiting for transfers between devices: 0.51 us -> 0.01 us  [per_device(): first = lax.ppermute(first, 'row', [(i, i ^ 1) for i in range(lines)])]
    ppermute x1, starting transfers between devices: 0.25 us -> 0.66 us  [per_device(): first = lax.ppermute(first, 'row', [(i, i ^ 1) for i in range(lines)])]
    ppermute x4, starting transfers between devices: 4.69 us -> 4.29 us  [swapped(): lax.ppermute(value, 'mem', [(i, i ^ by) for i in range(lax.axis_size('mem...]
    ppermute x1, starting transfers between devices: 2.79 us -> 2.38 us  [per_device(): lax.ppermute(second, 'row', [(i, (i + 1 if i % 2 else i - 1) % lines) for...]
  transfers between devices with their start and end apart: 9 -> 9, of which waited for: 6 -> 5; matrix products, arithmetic and copies ran while one was open for 0% -> 0% of each run, Pallas kernels for 26% -> 33%
where the time goes in v3:
time: 37 us; the launch traced here: 36.8 us
  Pallas kernels  14.7 us (40%)
  starting transfers between devices  13.9 us (38%)
  waiting for transfers between devices  6.69 us (18%)
  local copies, waits for them, and re-layouts  1.41 us (4%)
    pallas_call x10, Pallas kernels, call(): pl.pallas_call(kernel, out_shape=[jax.ShapeDtypeStruct(*o) for o in outs]...  14.7 us
    ppermute x3, starting transfers between devices, shifted(): lax.ppermute(value, 'row', [(i, (i + by) % peers) for i in range(peers)])  6.61 us
    ppermute x4, waiting for transfers between devices, swapped(): lax.ppermute(value, 'mem', [(i, i ^ by) for i in range(lax.axis_size('mem...  5.45 us
    ppermute x4, starting transfers between devices, swapped(): lax.ppermute(value, 'mem', [(i, i ^ by) for i in range(lax.axis_size('mem...  4.29 us
    ppermute x1, starting transfers between devices, per_device(): lax.ppermute(second, 'row', [(i, (i + 1 if i % 2 else i - 1) % lines) for...  2.38 us
    unnamed x16, local copies, waits for them, and re-layouts  1.36 us
    ppermute x1, waiting for transfers between devices, per_device(): lax.ppermute(second, 'row', [(i, (i + 1 if i % 2 else i - 1) % lines) for...  1.02 us
  transfers between devices with their start and end apart: 9, of which 5 were waited for; matrix products, arithmetic and copies ran while one was open for 0% of the time, Pallas kernels for 33%

profile of v3, /device:TPU:0, one launch (start us, length us, event | category | flops | bytes accessed | tf_op | source)
XLA Modules:
  0.0 36.8 jit_solution(7457778747840879382)
XLA Ops:
  0.0 0.0 copy-start
  0.0 1.3 %copy-done = bf16[2,5,16,4096]{3,2,1,0:T(8,128)(2,1)S(1)} copy-done((bf16[2,5,16,4096]{3,2,1,0:T(8,128)(2,1)S(1)}, bf16[2,5,16,4096]{3,2,1,0:T(8,128)(2,1)}, u32[]{:S(2)}) %copy-start) | copy-done | bytes 1310744
  1.3 0.0 copy-start.1
  1.3 0.0 copy-start.2
  1.3 0.0 copy-start.3
  1.3 0.0 copy-start.4
  1.3 0.0 copy-start.5
  1.3 0.2 shard_map.73
  1.6 3.9 %collective-permute-start.1 = (bf16[160,512]{1,0:T(8,128)(2,1)S(1)}, bf16[160,512]{1,0:T(8,128)(2,1)S(1)}, u32[]{:S(2)}, u32[]{:S(2)}) collective-permute-start(bf16[160,512]{1,0:T(8,128)(2,1)S(1)} %get-tuple-element.49), channel_id=1, source_target_pairs={{0,3},{1,0},{2,1},{3,2},{4,7},{5,4},{6,5},{7,6},{8,11},{9,8},{10,9... | collective-permute-start | bytes 491528 | tf_op jit(solution)/shard_map/ppermute | solution.py:464
  5.5 0.0 collective-permute-start
  5.5 0.0 copy-done.1
  5.5 0.0 copy-done.2
  5.5 0.0 copy-done.3
  5.6 0.0 copy-done.4
  5.6 0.0 copy-done.5
  5.6 4.4 %shard_map.74 = (bf16[2,1792,1024]{2,1,0:T(8,128)(2,1)S(1)}, f32[2,128,1024]{2,1,0:T(8,128)S(1)}, f32[2,128,1024]{2,1,0:T(8,128)S(1)}, f32[2,128,1024]{2,1,0:T(8...) custom-call(bf16[160,4096]{1,0:T(8,128)(2,1)S(1)} %bitcast.15, ...), custom_call_target="tpu_custom_call" | custom-call | flops 1000000000 | bytes 3000000 | tf_op jit(solution)/shard_map/pallas_call | solution.py:475
  9.9 0.2 collective-permute-done.1.got_ref
  10.1 1.6 %shard_map.75 = (bf16[2,128,1024]{2,1,0:T(8,128)(2,1)S(1)}, bf16[32,1024]{1,0:T(8,128)(2,1)S(1)}) custom-call(bf16[160,512]{1,0:T(8,128)(2,1)S(1)} %collective-permute-done.1.got_ref, bf16[2,256,256]{2,1,0:T(8,128)(2,1)S(1)} %get-tuple-element.44.spread_ref, bf16[2,128,128]{2,1,0:T(8,128)(2,1)S(1)} %get-tuple-element.50.w1_ref, ...), custom_call_target="tpu_custom_call" | custom-call | flops 1000000000 | bytes 3000000 | tf_op jit(solution)/shard_map/pallas_call | solution.py:475
  11.7 2.7 %collective-permute-start.2 = (bf16[32,1024]{1,0:T(8,128)(2,1)S(1)}, bf16[32,1024]{1,0:T(8,128)(2,1)S(1)}, u32[]{:S(2)}, u32[]{:S(2)}) collective-permute-start(bf16[32,1024]{1,0:T(8,128)(2,1)S(1)} %get-tuple-element.62), channel_id=1, source_target_pairs={{0,1},{1,2},{2,3},{3,0},{4,5},{5,6},{6,7},{7,4},{8,9},{9,10},{10,1... | collective-permute-start | bytes 196616 | tf_op jit(solution)/shard_map/ppermute | solution.py:464
  14.4 2.8 %shard_map.76 = (f32[2,128,1024]{2,1,0:T(8,128)S(1)}, f32[2,128,1024]{2,1,0:T(8,128)S(1)}, f32[2,32,1024]{2,1,0:T(8,128)S(1)}) custom-call(bf16[2,1792,1024]{2,1,0:T(8,128)(2,1)S(1)} %get-tuple-element.48.h1_ref, bf16[2,128,1024]{2,1,0:T(8,128)(2,1)S(1)} %get-tuple-element.54.h2_low, bf16[128,768]{1,0:T(8,128)(2,1)S(1)} %get-tuple-element.47.w2_ref, ...), custom_call_target="tpu_custom_call" | custom-call | flops 1000000000 | bytes 3000000 | tf_op jit(solution)/shard_map/pallas_call | solution.py:475
  17.2 0.0 copy-start.7
  17.2 0.0 copy-start.6
  17.2 0.0 collective-permute-done.got_ref
  17.2 2.1 %shard_map.77 = (f32[2,16,1024]{2,1,0:T(8,128)S(1)}, f32[96,1280]{1,0:T(8,128)S(1)}) custom-call(bf16[240,512]{1,0:T(8,128)(2,1)S(1)} %collective-permute-done.got_ref, bf16[2,256,256]{2,1,0:T(8,128)(2,1)S(1)} %get-tuple-element.44.spread_ref, bf16[2,256,160]{2,1,0:T(8,128)(2,1)S(1)} %get-tuple-element.45.w1_ref, ...), custom_call_target="tpu_custom_call" | custom-call | flops 1000000000 | bytes 3000000 | tf_op jit(solution)/shard_map/pallas_call | solution.py:475
  19.3 0.0 collective-permute-done.2.carry_ref
  19.3 0.4 shard_map.78
  19.7 0.0 collective-permute-start.3
  19.8 1.4 %collective-permute-done.3.got_ref = bf16[4,144,128]{2,1,0:T(8,128)(2,1)S(1)} collective-permute-done((bf16[4,144,128]{2,1,0:T(8,128)(2,1)S(1)}, bf16[4,144,128]{2,1,0:T(8,128)(2,1)S(1)}, u32[]{:S(2)}, u32[]{:S(2)}) %collective-permute-start.3) | collective-permute-done | bytes 147488 | tf_op jit(solution)/shard_map/ppermute | solution.py:468
  21.2 2.6 %collective-permute-start.5 = (bf16[144,128]{1,0:T(8,128)(2,1)S(1)}, bf16[144,128]{1,0:T(8,128)(2,1)S(1)}, u32[]{:S(2)}, u32[]{:S(2)}) collective-permute-start(bf16[144,128]{1,0:T(8,128)(2,1)S(1)} %get-tuple-element.68), channel_id=1, source_target_pairs={{0,16},{4,20},{8,24},{12,28},{16,0},{20,4},{24,8},{28,12},{1,17},{... | collective-permute-start | bytes 110600 | tf_op jit(solution)/shard_map/ppermute | solution.py:468
  23.8 1.4 %collective-permute-start.6 = (bf16[144,128]{1,0:T(8,128)(2,1)S(1)}, bf16[144,128]{1,0:T(8,128)(2,1)S(1)}, u32[]{:S(2)}, u32[]{:S(2)}) collective-permute-start(bf16[144,128]{1,0:T(8,128)(2,1)S(1)} %get-tuple-element.69), channel_id=1, source_target_pairs={{0,24},{4,28},{8,16},{12,20},{16,8},{20,12},{24,0},{28,4},{1,25},{... | collective-permute-start | bytes 110600 | tf_op jit(solution)/shard_map/ppermute | solution.py:468
  25.2 0.2 collective-permute-start.4
  25.4 0.0 copy-done.7
  25.4 0.0 copy-done.6
  25.5 1.0 %collective-permute-done.5.refs_1_ = bf16[144,128]{1,0:T(8,128)(2,1)S(1)} collective-permute-done((bf16[144,128]{1,0:T(8,128)(2,1)S(1)}, bf16[144,128]{1,0:T(8,128)(2,1)S(1)}, u32[]{:S(2)}, u32[]{:S(2)}) %collective-permute-start.5) | collective-permute-done | bytes 36896 | tf_op jit(solution)/shard_map/ppermute | solution.py:468
  26.5 3.1 %collective-permute-done.6.refs_2_ = bf16[144,128]{1,0:T(8,128)(2,1)S(1)} collective-permute-done((bf16[144,128]{1,0:T(8,128)(2,1)S(1)}, bf16[144,128]{1,0:T(8,128)(2,1)S(1)}, u32[]{:S(2)}, u32[]{:S(2)}) %collective-permute-start.6) | collective-permute-done | bytes 36896 | tf_op jit(solution)/shard_map/ppermute | solution.py:468
  29.6 0.0 collective-permute-done.4.refs_0_
  29.6 0.3 shard_map.80
  29.8 0.7 %collective-permute-start.7 = (bf16[32,256]{1,0:T(8,128)(2,1)S(1)}, bf16[32,256]{1,0:T(8,128)(2,1)S(1)}, u32[]{:S(2)}, u32[]{:S(2)}) collective-permute-start(bf16[32,256]{1,0:T(8,128)(2,1)S(1)} %get-tuple-element.71), channel_id=1, source_target_pairs={{0,1},{1,0},{2,3},{3,2},{4,5},{5,4},{6,7},{7,6},{8,9},{9,8},{10,11... | collective-permute-start | bytes 49160 | tf_op jit(solution)/shard_map/ppermute | solution.py:572
  30.5 2.4 %collective-permute-start.8 = (bf16[32,256]{1,0:T(8,128)(2,1)S(1)}, bf16[32,256]{1,0:T(8,128)(2,1)S(1)}, u32[]{:S(2)}, u32[]{:S(2)}) collective-permute-start(bf16[32,256]{1,0:T(8,128)(2,1)S(1)} %get-tuple-element.72), channel_id=1, source_target_pairs={{0,3},{1,2},{2,1},{3,0},{4,7},{5,6},{6,5},{7,4},{8,11},{9,10},{10,... | collective-permute-start | bytes 49160 | tf_op jit(solution)/shard_map/ppermute | solution.py:573
  32.9 1.2 %shard_map.81 = (bf16[128,288]{1,0:T(8,128)(2,1)S(1)}, bf16[128,384]{1,0:T(8,128)(2,1)S(1)}, bf16[1280,128]{1,0:T(8,128)(2,1)S(1)}, bf16[512,512]{1,0:T(8,128)(2...) custom-call(bf16[4,96,256]{2,1,0:T(8,128)(2,1)S(1)} %get-tuple-element.70.ext_ref, ...), custom_call_target="tpu_custom_call" | custom-call | flops 1000000000 | bytes 3000000 | tf_op jit(solution)/shard_map/pallas_call | solution.py:475
  34.1 0.0 collective-permute-done.7.first_ref
  34.1 1.0 %collective-permute-done.8.second_ref = bf16[32,256]{1,0:T(8,128)(2,1)S(1)} collective-permute-done((bf16[32,256]{1,0:T(8,128)(2,1)S(1)}, bf16[32,256]{1,0:T(8,128)(2,1)S(1)}, u32[]{:S(2)}, u32[]{:S(2)}) %collective-permute-start.8) | collective-permute-done | bytes 16416 | tf_op jit(solution)/shard_map/ppermute | solution.py:573
  35.1 1.7 %shard_map.82 = bf16[16,16,512]{2,1,0:T(8,128)(2,1)} custom-call(bf16[4,96,256]{2,1,0:T(8,128)(2,1)S(1)} %get-tuple-element.70.ext_ref, bf16[32,256]{1,0:T(8,128)(2,1)S(1)} %collective-permute-done.7.first_ref, bf16[32,256]{1,0:T(8,128)(2,1)S(1)} %collective-permute-done.8.second_ref, bf16[128,288]{1,0:T(8,128)(2,1)S(1)} %get-tuple-element.75.w1_ref, ...), custom_call_target="tpu_custom_call" | custom-call | flops 1000000000 | bytes 3000000 | tf_op jit(solution)/shard_map/pallas_call | solution.py:475
  (3 shorter events, 0.1 us)
Async XLA Ops:
  0.0 1.3 %copy-start = (bf16[2,5,16,4096]{3,2,1,0:T(8,128)(2,1)S(1)}, bf16[2,5,16,4096]{3,2,1,0:T(8,128)(2,1)}, u32[]{:S(2)}) copy-start(bf16[2,5,16,4096]{3,2,1,0:T(8,128)(2,1)} %param.7) | copy-start | bytes 3932164
  1.3 4.2 %copy-start.1 = (bf16[2,5,16,4096]{3,2,1,0:T(8,128)(2,1)S(1)}, bf16[2,5,16,4096]{3,2,1,0:T(8,128)(2,1)}, u32[]{:S(2)}) copy-start(bf16[2,5,16,4096]{3,2,1,0:T(8,128)(2,1)} %param.7) | copy-start | bytes 3932164
  1.3 4.2 %copy-start.2 = (bf16[64,64,3,3]{1,0,3,2:T(8,128)(2,1)S(1)}, bf16[64,64,3,3]{1,0,3,2:T(8,128)(2,1)}, u32[]{:S(2)}) copy-start(bf16[64,64,3,3]{1,0,3,2:T(8,128)(2,1)} %param.9) | copy-start | bytes 221188
  1.3 4.2 %copy-start.3 = (bf16[16,64,3,3]{1,0,3,2:T(8,128)(2,1)S(1)}, bf16[16,64,3,3]{1,0,3,2:T(8,128)(2,1)}, u32[]{:S(2)}) copy-start(bf16[16,64,3,3]{1,0,3,2:T(8,128)(2,1)} %param.10) | copy-start | bytes 55300
  1.3 4.2 %copy-start.4 = (bf16[32,256]{1,0:T(8,128)(2,1)S(1)}, bf16[32,256]{1,0:T(8,128)(2,1)}, u32[]{:S(2)}) copy-start(bf16[32,256]{1,0:T(8,128)(2,1)} %mix_ref.1) | copy-start | bytes 49156
  1.3 4.2 %copy-start.5 = (bf16[64,5,3,3]{0,3,2,1:T(4,128)(2,1)S(1)}, bf16[64,5,3,3]{0,3,2,1:T(4,128)(2,1)}, u32[]{:S(2)}) copy-start(bf16[64,5,3,3]{0,3,2,1:T(4,128)(2,1)} %param.8) | copy-start | bytes 17284
  1.6 8.6 %collective-permute-start.1 = (bf16[160,512]{1,0:T(8,128)(2,1)S(1)}, bf16[160,512]{1,0:T(8,128)(2,1)S(1)}, u32[]{:S(2)}, u32[]{:S(2)}) collective-permute-start(bf16[160,512]{1,0:T(8,128)(2,1)S(1)} %get-tuple-element.49), channel_id=1, source_target_pairs={{0,3},{1,0},{2,1},{3,2},{4,7},{5,4},{6,5},{7,6},{8,11},{9,8},{10,9... | collective-permute-start | bytes 491528 | tf_op jit(solution)/shard_map/ppermute | solution.py:464
  5.5 11.7 %collective-permute-start = (bf16[240,512]{1,0:T(8,128)(2,1)S(1)}, bf16[240,512]{1,0:T(8,128)(2,1)S(1)}, u32[]{:S(2)}, u32[]{:S(2)}) collective-permute-start(bf16[240,512]{1,0:T(8,128)(2,1)S(1)} %get-tuple-element.43), channel_id=1, source_target_pairs={{0,1},{1,2},{2,3},{3,0},{4,5},{5,6},{6,7},{7,4},{8,9},{9,10},{10,1... | collective-permute-start | bytes 737288 | tf_op jit(solution)/shard_map/ppermute | solution.py:464
  11.7 7.6 %collective-permute-start.2 = (bf16[32,1024]{1,0:T(8,128)(2,1)S(1)}, bf16[32,1024]{1,0:T(8,128)(2,1)S(1)}, u32[]{:S(2)}, u32[]{:S(2)}) collective-permute-start(bf16[32,1024]{1,0:T(8,128)(2,1)S(1)} %get-tuple-element.62), channel_id=1, source_target_pairs={{0,1},{1,2},{2,3},{3,0},{4,5},{5,6},{6,7},{7,4},{8,9},{9,10},{10,1... | collective-permute-start | bytes 196616 | tf_op jit(solution)/shard_map/ppermute | solution.py:464
  17.2 8.2 %copy-start.7 = (bf16[16,32,4,4]{1,3,2,0:T(4,128)(2,1)S(1)}, bf16[16,32,4,4]{1,3,2,0:T(4,128)(2,1)}, u32[]{:S(2)}) copy-start(bf16[16,32,4,4]{1,3,2,0:T(4,128)(2,1)} %param.13) | copy-start | bytes 49156
  17.2 8.2 %copy-start.6 = (bf16[32,32,4,4]{1,3,2,0:T(4,128)(2,1)S(1)}, bf16[32,32,4,4]{1,3,2,0:T(4,128)(2,1)}, u32[]{:S(2)}) copy-start(bf16[32,32,4,4]{1,3,2,0:T(4,128)(2,1)} %param.12) | copy-start | bytes 98308
  19.7 1.4 %collective-permute-start.3 = (bf16[4,144,128]{2,1,0:T(8,128)(2,1)S(1)}, bf16[4,144,128]{2,1,0:T(8,128)(2,1)S(1)}, u32[]{:S(2)}, u32[]{:S(2)}) collective-permute-start(bf16[4,144,128]{2,1,0:T(8,128)(2,1)S(1)} %get-tuple-element.65), channel_id=1, source_target_pairs={{0,4},{4,0},{8,12},{12,8},{16,20},{20,16},{24,28},{28,24},{1,5},{5... | collective-permute-start | bytes 442376 | tf_op jit(solution)/shard_map/ppermute | solution.py:468
  21.2 5.3 %collective-permute-start.5 = (bf16[144,128]{1,0:T(8,128)(2,1)S(1)}, bf16[144,128]{1,0:T(8,128)(2,1)S(1)}, u32[]{:S(2)}, u32[]{:S(2)}) collective-permute-start(bf16[144,128]{1,0:T(8,128)(2,1)S(1)} %get-tuple-element.68), channel_id=1, source_target_pairs={{0,16},{4,20},{8,24},{12,28},{16,0},{20,4},{24,8},{28,12},{1,17},{... | collective-permute-start | bytes 110600 | tf_op jit(solution)/shard_map/ppermute | solution.py:468
  23.8 5.8 %collective-permute-start.6 = (bf16[144,128]{1,0:T(8,128)(2,1)S(1)}, bf16[144,128]{1,0:T(8,128)(2,1)S(1)}, u32[]{:S(2)}, u32[]{:S(2)}) collective-permute-start(bf16[144,128]{1,0:T(8,128)(2,1)S(1)} %get-tuple-element.69), channel_id=1, source_target_pairs={{0,24},{4,28},{8,16},{12,20},{16,8},{20,12},{24,0},{28,4},{1,25},{... | collective-permute-start | bytes 110600 | tf_op jit(solution)/shard_map/ppermute | solution.py:468
  25.2 4.4 %collective-permute-start.4 = (bf16[144,128]{1,0:T(8,128)(2,1)S(1)}, bf16[144,128]{1,0:T(8,128)(2,1)S(1)}, u32[]{:S(2)}, u32[]{:S(2)}) collective-permute-start(bf16[144,128]{1,0:T(8,128)(2,1)S(1)} %get-tuple-element.67), channel_id=1, source_target_pairs={{0,8},{4,12},{8,0},{12,4},{16,24},{20,28},{24,16},{28,20},{1,9},{5... | collective-permute-start | bytes 110600 | tf_op jit(solution)/shard_map/ppermute | solution.py:468
  29.8 4.3 %collective-permute-start.7 = (bf16[32,256]{1,0:T(8,128)(2,1)S(1)}, bf16[32,256]{1,0:T(8,128)(2,1)S(1)}, u32[]{:S(2)}, u32[]{:S(2)}) collective-permute-start(bf16[32,256]{1,0:T(8,128)(2,1)S(1)} %get-tuple-element.71), channel_id=1, source_target_pairs={{0,1},{1,0},{2,3},{3,2},{4,5},{5,4},{6,7},{7,6},{8,9},{9,8},{10,11... | collective-permute-start | bytes 49160 | tf_op jit(solution)/shard_map/ppermute | solution.py:572
  30.5 4.6 %collective-permute-start.8 = (bf16[32,256]{1,0:T(8,128)(2,1)S(1)}, bf16[32,256]{1,0:T(8,128)(2,1)S(1)}, u32[]{:S(2)}, u32[]{:S(2)}) collective-permute-start(bf16[32,256]{1,0:T(8,128)(2,1)S(1)} %get-tuple-element.72), channel_id=1, source_target_pairs={{0,3},{1,2},{2,1},{3,0},{4,7},{5,6},{6,5},{7,4},{8,11},{9,10},{10,... | collective-permute-start | bytes 49160 | tf_op jit(solution)/shard_map/ppermute | solution.py:573

commit v4 on v3

--- a/solution.py
+++ b/solution.py
@@ -52,13 +52,17 @@
     return jnp.where(lax.axis_index("row") == at, 0.0, 1.0).astype(F32)
 
 
-def put_hidden(ref, at, value):
+def put_hidden(ref, at, lanes, value):
     v = value.astype(BF)
     even, odd = v[0:64], v[64:128]
-    ref[at * 256 + 64 : at * 256 + 128, :] = even
-    ref[at * 256 + 128 : at * 256 + 192, :] = odd
-    ref[at * 256 : at * 256 + 64, :] = shift_right(odd)
-    ref[at * 256 + 192 : at * 256 + 256, :] = shift_left(even)
+    ref[at * 256 + 64 : at * 256 + 128, lanes] = even
+    ref[at * 256 + 128 : at * 256 + 192, lanes] = odd
+    ref[at * 256 : at * 256 + 64, lanes] = shift_right(odd)
+    ref[at * 256 + 192 : at * 256 + 256, lanes] = shift_left(even)
+
+
+def bottleneck(w):
+    return silu_of_half(w[0:16] + shift_right(w[16:32])).astype(BF)
 
 
 def apart(block, even_ref, odd_ref):
@@ -74,21 +78,65 @@
 
 
 def place_halo(source, spread_ref, y_ref, count, per):
-    y_ref[...] = jnp.zeros_like(y_ref)
+    cols = y_ref.shape[1]
+    if count % 8:
+        for q in range(5):
+            y_ref[q * per + count // 8 * 8 : (q + 1) * per, :] = jnp.zeros((8, cols), F32)
+    if 5 * per < y_ref.shape[0]:
+        y_ref[5 * per :, :] = jnp.zeros((y_ref.shape[0] - 5 * per, cols), F32)
     for q, z in enumerate(apart(source, spread_ref[0], spread_ref[1])):
-        for t in range(y_ref.shape[1] // 128):
+        for t in range(cols // 128):
             y_ref[(q + 1) * per : (q + 1) * per + count, t * 128 : (t + 1) * 128] = z[t * count : (t + 1) * count]
     y_ref[0:per, :] = shift_right(y_ref[4 * per : 5 * per, :])
     return y_ref[...].astype(BF)
 
 
-def pack_kernel(members, channels, rows, x_ref, down_ref, up_ref, d_scr, u_scr):
-    wide = x_ref.shape[1]
+def prepare_kernel(members, channels, per, spread_ref, own_ref, above_ref, below_ref):
+    row_of = lax.broadcasted_iota(jnp.int32, (256, 256), 0)
+    lane_of = lax.broadcasted_iota(jnp.int32, (256, 256), 1)
+    place = lane_of // 64
+    for odd in range(2):
+        spread_ref[odd] = jnp.where(row_of == 4 * (lane_of - 64 * place) + (place ^ odd), 1.0, 0.0).astype(BF)
+
+    def tap_of(lanes):
+        tap = lax.broadcasted_iota(jnp.int32, (48, lanes), 0)
+        c = sum(((tap >= 9 * k).astype(jnp.int32) for k in range(1, channels)), jnp.zeros_like(tap))
+        rest = tap - 9 * c
+        dr = (rest >= 3).astype(jnp.int32) + (rest >= 6).astype(jnp.int32)
+        return c, dr, rest - 3 * dr, lax.broadcasted_iota(jnp.int32, (48, lanes), 1)
+
+    def one_hot(hit):
+        return jnp.where(hit, 1.0, 0.0).astype(BF)
+
+    c, dr, dc, lane = tap_of(own_ref.shape[3])
+    for j in range(5):
+        row = 2 * j + dr - 1
+        for pc in range(2):
+            at = ((2 * pc + dc) * channels + c) * 8 + row
+            own_ref[j, pc] = one_hot((lane == at) & (row >= 0) & (row < 8))
+    c, dr, dc, lane = tap_of(above_ref.shape[4])
+    for m in range(members):
+        for kind in range(2):
+            slot = dr + 2 * kind
+            for pc in range(2):
+                at = (2 * pc + dc) * per[0] + (m * channels + c) * UP + slot
+                above_ref[m, kind, pc] = one_hot((lane == at) & (slot < UP))
+    c, dr, dc, lane = tap_of(below_ref.shape[3])
+    for m in range(members):
+        for pc in range(2):
+            at = (2 * pc + dc) * per[1] + (m * channels + c) * DOWN + dr - 1
+            below_ref[m, pc] = one_hot((lane == at) & (dr >= 1))
+
+
+def pack_kernel(members, channels, rows, xa_ref, xb_ref, _, down_ref, up_ref, d_scr, u_scr):
+    wide = xa_ref.shape[1]
     lanes = down_ref.shape[1]
+    cut = xa_ref.shape[0]
     nd, nu = members * channels * UP, members * channels * DOWN
     for t in range(wide // lanes):
         for g in range(members * channels):
-            block = x_ref[g * rows : (g + 1) * rows, t * lanes : (t + 1) * lanes].astype(F32)
+            ref, at = (xa_ref, g * rows) if g * rows < cut else (xb_ref, g * rows - cut)
+            block = ref[at : at + rows, t * lanes : (t + 1) * lanes].astype(F32)
             d_scr[t * nd + g * UP : t * nd + (g + 1) * UP, :] = block[rows - UP : rows]
             u_scr[t * nu + g * DOWN : t * nu + (g + 1) * DOWN, :] = block[0:DOWN]
     down_ref[...] = d_scr[...].astype(BF)
@@ -96,22 +144,15 @@
 
 
 def inner_kernel(
-    members, channels, rows, per,
-    x_ref, w1_ref, w2_ref, w3_ref, mix_ref,
-    h1_ref, h_first, h_last, a_last, v_second, v_third,
-    w2_big, w3_big, w1_down, w1_up, spread_ref, mix_own,
+    members, channels, rows,
+    x_ref, w1_ref, w2_ref, w3_ref, mix_ref, spread_ref, own_ref, above_ref, below_ref,
+    h1_ref, h_first, h_last, a_last, v_second, v_third, h2_mid,
+    w2_big, w3_big, w1_down, w1_up, mix_own,
     w1_flat, w1_own, y_ref, out1_ref, h2_ref,
 ):
     half, groups = rows // 2, rows // 8
     wide = x_ref.shape[1]
     cols = wide // 4
-
-    row_of = lax.broadcasted_iota(jnp.int32, (256, 256), 0)
-    lane_of = lax.broadcasted_iota(jnp.int32, (256, 256), 1)
-    place = lane_of // 64
-    for odd in range(2):
-        q = place ^ odd
-        spread_ref[odd] = jnp.where(row_of == 4 * (lane_of - 64 * place) + q, 1.0, 0.0).astype(BF)
 
     w1_flat[...] = jnp.zeros_like(w1_flat)
     for c in range(channels):
@@ -119,34 +160,16 @@
             at = (c * 3 + dr) * 3
             w1_flat[at : at + 3, :] = 0.5 * w1_ref[c, dr].astype(F32)
     w1 = w1_flat[...].astype(BF)
-    taps = w1.shape[0]
-
-    def taps_at(lanes, target):
-        tap = lax.broadcasted_iota(jnp.int32, (taps, lanes), 0)
-        c = sum(((tap >= 9 * k).astype(jnp.int32) for k in range(1, channels)), jnp.zeros_like(tap))
-        rest = tap - 9 * c
-        dr = (rest >= 3).astype(jnp.int32) + (rest >= 6).astype(jnp.int32)
-        dc = rest - 3 * dr
-        to, valid = target(c, dr, dc)
-        at = lax.broadcasted_iota(jnp.int32, (taps, lanes), 1)
-        return dot_t(w1, jnp.where((at == to) & valid, 1.0, 0.0).astype(BF)).astype(BF)
-
     for pc in range(2):
         for j in range(5):
-            def own(c, dr, dc):
-                row = 2 * j + dr - 1
-                return ((2 * pc + dc) * channels + c) * 8 + row, (row >= 0) & (row < 8)
-            w1_own[j * 128 + pc * 64 : j * 128 + pc * 64 + 64, :] = taps_at(w1_own.shape[1], own)
+            at = j * 128 + pc * 64
+            w1_own[at : at + 64, :] = dot_t(w1, own_ref[j, pc]).astype(BF)
         for m in range(members):
             for kind in range(2):
-                def above(c, dr, dc):
-                    slot = dr if kind == 0 else dr + 2
-                    return (2 * pc + dc) * per[0] + (m * channels + c) * UP + slot, slot < UP
-                w1_down[m, kind * 128 + pc * 64 : kind * 128 + pc * 64 + 64, :] = taps_at(w1_down.shape[2], above)
-            def below(c, dr, dc):
-                return (2 * pc + dc) * per[1] + (m * channels + c) * DOWN + dr - 1, dr >= 1
-            w1_up[m, pc * 64 : pc * 64 + 64, :] = taps_at(w1_up.shape[2], below)
-
+                at = m * 256 + kind * 128 + pc * 64
+                w1_down[at : at + 64, :] = dot_t(w1, above_ref[m, kind, pc]).astype(BF)
+            at = m * 128 + pc * 64
+            w1_up[at : at + 64, :] = dot_t(w1, below_ref[m, pc]).astype(BF)
     w2_big[...] = jnp.zeros_like(w2_big)
     for ocol in range(2):
         for dr in range(3):
@@ -181,23 +204,24 @@
     for m in range(members):
         for g in range(groups):
             out1_ref[g] = dot(w1_own[...], y_ref[m, g].astype(BF))
-        h_first[m] = out1_ref[0, 0:128]
-        h_last[m] = out1_ref[groups - 1, 512:640]
-        rows_of = h1_ref.at[m]
+        lanes = slice(m * cols, (m + 1) * cols)
+        h_first[:, lanes] = out1_ref[0, 0:128]
+        h_last[:, lanes] = out1_ref[groups - 1, 512:640]
         for h in range(1, half):
             g, j = h // 4, h % 4
             v = out1_ref[g, j * 128 : j * 128 + 128]
             if j == 0:
                 v = v + out1_ref[g - 1, 512:640]
-            put_hidden(rows_of, h - 1, silu_of_half(v))
-        a_last[m] = dot(w2_big[:, 0:512], h1_ref[m, (half - 3) * 256 : (half - 1) * 256, :])
-        for o in range(2):
-            h2_ref[o * 128 : o * 128 + 128, :] = silu_of_half(
-                dot(w2_big[...], h1_ref[m, o * 256 : (o + 3) * 256, :])
-            ).astype(BF)
-        v = dot(w3_big[...], h2_ref[...])
-        v_second[m] = v[0:32]
-        v_third[m] = v[32:64]
+            put_hidden(h1_ref, h - 1, lanes, silu_of_half(v))
+    a_last[...] = dot(w2_big[:, 0:512], h1_ref[(half - 3) * 256 : (half - 1) * 256, :])
+    for o in range(2):
+        h2_ref[o * 128 : o * 128 + 128, :] = silu_of_half(
+            dot(w2_big[...], h1_ref[o * 256 : (o + 3) * 256, :])
+        ).astype(BF)
+    v = dot(w3_big[...], h2_ref[...])
+    v_second[...] = v[0:32]
+    v_third[...] = v[32:64]
+    h2_mid[...] = silu_of_half(dot(w2_big[...], h1_ref[512:1280, :])).astype(BF)
 
 
 def low_kernel(
@@ -207,37 +231,48 @@
 ):
     below = is_row(lax.axis_size("row") - 1)
     y = place_halo(got_ref[...], spread_ref, y_ref, members * channels * DOWN, per)
-    for m in range(members):
-        put_hidden(h1_ref, m, silu_of_half((dot(w1_ref[m], y) + h_ref[m]) * below))
-        h2 = silu_of_half(dot(w2_ref[:, 512:768], h1_ref[m * 256 : m * 256 + 256, :]) + a_ref[m]).astype(BF)
-        h2_ref[m] = h2
-        v = dot(w3_ref[32:64, 128:256], h2)
-        carry_ref[m * 16 : m * 16 + 16, :] = (v[0:16] + shift_right(v[16:32])).astype(BF)
+    cols = y_ref.shape[1]
+    fresh = dot(w1_ref[...], y)
+    for m in range(members):
+        lanes = slice(m * cols, (m + 1) * cols)
+        put_hidden(h1_ref, 0, lanes, silu_of_half((fresh[m * 128 : m * 128 + 128] + h_ref[:, lanes]) * below))
+    h2 = silu_of_half(dot(w2_ref[:, 512:768], h1_ref[...]) + a_ref[...]).astype(BF)
+    h2_ref[...] = h2
+    v = dot(w3_ref[32:64, 128:256], h2)
+    for m in range(members):
+        lanes = slice(m * cols, (m + 1) * cols)
+        carry_ref[m * 16 : m * 16 + 16, :] = (v[0:16, lanes] + shift_right(v[16:32, lanes])).astype(BF)
 
 
 def middle_kernel(
     members, half,
-    h1_ref, h2_low, w2_ref, w3_ref, v_ref, mix_ref,
+    h1_ref, h2_mid, h2_low, w2_ref, w3_ref, v_ref, mix_ref,
     a_first, a_second, mixed_ref, h2_ref,
 ):
-    parts = {}
-    for m in range(members):
-        a_first[m] = dot(w2_ref[:, 512:768], h1_ref[m, 0:256, :])
-        a_second[m] = dot(w2_ref[:, 256:768], h1_ref[m, 0:512, :])
-        carry = v_ref[m]
-        for a in range(4, half, 2):
-            for o in (a, a + 1):
-                at = slice((o - a) * 128, (o - a) * 128 + 128)
-                if o == half - 1:
-                    h2_ref[at, :] = h2_low[m]
-                else:
-                    h2_ref[at, :] = silu_of_half(dot(w2_ref[...], h1_ref[m, (o - 2) * 256 : (o + 1) * 256, :])).astype(BF)
-            v = dot(w3_ref[...], h2_ref[...])
-            w = v[0:32] + carry
-            carry = v[32:64]
-            parts[a // 2, m] = silu_of_half(w[0:16] + shift_right(w[16:32])).astype(BF)
-    for r in range(2, half // 2):
-        mixed_ref[r - 2] = dot(mix_ref[...], jnp.concatenate([parts[r, m] for m in range(members)], axis=0))
+    wide = h1_ref.shape[1]
+    cols = wide // members
+    a_first[...] = dot(w2_ref[:, 512:768], h1_ref[0:256, :])
+    a_second[...] = dot(w2_ref[:, 256:768], h1_ref[0:512, :])
+    pairs = range(4, half, 2)
+    for n, a in enumerate(pairs):
+        lanes = slice(n * wide, (n + 1) * wide)
+        for o in (a, a + 1):
+            at = slice((o - a) * 128, (o - a) * 128 + 128)
+            if o == half - 1:
+                h2_ref[at, lanes] = h2_low[...]
+            elif o == 4:
+                h2_ref[at, lanes] = h2_mid[...]
+            else:
+                h2_ref[at, lanes] = silu_of_half(
+                    dot(w2_ref[...], h1_ref[(o - 2) * 256 : (o + 1) * 256, :])
+                ).astype(BF)
+    v = dot(w3_ref[...], h2_ref[...])
+    carry = v_ref[...]
+    for n in range(len(pairs)):
+        w = v[0:32, n * wide : (n + 1) * wide] + carry
+        carry = v[32:64, n * wide : (n + 1) * wide]
+        parts = [bottleneck(w[:, m * cols : (m + 1) * cols]) for m in range(members)]
+        mixed_ref[n] = dot(mix_ref[...], jnp.concatenate(parts, axis=0))
 
 
 def top_kernel(
@@ -247,19 +282,20 @@
 ):
     source = (got_ref[...].astype(F32) * is_row(0)).astype(BF)
     y = place_halo(source, spread_ref, y_ref, members * channels * UP, per)
+    cols = y_ref.shape[1]
+    fresh = dot(w1_ref[...], y)
+    for m in range(members):
+        lanes = slice(m * cols, (m + 1) * cols)
+        put_hidden(h1_ref, 0, lanes, silu_of_half(fresh[m * 256 : m * 256 + 128]))
+        put_hidden(h1_ref, 1, lanes, silu_of_half(fresh[m * 256 + 128 : m * 256 + 256] + h_ref[:, lanes]))
+    h2_ref[0:128, :] = silu_of_half(dot(w2_ref[:, 0:512], h1_ref[...]) + a_first[...]).astype(BF)
+    h2_ref[128:256, :] = silu_of_half(dot(w2_ref[:, 0:256], h1_ref[256:512, :]) + a_second[...]).astype(BF)
+    v = dot(w3_ref[...], h2_ref[...])
     second = []
     for m in range(members):
-        fresh = dot(w1_ref[m], y)
-        put_hidden(h1_ref, 2 * m, silu_of_half(fresh[0:128]))
-        put_hidden(h1_ref, 2 * m + 1, silu_of_half(fresh[128:256] + h_ref[m]))
-        both = h1_ref[m * 512 : m * 512 + 512, :]
-        h2_ref[0:128, :] = silu_of_half(dot(w2_ref[:, 0:512], both) + a_first[m]).astype(BF)
-        h2_ref[128:256, :] = silu_of_half(dot(w2_ref[:, 0:256], both[256:512]) + a_second[m]).astype(BF)
-        v = dot(w3_ref[...], h2_ref[...])
-        pre_ref[m] = v[0:16] + shift_right(v[16:32])
-        w = v[32:64] + v_ref[m]
-        second.append(silu_of_half(w[0:16] + shift_right(w[16:32])).astype(BF))
-    cols = y_ref.shape[1]
+        lanes = slice(m * cols, (m + 1) * cols)
+        pre_ref[m] = v[0:16, lanes] + shift_right(v[16:32, lanes])
+        second.append(bottleneck(v[32:64, lanes] + v_ref[:, lanes]))
     tall = tail_ref.shape[0]
     tail_ref[:, 0:128] = jnp.zeros((tall, 128), F32)
     tail_ref[:, 128 + cols : 256 + cols] = jnp.zeros((tall, 128), F32)
@@ -402,7 +438,20 @@
     return inside, [a for a in range(2 * rows) if a not in inside]
 
 
-def decoder_inner(nb, ext_ref, d1_ref, d2_ref, wd1, wd2, u_ref, join_ref, turn_ref, part_ref, l_ref, g_ref):
+def by_phase(v):
+    return jnp.concatenate(
+        [v[(pr * 4 + ph) * 16 : (pr * 4 + ph + 1) * 16] for ph in range(4) for pr in range(2)], axis=0
+    )
+
+
+def merge_phases(a, b):
+    return jnp.concatenate([v[ph * 32 : ph * 32 + 32] for ph in range(4) for v in (a, b)], axis=0)
+
+
+def decoder_inner(
+    nb, ext_ref, d1_ref, d2_ref,
+    w_edge, w_field, up_part, field_part, join_ref, turn_ref, part_ref, wd1, wd2, l_ref, u_ref, g_ref,
+):
     wd1[...] = jnp.zeros_like(wd1)
     wd2[...] = jnp.zeros_like(wd2)
     for pr, rr, tr in TRANSPOSED:
@@ -421,6 +470,7 @@
     join_ref[...] = jnp.where(to == 4 * (frm - nb * place) + place, 1.0, 0.0).astype(BF)
     inside, outside = split_rows(rows)
     turn_ref[...] = level_first(4 * rows, outside)
+
     l_ref[0] = jnp.zeros_like(l_ref[0])
     l_ref[1] = jnp.zeros_like(l_ref[0])
     l_ref[2 : rows + 2] = ext_ref[...]
@@ -433,28 +483,51 @@
     g = dot(level_first(4 * rows, inside), g_ref[...]).astype(BF)
     part_ref[...] = dot(g, join_ref[...])
 
+    w_edge[0, 0:64, :] = wd1[64:128, 96:192]
+    w_edge[0, 64:128, :] = wd1[0:64, 0:96]
+    w_edge[1, 0:64, :] = wd1[64:128, 192:288]
+    w_edge[1, 64:128, :] = wd1[0:64, 96:192]
+    up_part[0] = dot(w_edge[1], ext_ref[0])
+    up_part[1] = dot(w_edge[0], ext_ref[rows - 1])
+
+    def known(taps, first, count):
+        return by_phase(dot(wd2[:, taps : taps + 128 * count], u_ref[(first + 1) * 128 : (first + 1 + count) * 128, :]))
+
+    last = 2 * rows - 1
+    field_part[0] = merge_phases(known(256, 1, 1), known(128, 1, 2))
+    field_part[1] = merge_phases(known(0, last - 2, 2), known(0, last - 1, 1))
+    none = jnp.zeros((128, 128), BF)
+    w = [by_phase(wd2[:, rr * 128 : rr * 128 + 128]) for rr in range(3)]
+    w_field[0] = merge_phases(jnp.concatenate([w[0], w[1]], axis=1), jnp.concatenate([none, w[0]], axis=1))
+    w_field[1] = merge_phases(jnp.concatenate([w[2], none], axis=1), jnp.concatenate([w[1], w[2]], axis=1))
+
 
 def decoder_kernel(
-    nb, ext_ref, first_ref, second_ref, w1_ref, w2_ref, u_in, join_ref, turn_ref, part_ref,
+    nb, first_ref, second_ref, w_edge, w_field, up_part, field_part, join_ref, turn_ref, part_ref,
     out_ref, l_ref, u_ref, g_ref,
 ):
     odd_row = lax.rem(lax.axis_index("row"), 2) == 1
-    keep_first, keep_last = is_row(0), is_row(lax.axis_size("row") - 1)
-    rows, _, wide = ext_ref.shape
+    keeps = is_row(0), is_row(lax.axis_size("row") - 1)
+    wide = l_ref.shape[2]
     first, second = first_ref[...].astype(F32), second_ref[...].astype(F32)
-    l_ref[0] = jnp.zeros_like(l_ref[0])
-    l_ref[rows + 3] = jnp.zeros_like(l_ref[0])
-    put_latent(l_ref, 1, jnp.where(odd_row, first, second) * keep_first)
-    l_ref[2 : rows + 2] = ext_ref[...]
-    put_latent(l_ref, rows + 2, jnp.where(odd_row, second, first) * keep_last)
-    u_ref[...] = u_in[...]
+    put_latent(l_ref, 0, jnp.where(odd_row, first, second) * keeps[0])
+    put_latent(l_ref, 1, jnp.where(odd_row, second, first) * keeps[1])
     keep_even, keep_odd = column_keeps(nb, wide)
-    keeps = {-1: keep_first, 2 * rows: keep_last}
-    for a in (-1, 0, rows - 1, rows):
-        upsample_row(
-            w1_ref[...], l_ref, a, keep_even, keep_odd, rows, u_ref, (-1, 0, 2 * rows - 1, 2 * rows), keeps
-        )
-    field_rows(w2_ref[...], u_ref, g_ref, split_rows(rows)[1])
+    for side in range(2):
+        v = silu_of_half(dot(w_edge[side], l_ref[side]) + up_part[side])
+        for line in range(2):
+            even = v[line * 64 : line * 64 + 32] * keep_even
+            odd = v[line * 64 + 32 : line * 64 + 64] * keep_odd
+            if line == side:
+                even, odd = even * keeps[side], odd * keeps[side]
+            at = line * 128
+            u_ref[side, at : at + 32, :] = pltpu.roll(odd, 1, 1)[:, 0:nb].astype(BF)
+            u_ref[side, at + 32 : at + 64, :] = even[:, 0:nb].astype(BF)
+            u_ref[side, at + 64 : at + 96, :] = odd[:, 0:nb].astype(BF)
+            u_ref[side, at + 96 : at + 128, :] = pltpu.roll(even, wide - 1, 1)[:, 0:nb].astype(BF)
+        v = (dot(w_field[side], u_ref[side]) + field_part[side]).astype(BF)
+        for ph in range(4):
+            g_ref[side * 64 : side * 64 + 64, ph * nb : (ph + 1) * nb] = v[ph * 64 : ph * 64 + 64]
     g = dot(g_ref[...], join_ref[...]).astype(BF)
     out_ref[...] = (dot(turn_ref[...], g) + part_ref[...]).astype(BF).reshape(out_ref.shape)
 
@@ -497,29 +570,41 @@
     total = padded(5 * per[0], 16), padded(5 * per[1], 16)
     pack = functools.partial(pack_kernel, count, channels, rows)
     sizes = [(nd * chunks, lanes), (nu * chunks, lanes)]
-    down, up = call(pack, [(s, BF) for s in sizes], [(s, F32) for s in sizes], x, mb=16, us=20)
+    cut = (count * channels) // 2 * rows
+    spreads, own, above, below = call(
+        functools.partial(prepare_kernel, count, channels, per),
+        [
+            ((2, 256, 256), BF),
+            ((5, 2, 48, 5 * channels * 8), BF),
+            ((count, 2, 2, 48, total[0]), BF),
+            ((count, 2, 48, total[1]), BF),
+        ],
+        [],
+    )
+    down, up = call(pack, [(s, BF) for s in sizes], [(s, F32) for s in sizes], x[:cut], x[cut:], below, mb=16, us=20)
     up = shifted(up, -1)
     down = shifted(down, 1)
 
     w1 = enc_first.transpose(1, 2, 3, 0)
     w2 = enc_second.transpose(2, 3, 0, 1).reshape(9, 64, 64)
     w3 = enc_third.transpose(2, 3, 0, 1).reshape(9, 16, 64)
-    row_f32 = ((count, 128, cols), F32)
-    third_f32 = ((count, 32, cols), F32)
+    wide_cols = count * cols
+    row_f32 = ((128, wide_cols), F32)
+    third_f32 = ((32, wide_cols), F32)
     (
-        h1, h_first, h_last, a_last, v_second, v_third,
-        w2_big, w3_big, w1_down, w1_up, spreads, mix,
+        h1, h_first, h_last, a_last, v_second, v_third, h2_mid,
+        w2_big, w3_big, w1_down, w1_up, mix,
     ) = call(
-        functools.partial(inner_kernel, count, channels, rows, per),
-        [((count, 256 * (half - 1), cols), BF)]
+        functools.partial(inner_kernel, count, channels, rows),
+        [((256 * (half - 1), wide_cols), BF)]
         + [row_f32] * 3
         + [third_f32] * 2
         + [
+            ((128, wide_cols), BF),
             ((128, 768), BF),
             ((64, 256), BF),
-            ((count, 256, total[0]), BF),
-            ((count, 128, total[1]), BF),
-            ((2, 256, 256), BF),
+            ((count * 256, total[0]), BF),
+            ((count * 128, total[1]), BF),
             ((32, count * CH_BOT), BF),
         ],
         [
@@ -527,27 +612,27 @@
             ((640, 5 * channels * 8), BF),
             ((count, rows // 8, 5 * channels * 8, cols), F32),
             ((rows // 8, 640, cols), F32),
-            ((256, cols), BF),
+            ((256, wide_cols), BF),
         ],
-        x, w1, w2, w3, mix_weight, mb=24,
+        x, w1, w2, w3, mix_weight, spreads, own, above, below, mb=24,
     )
     h2_low, carry = call(
         functools.partial(low_kernel, count, channels, per[1]),
-        [((count, 128, cols), BF), ((count * CH_BOT, cols), BF)],
-        [((total[1], cols), F32), ((count * 256, cols), BF)],
+        [((128, wide_cols), BF), ((count * CH_BOT, cols), BF)],
+        [((total[1], cols), F32), ((256, wide_cols), BF)],
         up, spreads, w1_up, h_last, w2_big, a_last, w3_big, mb=12,
     )
     carry = shifted(carry, 1)
     a_first, a_second, mid = call(
         functools.partial(middle_kernel, count, half),
         [row_f32, row_f32, ((quarter - 2, 32, cols), F32)],
-        [((256, cols), BF)],
-        h1, h2_low, w2_big, w3_big, v_third, mix, mb=12,
+        [((256, (half // 2 - 2) * wide_cols), BF)],
+        h1, h2_mid, h2_low, w2_big, w3_big, v_third, mix, mb=12,
     )
     pre, tail = call(
         functools.partial(top_kernel, count, channels, per[0]),
         [((count, CH_BOT, cols), F32), ((quarter * 32 - 32, cols + 256), F32)],
-        [((total[0], cols), F32), ((count * 512, cols), BF), ((256, cols), BF)],
+        [((total[0], cols), F32), ((512, wide_cols), BF), ((256, wide_cols), BF)],
         down, spreads, w1_down, h_first, w2_big, a_first, a_second, w3_big, v_second, mix, mid, mb=12,
     )
     slots = peers // 2
@@ -576,24 +661,31 @@
     d1 = d1.transpose(2, 3, 0, 1).reshape(16, 32, 32)
     d2 = d2.transpose(2, 3, 0, 1).reshape(16, 16, 32)
     inside, outside = split_rows(quarter)
-    wd1, wd2, u, join, turn, part = call(
+    edge_parts = call(
         functools.partial(decoder_inner, nb),
         [
-            ((128, 288), BF),
-            ((128, 384), BF),
-            ((128 * (half + 2), nb), BF),
+            ((2, 128, 96), BF),
+            ((2, 256, 256), BF),
+            ((2, 128, ext), F32),
+            ((2, 256, nb), F32),
             ((4 * nb, 4 * nb), BF),
             ((16 * rows, 32 * len(outside)), BF),
             ((16 * rows, 4 * nb), F32),
         ],
-        [((quarter + 3, 96, ext), BF), ((32 * len(inside), 4 * nb), BF)],
+        [
+            ((128, 288), BF),
+            ((128, 384), BF),
+            ((quarter + 3, 96, ext), BF),
+            ((128 * (half + 2), nb), BF),
+            ((32 * len(inside), 4 * nb), BF),
+        ],
         latent, d1, d2,
     )
     (out,) = call(
         functools.partial(decoder_kernel, nb),
         [((16, rows, 4 * nb), BF)],
-        [((quarter + 4, 96, ext), BF), ((128 * (half + 2), nb), BF), ((32 * len(outside), 4 * nb), BF)],
-        latent, first, second, wd1, wd2, u, join, turn, part,
+        [((2, 96, ext), BF), ((2, 256, nb), BF), ((128, 4 * nb), BF)],
+        first, second, *edge_parts,
     )
     return out
 

time: 37 us -> 36.3 us (0.981)
  Pallas kernels: 14.7 us -> 13.8 us
  waiting for transfers between devices: 6.69 us -> 7.34 us
    ppermute x1, starting transfers between devices: 2.38 us -> 1.44 us  [per_device(): lax.ppermute(second, 'row', [(i, (i + 1 if i % 2 else i - 1) % lines) for...]
    ppermute x1, starting transfers between devices: 0.66 us -> 1.6 us  [per_device(): first = lax.ppermute(first, 'row', [(i, i ^ 1) for i in range(lines)])]
    pallas_call x10 -> x11, Pallas kernels: 14.7 us -> 13.8 us  [call(): pl.pallas_call(kernel, out_shape=[jax.ShapeDtypeStruct(*o) for o in outs]...]
    ppermute x1, waiting for transfers between devices: 1.02 us -> 1.87 us  [per_device(): lax.ppermute(second, 'row', [(i, (i + 1 if i % 2 else i - 1) % lines) for...]
    unnamed x16 -> x14, local copies, waits for them, and re-layouts: 1.36 us -> 1.12 us
  transfers between devices with their start and end apart: 9 -> 9, of which waited for: 5 -> 4; matrix products, arithmetic and copies ran while one was open for 0% -> 0% of each run, Pallas kernels for 33% -> 30%
where the time goes in v4:
time: 36.3 us; the launch traced here: 36.2 us
  Pallas kernels  13.8 us (38%)
  starting transfers between devices  13.6 us (37%)
  waiting for transfers between devices  7.34 us (20%)
  local copies, waits for them, and re-layouts  1.27 us (3%)
    pallas_call x11, Pallas kernels, call(): pl.pallas_call(kernel, out_shape=[jax.ShapeDtypeStruct(*o) for o in outs]...  13.8 us
    ppermute x3, starting transfers between devices, shifted(): lax.ppermute(value, 'row', [(i, (i + by) % peers) for i in range(peers)])  6.29 us
    ppermute x4, waiting for transfers between devices, swapped(): lax.ppermute(value, 'mem', [(i, i ^ by) for i in range(lax.axis_size('mem...  5.46 us
    ppermute x4, starting transfers between devices, swapped(): lax.ppermute(value, 'mem', [(i, i ^ by) for i in range(lax.axis_size('mem...  4.29 us
    ppermute x1, waiting for transfers between devices, per_device(): lax.ppermute(second, 'row', [(i, (i + 1 if i % 2 else i - 1) % lines) for...  1.87 us
    ppermute x1, starting transfers between devices, per_device(): first = lax.ppermute(first, 'row', [(i, i ^ 1) for i in range(lines)])  1.6 us
    ppermute x1, starting transfers between devices, per_device(): lax.ppermute(second, 'row', [(i, (i + 1 if i % 2 else i - 1) % lines) for...  1.44 us
    unnamed x14, local copies, waits for them, and re-layouts  1.12 us
  transfers between devices with their start and end apart: 9, of which 4 were waited for; matrix products, arithmetic and copies ran while one was open for 0% of the time, Pallas kernels for 30%

profile of v4, /device:TPU:0, one launch (start us, length us, event | category | flops | bytes accessed | tf_op | source)
XLA Modules:
  0.0 36.2 jit_solution(1872794813108440121)
XLA Ops:
  0.0 0.0 copy-start
  0.0 0.2 shard_map.73
  0.2 1.1 %copy-done = bf16[2,5,16,4096]{3,2,1,0:T(8,128)(2,1)S(1)} copy-done((bf16[2,5,16,4096]{3,2,1,0:T(8,128)(2,1)S(1)}, bf16[2,5,16,4096]{3,2,1,0:T(8,128)(2,1)}, u32[]{:S(2)}) %copy-start) | copy-done | bytes 1310744
  1.3 0.1 fusion
  1.4 0.0 copy-start.1
  1.4 0.0 copy-start.2
  1.4 0.0 copy-start.3
  1.5 0.0 copy-start.4
  1.5 0.2 shard_map.74
  1.7 3.9 %collective-permute-start.1 = (bf16[160,512]{1,0:T(8,128)(2,1)S(1)}, bf16[160,512]{1,0:T(8,128)(2,1)S(1)}, u32[]{:S(2)}, u32[]{:S(2)}) collective-permute-start(bf16[160,512]{1,0:T(8,128)(2,1)S(1)} %get-tuple-element.58), channel_id=1, source_target_pairs={{0,3},{1,0},{2,1},{3,2},{4,7},{5,4},{6,5},{7,6},{8,11},{9,8},{10,9... | collective-permute-start | bytes 491528 | tf_op jit(solution)/shard_map/ppermute | solution.py:537
  5.7 0.0 collective-permute-start
  5.7 0.0 copy-done.1
  5.7 0.0 copy-done.2
  5.7 0.0 copy-done.3
  5.7 0.0 copy-done.4
  5.7 4.7 %shard_map.75 = (bf16[1792,2048]{1,0:T(8,128)(2,1)S(1)}, f32[128,2048]{1,0:T(8,128)S(1)}, f32[128,2048]{1,0:T(8,128)S(1)}, f32[128,2048]{1,0:T(8,128)S(1)}, f32[...) custom-call(bf16[160,4096]{1,0:T(8,128)(2,1)S(1)} %bitcast.14, ...), custom_call_target="tpu_custom_call" | custom-call | flops 1000000000 | bytes 3000000 | tf_op jit(solution)/shard_map/pallas_call | solution.py:548
  10.4 0.0 collective-permute-done.1.got_ref
  10.4 1.2 %shard_map.76 = (bf16[128,2048]{1,0:T(8,128)(2,1)S(1)}, bf16[32,1024]{1,0:T(8,128)(2,1)S(1)}) custom-call(bf16[160,512]{1,0:T(8,128)(2,1)S(1)} %collective-permute-done.1.got_ref, bf16[2,256,256]{2,1,0:T(8,128)(2,1)S(1)} %get-tuple-element.50.spread_ref, bf16[256,128]{1,0:T(8,128)(2,1)S(1)} %get-tuple-element.59.w1_ref, ...), custom_call_target="tpu_custom_call" | custom-call | flops 1000000000 | bytes 3000000 | tf_op jit(solution)/shard_map/pallas_call | solution.py:548
  11.7 2.3 %collective-permute-start.2 = (bf16[32,1024]{1,0:T(8,128)(2,1)S(1)}, bf16[32,1024]{1,0:T(8,128)(2,1)S(1)}, u32[]{:S(2)}, u32[]{:S(2)}) collective-permute-start(bf16[32,1024]{1,0:T(8,128)(2,1)S(1)} %get-tuple-element.71), channel_id=1, source_target_pairs={{0,1},{1,2},{2,3},{3,0},{4,5},{5,6},{6,7},{7,4},{8,9},{9,10},{10,1... | collective-permute-start | bytes 196616 | tf_op jit(solution)/shard_map/ppermute | solution.py:537
  14.0 2.0 %shard_map.77 = (f32[128,2048]{1,0:T(8,128)S(1)}, f32[128,2048]{1,0:T(8,128)S(1)}, f32[2,32,1024]{2,1,0:T(8,128)S(1)}) custom-call(bf16[1792,2048]{1,0:T(8,128)(2,1)S(1)} %get-tuple-element.56.h1_ref, bf16[128,2048]{1,0:T(8,128)(2,1)S(1)} %get-tuple-element.57.h2_mid, bf16[128,2048]{1,0:T(8,128)(2,1)S(1)} %get-tuple-element.63.h2_low, ...), custom_call_target="tpu_custom_call" | custom-call | flops 1000000000 | bytes 3000000 | tf_op jit(solution)/shard_map/pallas_call | solution.py:548
  16.0 0.0 collective-permute-done.got_ref
  16.0 1.8 %shard_map.78 = (f32[2,16,1024]{2,1,0:T(8,128)S(1)}, f32[96,1280]{1,0:T(8,128)S(1)}) custom-call(bf16[240,512]{1,0:T(8,128)(2,1)S(1)} %collective-permute-done.got_ref, bf16[2,256,256]{2,1,0:T(8,128)(2,1)S(1)} %get-tuple-element.50.spread_ref, bf16[512,160]{1,0:T(8,128)(2,1)S(1)} %get-tuple-element.53.w1_ref, f32[128,2048]{1,0:T(8,128)S(1)} %get-tuple-element.54.h_ref, ...), custom_call_target="tpu_custom_call" | custom-call | flops 1000000000 | bytes 3000000 | tf_op jit(solution)/shard_map/pallas_call | solution.py:548
  17.8 0.0 collective-permute-done.2.carry_ref
  17.8 0.4 shard_map.79
  18.1 0.0 collective-permute-start.3
  18.2 1.4 %collective-permute-done.3.got_ref = bf16[4,144,128]{2,1,0:T(8,128)(2,1)S(1)} collective-permute-done((bf16[4,144,128]{2,1,0:T(8,128)(2,1)S(1)}, bf16[4,144,128]{2,1,0:T(8,128)(2,1)S(1)}, u32[]{:S(2)}, u32[]{:S(2)}) %collective-permute-start.3) | collective-permute-done | bytes 147488 | tf_op jit(solution)/shard_map/ppermute | solution.py:541
  19.6 0.0 copy-start.6
  19.6 0.0 copy-start.5
  19.6 2.7 %collective-permute-start.5 = (bf16[144,128]{1,0:T(8,128)(2,1)S(1)}, bf16[144,128]{1,0:T(8,128)(2,1)S(1)}, u32[]{:S(2)}, u32[]{:S(2)}) collective-permute-start(bf16[144,128]{1,0:T(8,128)(2,1)S(1)} %get-tuple-element.77), channel_id=1, source_target_pairs={{0,16},{4,20},{8,24},{12,28},{16,0},{20,4},{24,8},{28,12},{1,17},{... | collective-permute-start | bytes 110600 | tf_op jit(solution)/shard_map/ppermute | solution.py:541
  22.3 1.3 %collective-permute-start.6 = (bf16[144,128]{1,0:T(8,128)(2,1)S(1)}, bf16[144,128]{1,0:T(8,128)(2,1)S(1)}, u32[]{:S(2)}, u32[]{:S(2)}) collective-permute-start(bf16[144,128]{1,0:T(8,128)(2,1)S(1)} %get-tuple-element.78), channel_id=1, source_target_pairs={{0,24},{4,28},{8,16},{12,20},{16,8},{20,12},{24,0},{28,4},{1,25},{... | collective-permute-start | bytes 110600 | tf_op jit(solution)/shard_map/ppermute | solution.py:541
  23.6 0.2 collective-permute-start.4
  23.8 0.0 copy-done.6
  23.9 0.0 copy-done.5
  23.9 1.0 %collective-permute-done.5.refs_1_ = bf16[144,128]{1,0:T(8,128)(2,1)S(1)} collective-permute-done((bf16[144,128]{1,0:T(8,128)(2,1)S(1)}, bf16[144,128]{1,0:T(8,128)(2,1)S(1)}, u32[]{:S(2)}, u32[]{:S(2)}) %collective-permute-start.5) | collective-permute-done | bytes 36896 | tf_op jit(solution)/shard_map/ppermute | solution.py:541
  24.9 3.1 %collective-permute-done.6.refs_2_ = bf16[144,128]{1,0:T(8,128)(2,1)S(1)} collective-permute-done((bf16[144,128]{1,0:T(8,128)(2,1)S(1)}, bf16[144,128]{1,0:T(8,128)(2,1)S(1)}, u32[]{:S(2)}, u32[]{:S(2)}) %collective-permute-start.6) | collective-permute-done | bytes 36896 | tf_op jit(solution)/shard_map/ppermute | solution.py:541
  28.0 0.0 collective-permute-done.4.refs_0_
  28.0 0.3 shard_map.81
  28.3 1.6 %collective-permute-start.7 = (bf16[32,256]{1,0:T(8,128)(2,1)S(1)}, bf16[32,256]{1,0:T(8,128)(2,1)S(1)}, u32[]{:S(2)}, u32[]{:S(2)}) collective-permute-start(bf16[32,256]{1,0:T(8,128)(2,1)S(1)} %get-tuple-element.79), channel_id=1, source_target_pairs={{0,1},{1,0},{2,3},{3,2},{4,5},{5,4},{6,7},{7,6},{8,9},{9,8},{10,11... | collective-permute-start | bytes 49160 | tf_op jit(solution)/shard_map/ppermute | solution.py:657
  29.9 1.4 %collective-permute-start.8 = (bf16[32,256]{1,0:T(8,128)(2,1)S(1)}, bf16[32,256]{1,0:T(8,128)(2,1)S(1)}, u32[]{:S(2)}, u32[]{:S(2)}) collective-permute-start(bf16[32,256]{1,0:T(8,128)(2,1)S(1)} %get-tuple-element.80), channel_id=1, source_target_pairs={{0,3},{1,2},{2,1},{3,0},{4,7},{5,6},{6,5},{7,4},{8,11},{9,10},{10,... | collective-permute-start | bytes 49160 | tf_op jit(solution)/shard_map/ppermute | solution.py:658
  31.3 1.3 %shard_map.82 = (bf16[2,128,96]{2,1,0:T(8,128)(2,1)S(1)}, bf16[2,256,256]{2,1,0:T(8,128)(2,1)S(1)}, f32[2,128,256]{2,1,0:T(8,128)S(1)}, f32[2,256,128]{2,1,0:T(8...) custom-call(bf16[4,96,256]{2,1,0:T(8,128)(2,1)S(1)} %get-tuple-element.81.ext_ref, ...), custom_call_target="tpu_custom_call" | custom-call | flops 1000000000 | bytes 3000000 | tf_op jit(solution)/shard_map/pallas_call | solution.py:548
  32.7 0.0 collective-permute-done.7.first_ref
  32.7 1.9 %collective-permute-done.8.second_ref = bf16[32,256]{1,0:T(8,128)(2,1)S(1)} collective-permute-done((bf16[32,256]{1,0:T(8,128)(2,1)S(1)}, bf16[32,256]{1,0:T(8,128)(2,1)S(1)}, u32[]{:S(2)}, u32[]{:S(2)}) %collective-permute-start.8) | collective-permute-done | bytes 16416 | tf_op jit(solution)/shard_map/ppermute | solution.py:658
  34.5 1.6 %shard_map.83 = bf16[16,16,512]{2,1,0:T(8,128)(2,1)} custom-call(bf16[32,256]{1,0:T(8,128)(2,1)S(1)} %collective-permute-done.7.first_ref, bf16[32,256]{1,0:T(8,128)(2,1)S(1)} %collective-permute-done.8.second_ref, bf16[2,128,96]{2,1,0:T(8,128)(2,1)S(1)} %get-tuple-element.84.w_edge, bf16[2,256,256]{2,1,0:T(8,128)(2,1)S(1)} %get-tuple-element.85.w_field, ...), custom_call_target="tpu_custom_call" | custom-call | flops 1000000000 | bytes 3000000 | tf_op jit(solution)/shard_map/pallas_call | solution.py:548
  (3 shorter events, 0.1 us)
Async XLA Ops:
  0.0 1.3 %copy-start = (bf16[2,5,16,4096]{3,2,1,0:T(8,128)(2,1)S(1)}, bf16[2,5,16,4096]{3,2,1,0:T(8,128)(2,1)}, u32[]{:S(2)}) copy-start(bf16[2,5,16,4096]{3,2,1,0:T(8,128)(2,1)} %param.7) | copy-start | bytes 3932164
  1.4 4.2 %copy-start.1 = (bf16[64,64,3,3]{1,0,3,2:T(8,128)(2,1)S(1)}, bf16[64,64,3,3]{1,0,3,2:T(8,128)(2,1)}, u32[]{:S(2)}) copy-start(bf16[64,64,3,3]{1,0,3,2:T(8,128)(2,1)} %param.9) | copy-start | bytes 221188
  1.4 4.2 %copy-start.2 = (bf16[16,64,3,3]{1,0,3,2:T(8,128)(2,1)S(1)}, bf16[16,64,3,3]{1,0,3,2:T(8,128)(2,1)}, u32[]{:S(2)}) copy-start(bf16[16,64,3,3]{1,0,3,2:T(8,128)(2,1)} %param.10) | copy-start | bytes 55300
  1.4 4.2 %copy-start.3 = (bf16[32,256]{1,0:T(8,128)(2,1)S(1)}, bf16[32,256]{1,0:T(8,128)(2,1)}, u32[]{:S(2)}) copy-start(bf16[32,256]{1,0:T(8,128)(2,1)} %mix_ref.1) | copy-start | bytes 49156
  1.5 4.2 %copy-start.4 = (bf16[64,5,3,3]{0,3,2,1:T(4,128)(2,1)S(1)}, bf16[64,5,3,3]{0,3,2,1:T(4,128)(2,1)}, u32[]{:S(2)}) copy-start(bf16[64,5,3,3]{0,3,2,1:T(4,128)(2,1)} %param.8) | copy-start | bytes 17284
  1.7 8.7 %collective-permute-start.1 = (bf16[160,512]{1,0:T(8,128)(2,1)S(1)}, bf16[160,512]{1,0:T(8,128)(2,1)S(1)}, u32[]{:S(2)}, u32[]{:S(2)}) collective-permute-start(bf16[160,512]{1,0:T(8,128)(2,1)S(1)} %get-tuple-element.58), channel_id=1, source_target_pairs={{0,3},{1,0},{2,1},{3,2},{4,7},{5,4},{6,5},{7,6},{8,11},{9,8},{10,9... | collective-permute-start | bytes 491528 | tf_op jit(solution)/shard_map/ppermute | solution.py:537
  5.7 10.4 %collective-permute-start = (bf16[240,512]{1,0:T(8,128)(2,1)S(1)}, bf16[240,512]{1,0:T(8,128)(2,1)S(1)}, u32[]{:S(2)}, u32[]{:S(2)}) collective-permute-start(bf16[240,512]{1,0:T(8,128)(2,1)S(1)} %get-tuple-element.49), channel_id=1, source_target_pairs={{0,1},{1,2},{2,3},{3,0},{4,5},{5,6},{6,7},{7,4},{8,9},{9,10},{10,1... | collective-permute-start | bytes 737288 | tf_op jit(solution)/shard_map/ppermute | solution.py:537
  11.7 6.1 %collective-permute-start.2 = (bf16[32,1024]{1,0:T(8,128)(2,1)S(1)}, bf16[32,1024]{1,0:T(8,128)(2,1)S(1)}, u32[]{:S(2)}, u32[]{:S(2)}) collective-permute-start(bf16[32,1024]{1,0:T(8,128)(2,1)S(1)} %get-tuple-element.71), channel_id=1, source_target_pairs={{0,1},{1,2},{2,3},{3,0},{4,5},{5,6},{6,7},{7,4},{8,9},{9,10},{10,1... | collective-permute-start | bytes 196616 | tf_op jit(solution)/shard_map/ppermute | solution.py:537
  18.1 1.4 %collective-permute-start.3 = (bf16[4,144,128]{2,1,0:T(8,128)(2,1)S(1)}, bf16[4,144,128]{2,1,0:T(8,128)(2,1)S(1)}, u32[]{:S(2)}, u32[]{:S(2)}) collective-permute-start(bf16[4,144,128]{2,1,0:T(8,128)(2,1)S(1)} %get-tuple-element.74), channel_id=1, source_target_pairs={{0,4},{4,0},{8,12},{12,8},{16,20},{20,16},{24,28},{28,24},{1,5},{5... | collective-permute-start | bytes 442376 | tf_op jit(solution)/shard_map/ppermute | solution.py:541
  19.6 4.3 %copy-start.6 = (bf16[16,32,4,4]{1,3,2,0:T(4,128)(2,1)S(1)}, bf16[16,32,4,4]{1,3,2,0:T(4,128)(2,1)}, u32[]{:S(2)}) copy-start(bf16[16,32,4,4]{1,3,2,0:T(4,128)(2,1)} %param.13) | copy-start | bytes 49156
  19.6 4.3 %copy-start.5 = (bf16[32,32,4,4]{1,3,2,0:T(4,128)(2,1)S(1)}, bf16[32,32,4,4]{1,3,2,0:T(4,128)(2,1)}, u32[]{:S(2)}) copy-start(bf16[32,32,4,4]{1,3,2,0:T(4,128)(2,1)} %param.12) | copy-start | bytes 98308
  19.6 5.3 %collective-permute-start.5 = (bf16[144,128]{1,0:T(8,128)(2,1)S(1)}, bf16[144,128]{1,0:T(8,128)(2,1)S(1)}, u32[]{:S(2)}, u32[]{:S(2)}) collective-permute-start(bf16[144,128]{1,0:T(8,128)(2,1)S(1)} %get-tuple-element.77), channel_id=1, source_target_pairs={{0,16},{4,20},{8,24},{12,28},{16,0},{20,4},{24,8},{28,12},{1,17},{... | collective-permute-start | bytes 110600 | tf_op jit(solution)/shard_map/ppermute | solution.py:541
  22.3 5.8 %collective-permute-start.6 = (bf16[144,128]{1,0:T(8,128)(2,1)S(1)}, bf16[144,128]{1,0:T(8,128)(2,1)S(1)}, u32[]{:S(2)}, u32[]{:S(2)}) collective-permute-start(bf16[144,128]{1,0:T(8,128)(2,1)S(1)} %get-tuple-element.78), channel_id=1, source_target_pairs={{0,24},{4,28},{8,16},{12,20},{16,8},{20,12},{24,0},{28,4},{1,25},{... | collective-permute-start | bytes 110600 | tf_op jit(solution)/shard_map/ppermute | solution.py:541
  23.6 4.4 %collective-permute-start.4 = (bf16[144,128]{1,0:T(8,128)(2,1)S(1)}, bf16[144,128]{1,0:T(8,128)(2,1)S(1)}, u32[]{:S(2)}, u32[]{:S(2)}) collective-permute-start(bf16[144,128]{1,0:T(8,128)(2,1)S(1)} %get-tuple-element.76), channel_id=1, source_target_pairs={{0,8},{4,12},{8,0},{12,4},{16,24},{20,28},{24,16},{28,20},{1,9},{5... | collective-permute-start | bytes 110600 | tf_op jit(solution)/shard_map/ppermute | solution.py:541
  28.3 4.4 %collective-permute-start.7 = (bf16[32,256]{1,0:T(8,128)(2,1)S(1)}, bf16[32,256]{1,0:T(8,128)(2,1)S(1)}, u32[]{:S(2)}, u32[]{:S(2)}) collective-permute-start(bf16[32,256]{1,0:T(8,128)(2,1)S(1)} %get-tuple-element.79), channel_id=1, source_target_pairs={{0,1},{1,0},{2,3},{3,2},{4,5},{5,4},{6,7},{7,6},{8,9},{9,8},{10,11... | collective-permute-start | bytes 49160 | tf_op jit(solution)/shard_map/ppermute | solution.py:657
  29.9 4.6 %collective-permute-start.8 = (bf16[32,256]{1,0:T(8,128)(2,1)S(1)}, bf16[32,256]{1,0:T(8,128)(2,1)S(1)}, u32[]{:S(2)}, u32[]{:S(2)}) collective-permute-start(bf16[32,256]{1,0:T(8,128)(2,1)S(1)} %get-tuple-element.80), channel_id=1, source_target_pairs={{0,3},{1,2},{2,1},{3,0},{4,7},{5,6},{6,5},{7,4},{8,11},{9,10},{10,... | collective-permute-start | bytes 49160 | tf_op jit(solution)/shard_map/ppermute | solution.py:658

commit v5 on v4

--- a/solution.py
+++ b/solution.py
@@ -378,9 +378,8 @@
         line = [latent[rows, 0:nb], turned[rows, 1:2], jnp.zeros((32, ext - nb - 2), F32), turned[rows, 0:1]]
         lines.append(jnp.concatenate(line, axis=1))
         put_latent(ext_ref, r, lines[-1])
-    odd = lax.rem(lax.axis_index("row"), 2) == 1
-    first_ref[...] = jnp.where(odd, lines[0], lines[-1]).astype(BF)
-    second_ref[...] = jnp.where(odd, lines[-1], lines[0]).astype(BF)
+    first_ref[...] = lines[-1].astype(BF)
+    second_ref[...] = lines[0].astype(BF)
 
 
 def upsample_row(w1, l_ref, a, keep_even, keep_odd, rows, u_ref, wanted, keeps):
@@ -510,8 +509,8 @@
     keeps = is_row(0), is_row(lax.axis_size("row") - 1)
     wide = l_ref.shape[2]
     first, second = first_ref[...].astype(F32), second_ref[...].astype(F32)
-    put_latent(l_ref, 0, jnp.where(odd_row, first, second) * keeps[0])
-    put_latent(l_ref, 1, jnp.where(odd_row, second, first) * keeps[1])
+    put_latent(l_ref, 0, first * keeps[0])
+    put_latent(l_ref, 1, second * keeps[1])
     keep_even, keep_odd = column_keeps(nb, wide)
     for side in range(2):
         v = silu_of_half(dot(w_edge[side], l_ref[side]) + up_part[side])
@@ -654,8 +653,8 @@
         [],
         mine, *[moved[k] for k in range(slots - 1)],
     )
-    first = lax.ppermute(first, "row", [(i, i ^ 1) for i in range(lines)])
-    second = lax.ppermute(second, "row", [(i, (i + 1 if i % 2 else i - 1) % lines) for i in range(lines)])
+    first = shifted(first, 1)
+    second = shifted(second, -1)
 
     d1, d2, _ = lax.optimization_barrier((dec_first, dec_second, others[0]))
     d1 = d1.transpose(2, 3, 0, 1).reshape(16, 32, 32)

time: 36.3 us -> 35.4 us (0.975)
  waiting for transfers between devices: 7.34 us -> 6.51 us
    ppermute x2 -> x0, starting transfers between devices: 3.05 us -> none  [the longest x1 1.6 us: per_device(): first = lax.ppermute(first, 'row', [(i, i ^ 1) for i in range(lines)])]
    ppermute x3 -> x5, starting transfers between devices: 6.29 us -> 9.27 us  [shifted(): lax.ppermute(value, 'row', [(i, (i + by) % peers) for i in range(peers)])]
    ppermute x2 -> x0, waiting for transfers between devices: 1.87 us -> none  [the longest x1 1.87 us: per_device(): lax.ppermute(second, 'row', [(i, (i + 1 if i % 2 else i - 1) % lines) for...]
    ppermute x3 -> x5, waiting for transfers between devices: 0.01 us -> 1.05 us  [shifted(): lax.ppermute(value, 'row', [(i, (i + by) % peers) for i in range(peers)])]
  transfers between devices with their start and end apart: 9 -> 9, of which waited for: 4 -> 5; matrix products, arithmetic and copies ran while one was open for 0% -> 0% of each run, Pallas kernels for 30% -> 31%
where the time goes in v5:
time: 35.4 us; the launch traced here: 35.2 us
  Pallas kernels  13.7 us (39%)
  starting transfers between devices  13.6 us (38%)
  waiting for transfers between devices  6.51 us (18%)
  local copies, waits for them, and re-layouts  1.27 us (4%)
    pallas_call x11, Pallas kernels, call(): pl.pallas_call(kernel, out_shape=[jax.ShapeDtypeStruct(*o) for o in outs]...  13.7 us
    ppermute x5, starting transfers between devices, shifted(): lax.ppermute(value, 'row', [(i, (i + by) % peers) for i in range(peers)])  9.27 us
    ppermute x4, waiting for transfers between devices, swapped(): lax.ppermute(value, 'mem', [(i, i ^ by) for i in range(lax.axis_size('mem...  5.46 us
    ppermute x4, starting transfers between devices, swapped(): lax.ppermute(value, 'mem', [(i, i ^ by) for i in range(lax.axis_size('mem...  4.29 us
    unnamed x14, local copies, waits for them, and re-layouts  1.12 us
    ppermute x5, waiting for transfers between devices, shifted(): lax.ppermute(value, 'row', [(i, (i + by) % peers) for i in range(peers)])  1.05 us
  transfers between devices with their start and end apart: 9, of which 5 were waited for; matrix products, arithmetic and copies ran while one was open for 0% of the time, Pallas kernels for 31%

profile of v5, /device:TPU:0, one launch (start us, length us, event | category | flops | bytes accessed | tf_op | source)
XLA Modules:
  0.0 35.2 jit_solution(9613490381275246634)
XLA Ops:
  0.0 0.0 copy-start
  0.0 0.2 shard_map.73
  0.2 1.1 %copy-done = bf16[2,5,16,4096]{3,2,1,0:T(8,128)(2,1)S(1)} copy-done((bf16[2,5,16,4096]{3,2,1,0:T(8,128)(2,1)S(1)}, bf16[2,5,16,4096]{3,2,1,0:T(8,128)(2,1)}, u32[]{:S(2)}) %copy-start) | copy-done | bytes 1310744
  1.3 0.1 fusion
  1.4 0.0 copy-start.1
  1.4 0.0 copy-start.2
  1.4 0.0 copy-start.3
  1.5 0.0 copy-start.4
  1.5 0.2 shard_map.74
  1.7 3.9 %collective-permute-start.1 = (bf16[160,512]{1,0:T(8,128)(2,1)S(1)}, bf16[160,512]{1,0:T(8,128)(2,1)S(1)}, u32[]{:S(2)}, u32[]{:S(2)}) collective-permute-start(bf16[160,512]{1,0:T(8,128)(2,1)S(1)} %get-tuple-element.58), channel_id=1, source_target_pairs={{0,3},{1,0},{2,1},{3,2},{4,7},{5,4},{6,5},{7,6},{8,11},{9,8},{10,9... | collective-permute-start | bytes 491528 | tf_op jit(solution)/shard_map/ppermute | solution.py:536
  5.7 0.0 collective-permute-start
  5.7 0.0 copy-done.1
  5.7 0.0 copy-done.2
  5.7 0.0 copy-done.3
  5.7 0.0 copy-done.4
  5.7 4.7 %shard_map.75 = (bf16[1792,2048]{1,0:T(8,128)(2,1)S(1)}, f32[128,2048]{1,0:T(8,128)S(1)}, f32[128,2048]{1,0:T(8,128)S(1)}, f32[128,2048]{1,0:T(8,128)S(1)}, f32[...) custom-call(bf16[160,4096]{1,0:T(8,128)(2,1)S(1)} %bitcast.14, ...), custom_call_target="tpu_custom_call" | custom-call | flops 1000000000 | bytes 3000000 | tf_op jit(solution)/shard_map/pallas_call | solution.py:547
  10.4 0.0 collective-permute-done.1.got_ref
  10.4 1.2 %shard_map.76 = (bf16[128,2048]{1,0:T(8,128)(2,1)S(1)}, bf16[32,1024]{1,0:T(8,128)(2,1)S(1)}) custom-call(bf16[160,512]{1,0:T(8,128)(2,1)S(1)} %collective-permute-done.1.got_ref, bf16[2,256,256]{2,1,0:T(8,128)(2,1)S(1)} %get-tuple-element.50.spread_ref, bf16[256,128]{1,0:T(8,128)(2,1)S(1)} %get-tuple-element.59.w1_ref, ...), custom_call_target="tpu_custom_call" | custom-call | flops 1000000000 | bytes 3000000 | tf_op jit(solution)/shard_map/pallas_call | solution.py:547
  11.7 2.3 %collective-permute-start.2 = (bf16[32,1024]{1,0:T(8,128)(2,1)S(1)}, bf16[32,1024]{1,0:T(8,128)(2,1)S(1)}, u32[]{:S(2)}, u32[]{:S(2)}) collective-permute-start(bf16[32,1024]{1,0:T(8,128)(2,1)S(1)} %get-tuple-element.71), channel_id=1, source_target_pairs={{0,1},{1,2},{2,3},{3,0},{4,5},{5,6},{6,7},{7,4},{8,9},{9,10},{10,1... | collective-permute-start | bytes 196616 | tf_op jit(solution)/shard_map/ppermute | solution.py:536
  14.0 2.0 %shard_map.77 = (f32[128,2048]{1,0:T(8,128)S(1)}, f32[128,2048]{1,0:T(8,128)S(1)}, f32[2,32,1024]{2,1,0:T(8,128)S(1)}) custom-call(bf16[1792,2048]{1,0:T(8,128)(2,1)S(1)} %get-tuple-element.56.h1_ref, bf16[128,2048]{1,0:T(8,128)(2,1)S(1)} %get-tuple-element.57.h2_mid, bf16[128,2048]{1,0:T(8,128)(2,1)S(1)} %get-tuple-element.63.h2_low, ...), custom_call_target="tpu_custom_call" | custom-call | flops 1000000000 | bytes 3000000 | tf_op jit(solution)/shard_map/pallas_call | solution.py:547
  16.0 0.0 collective-permute-done.got_ref
  16.0 1.8 %shard_map.78 = (f32[2,16,1024]{2,1,0:T(8,128)S(1)}, f32[96,1280]{1,0:T(8,128)S(1)}) custom-call(bf16[240,512]{1,0:T(8,128)(2,1)S(1)} %collective-permute-done.got_ref, bf16[2,256,256]{2,1,0:T(8,128)(2,1)S(1)} %get-tuple-element.50.spread_ref, bf16[512,160]{1,0:T(8,128)(2,1)S(1)} %get-tuple-element.53.w1_ref, f32[128,2048]{1,0:T(8,128)S(1)} %get-tuple-element.54.h_ref, ...), custom_call_target="tpu_custom_call" | custom-call | flops 1000000000 | bytes 3000000 | tf_op jit(solution)/shard_map/pallas_call | solution.py:547
  17.8 0.0 collective-permute-done.2.carry_ref
  17.8 0.4 %shard_map.79 = (bf16[4,144,128]{2,1,0:T(8,128)(2,1)S(1)}, bf16[4,144,128]{2,1,0:T(8,128)(2,1)S(1)}) custom-call(f32[2,16,1024]{2,1,0:T(8,128)S(1)} %get-tuple-element.70.pre_ref, bf16[32,1024]{1,0:T(8,128)(2,1)S(1)} %collective-permute-done.2.carry_ref, bf16[32,32]{1,0:T(8,128)(2,1)S(1)} %get-tuple-element.65.mix_ref, f32[96,1280]{1,0:T(8,128)S(1)} %get-tuple-element.72.tail_ref), custom_call_target="tpu_custom_call" | custom-call | flops 1000000000 | bytes 3000000 | tf_op jit(solution)/shard_map/pallas_call | solution.py:547
  18.1 0.0 collective-permute-start.3
  18.2 1.4 %collective-permute-done.3.got_ref = bf16[4,144,128]{2,1,0:T(8,128)(2,1)S(1)} collective-permute-done((bf16[4,144,128]{2,1,0:T(8,128)(2,1)S(1)}, bf16[4,144,128]{2,1,0:T(8,128)(2,1)S(1)}, u32[]{:S(2)}, u32[]{:S(2)}) %collective-permute-start.3) | collective-permute-done | bytes 147488 | tf_op jit(solution)/shard_map/ppermute | solution.py:540
  19.6 0.0 copy-start.6
  19.6 0.0 copy-start.5
  19.6 2.7 %collective-permute-start.5 = (bf16[144,128]{1,0:T(8,128)(2,1)S(1)}, bf16[144,128]{1,0:T(8,128)(2,1)S(1)}, u32[]{:S(2)}, u32[]{:S(2)}) collective-permute-start(bf16[144,128]{1,0:T(8,128)(2,1)S(1)} %get-tuple-element.77), channel_id=1, source_target_pairs={{0,16},{4,20},{8,24},{12,28},{16,0},{20,4},{24,8},{28,12},{1,17},{... | collective-permute-start | bytes 110600 | tf_op jit(solution)/shard_map/ppermute | solution.py:540
  22.3 1.3 %collective-permute-start.6 = (bf16[144,128]{1,0:T(8,128)(2,1)S(1)}, bf16[144,128]{1,0:T(8,128)(2,1)S(1)}, u32[]{:S(2)}, u32[]{:S(2)}) collective-permute-start(bf16[144,128]{1,0:T(8,128)(2,1)S(1)} %get-tuple-element.78), channel_id=1, source_target_pairs={{0,24},{4,28},{8,16},{12,20},{16,8},{20,12},{24,0},{28,4},{1,25},{... | collective-permute-start | bytes 110600 | tf_op jit(solution)/shard_map/ppermute | solution.py:540
  23.6 0.2 collective-permute-start.4
  23.8 0.0 copy-done.6
  23.9 0.0 copy-done.5
  23.9 1.0 %collective-permute-done.5.refs_1_ = bf16[144,128]{1,0:T(8,128)(2,1)S(1)} collective-permute-done((bf16[144,128]{1,0:T(8,128)(2,1)S(1)}, bf16[144,128]{1,0:T(8,128)(2,1)S(1)}, u32[]{:S(2)}, u32[]{:S(2)}) %collective-permute-start.5) | collective-permute-done | bytes 36896 | tf_op jit(solution)/shard_map/ppermute | solution.py:540
  24.9 3.1 %collective-permute-done.6.refs_2_ = bf16[144,128]{1,0:T(8,128)(2,1)S(1)} collective-permute-done((bf16[144,128]{1,0:T(8,128)(2,1)S(1)}, bf16[144,128]{1,0:T(8,128)(2,1)S(1)}, u32[]{:S(2)}, u32[]{:S(2)}) %collective-permute-start.6) | collective-permute-done | bytes 36896 | tf_op jit(solution)/shard_map/ppermute | solution.py:540
  28.0 0.0 collective-permute-done.4.refs_0_
  28.0 0.3 shard_map.81
  28.3 1.6 %collective-permute-start.7 = (bf16[32,256]{1,0:T(8,128)(2,1)S(1)}, bf16[32,256]{1,0:T(8,128)(2,1)S(1)}, u32[]{:S(2)}, u32[]{:S(2)}) collective-permute-start(bf16[32,256]{1,0:T(8,128)(2,1)S(1)} %get-tuple-element.79), channel_id=1, source_target_pairs={{0,1},{1,2},{2,3},{3,0},{4,5},{5,6},{6,7},{7,4},{8,9},{9,10},{10,1... | collective-permute-start | bytes 49160 | tf_op jit(solution)/shard_map/ppermute | solution.py:536
  29.9 1.4 %collective-permute-start.8 = (bf16[32,256]{1,0:T(8,128)(2,1)S(1)}, bf16[32,256]{1,0:T(8,128)(2,1)S(1)}, u32[]{:S(2)}, u32[]{:S(2)}) collective-permute-start(bf16[32,256]{1,0:T(8,128)(2,1)S(1)} %get-tuple-element.80), channel_id=1, source_target_pairs={{0,3},{1,0},{2,1},{3,2},{4,7},{5,4},{6,5},{7,6},{8,11},{9,8},{10,9... | collective-permute-start | bytes 49160 | tf_op jit(solution)/shard_map/ppermute | solution.py:536
  31.3 1.3 %shard_map.82 = (bf16[2,128,96]{2,1,0:T(8,128)(2,1)S(1)}, bf16[2,256,256]{2,1,0:T(8,128)(2,1)S(1)}, f32[2,128,256]{2,1,0:T(8,128)S(1)}, f32[2,256,128]{2,1,0:T(8...) custom-call(bf16[4,96,256]{2,1,0:T(8,128)(2,1)S(1)} %get-tuple-element.81.ext_ref, ...), custom_call_target="tpu_custom_call" | custom-call | flops 1000000000 | bytes 3000000 | tf_op jit(solution)/shard_map/pallas_call | solution.py:547
  32.6 0.4 %collective-permute-done.7.first_ref = bf16[32,256]{1,0:T(8,128)(2,1)S(1)} collective-permute-done((bf16[32,256]{1,0:T(8,128)(2,1)S(1)}, bf16[32,256]{1,0:T(8,128)(2,1)S(1)}, u32[]{:S(2)}, u32[]{:S(2)}) %collective-permute-start.7) | collective-permute-done | bytes 16416 | tf_op jit(solution)/shard_map/ppermute | solution.py:536
  33.0 0.6 %collective-permute-done.8.second_ref = bf16[32,256]{1,0:T(8,128)(2,1)S(1)} collective-permute-done((bf16[32,256]{1,0:T(8,128)(2,1)S(1)}, bf16[32,256]{1,0:T(8,128)(2,1)S(1)}, u32[]{:S(2)}, u32[]{:S(2)}) %collective-permute-start.8) | collective-permute-done | bytes 16416 | tf_op jit(solution)/shard_map/ppermute | solution.py:536
  33.6 1.6 %shard_map.83 = bf16[16,16,512]{2,1,0:T(8,128)(2,1)} custom-call(bf16[32,256]{1,0:T(8,128)(2,1)S(1)} %collective-permute-done.7.first_ref, bf16[32,256]{1,0:T(8,128)(2,1)S(1)} %collective-permute-done.8.second_ref, bf16[2,128,96]{2,1,0:T(8,128)(2,1)S(1)} %get-tuple-element.84.w_edge, bf16[2,256,256]{2,1,0:T(8,128)(2,1)S(1)} %get-tuple-element.85.w_field, ...), custom_call_target="tpu_custom_call" | custom-call | flops 1000000000 | bytes 3000000 | tf_op jit(solution)/shard_map/pallas_call | solution.py:547
  (3 shorter events, 0.1 us)
Async XLA Ops:
  0.0 1.3 %copy-start = (bf16[2,5,16,4096]{3,2,1,0:T(8,128)(2,1)S(1)}, bf16[2,5,16,4096]{3,2,1,0:T(8,128)(2,1)}, u32[]{:S(2)}) copy-start(bf16[2,5,16,4096]{3,2,1,0:T(8,128)(2,1)} %param.7) | copy-start | bytes 3932164
  1.4 4.2 %copy-start.1 = (bf16[64,64,3,3]{1,0,3,2:T(8,128)(2,1)S(1)}, bf16[64,64,3,3]{1,0,3,2:T(8,128)(2,1)}, u32[]{:S(2)}) copy-start(bf16[64,64,3,3]{1,0,3,2:T(8,128)(2,1)} %param.9) | copy-start | bytes 221188
  1.4 4.2 %copy-start.2 = (bf16[16,64,3,3]{1,0,3,2:T(8,128)(2,1)S(1)}, bf16[16,64,3,3]{1,0,3,2:T(8,128)(2,1)}, u32[]{:S(2)}) copy-start(bf16[16,64,3,3]{1,0,3,2:T(8,128)(2,1)} %param.10) | copy-start | bytes 55300
  1.4 4.2 %copy-start.3 = (bf16[32,256]{1,0:T(8,128)(2,1)S(1)}, bf16[32,256]{1,0:T(8,128)(2,1)}, u32[]{:S(2)}) copy-start(bf16[32,256]{1,0:T(8,128)(2,1)} %mix_ref.1) | copy-start | bytes 49156
  1.5 4.2 %copy-start.4 = (bf16[64,5,3,3]{0,3,2,1:T(4,128)(2,1)S(1)}, bf16[64,5,3,3]{0,3,2,1:T(4,128)(2,1)}, u32[]{:S(2)}) copy-start(bf16[64,5,3,3]{0,3,2,1:T(4,128)(2,1)} %param.8) | copy-start | bytes 17284
  1.7 8.7 %collective-permute-start.1 = (bf16[160,512]{1,0:T(8,128)(2,1)S(1)}, bf16[160,512]{1,0:T(8,128)(2,1)S(1)}, u32[]{:S(2)}, u32[]{:S(2)}) collective-permute-start(bf16[160,512]{1,0:T(8,128)(2,1)S(1)} %get-tuple-element.58), channel_id=1, source_target_pairs={{0,3},{1,0},{2,1},{3,2},{4,7},{5,4},{6,5},{7,6},{8,11},{9,8},{10,9... | collective-permute-start | bytes 491528 | tf_op jit(solution)/shard_map/ppermute | solution.py:536
  5.7 10.4 %collective-permute-start = (bf16[240,512]{1,0:T(8,128)(2,1)S(1)}, bf16[240,512]{1,0:T(8,128)(2,1)S(1)}, u32[]{:S(2)}, u32[]{:S(2)}) collective-permute-start(bf16[240,512]{1,0:T(8,128)(2,1)S(1)} %get-tuple-element.49), channel_id=1, source_target_pairs={{0,1},{1,2},{2,3},{3,0},{4,5},{5,6},{6,7},{7,4},{8,9},{9,10},{10,1... | collective-permute-start | bytes 737288 | tf_op jit(solution)/shard_map/ppermute | solution.py:536
  11.7 6.1 %collective-permute-start.2 = (bf16[32,1024]{1,0:T(8,128)(2,1)S(1)}, bf16[32,1024]{1,0:T(8,128)(2,1)S(1)}, u32[]{:S(2)}, u32[]{:S(2)}) collective-permute-start(bf16[32,1024]{1,0:T(8,128)(2,1)S(1)} %get-tuple-element.71), channel_id=1, source_target_pairs={{0,1},{1,2},{2,3},{3,0},{4,5},{5,6},{6,7},{7,4},{8,9},{9,10},{10,1... | collective-permute-start | bytes 196616 | tf_op jit(solution)/shard_map/ppermute | solution.py:536
  18.1 1.4 %collective-permute-start.3 = (bf16[4,144,128]{2,1,0:T(8,128)(2,1)S(1)}, bf16[4,144,128]{2,1,0:T(8,128)(2,1)S(1)}, u32[]{:S(2)}, u32[]{:S(2)}) collective-permute-start(bf16[4,144,128]{2,1,0:T(8,128)(2,1)S(1)} %get-tuple-element.74), channel_id=1, source_target_pairs={{0,4},{4,0},{8,12},{12,8},{16,20},{20,16},{24,28},{28,24},{1,5},{5... | collective-permute-start | bytes 442376 | tf_op jit(solution)/shard_map/ppermute | solution.py:540
  19.6 4.3 %copy-start.6 = (bf16[16,32,4,4]{1,3,2,0:T(4,128)(2,1)S(1)}, bf16[16,32,4,4]{1,3,2,0:T(4,128)(2,1)}, u32[]{:S(2)}) copy-start(bf16[16,32,4,4]{1,3,2,0:T(4,128)(2,1)} %param.13) | copy-start | bytes 49156
  19.6 4.3 %copy-start.5 = (bf16[32,32,4,4]{1,3,2,0:T(4,128)(2,1)S(1)}, bf16[32,32,4,4]{1,3,2,0:T(4,128)(2,1)}, u32[]{:S(2)}) copy-start(bf16[32,32,4,4]{1,3,2,0:T(4,128)(2,1)} %param.12) | copy-start | bytes 98308
  19.6 5.3 %collective-permute-start.5 = (bf16[144,128]{1,0:T(8,128)(2,1)S(1)}, bf16[144,128]{1,0:T(8,128)(2,1)S(1)}, u32[]{:S(2)}, u32[]{:S(2)}) collective-permute-start(bf16[144,128]{1,0:T(8,128)(2,1)S(1)} %get-tuple-element.77), channel_id=1, source_target_pairs={{0,16},{4,20},{8,24},{12,28},{16,0},{20,4},{24,8},{28,12},{1,17},{... | collective-permute-start | bytes 110600 | tf_op jit(solution)/shard_map/ppermute | solution.py:540
  22.3 5.8 %collective-permute-start.6 = (bf16[144,128]{1,0:T(8,128)(2,1)S(1)}, bf16[144,128]{1,0:T(8,128)(2,1)S(1)}, u32[]{:S(2)}, u32[]{:S(2)}) collective-permute-start(bf16[144,128]{1,0:T(8,128)(2,1)S(1)} %get-tuple-element.78), channel_id=1, source_target_pairs={{0,24},{4,28},{8,16},{12,20},{16,8},{20,12},{24,0},{28,4},{1,25},{... | collective-permute-start | bytes 110600 | tf_op jit(solution)/shard_map/ppermute | solution.py:540
  23.6 4.4 %collective-permute-start.4 = (bf16[144,128]{1,0:T(8,128)(2,1)S(1)}, bf16[144,128]{1,0:T(8,128)(2,1)S(1)}, u32[]{:S(2)}, u32[]{:S(2)}) collective-permute-start(bf16[144,128]{1,0:T(8,128)(2,1)S(1)} %get-tuple-element.76), channel_id=1, source_target_pairs={{0,8},{4,12},{8,0},{12,4},{16,24},{20,28},{24,16},{28,20},{1,9},{5... | collective-permute-start | bytes 110600 | tf_op jit(solution)/shard_map/ppermute | solution.py:540
  28.3 4.7 %collective-permute-start.7 = (bf16[32,256]{1,0:T(8,128)(2,1)S(1)}, bf16[32,256]{1,0:T(8,128)(2,1)S(1)}, u32[]{:S(2)}, u32[]{:S(2)}) collective-permute-start(bf16[32,256]{1,0:T(8,128)(2,1)S(1)} %get-tuple-element.79), channel_id=1, source_target_pairs={{0,1},{1,2},{2,3},{3,0},{4,5},{5,6},{6,7},{7,4},{8,9},{9,10},{10,1... | collective-permute-start | bytes 49160 | tf_op jit(solution)/shard_map/ppermute | solution.py:536
  29.9 3.7 %collective-permute-start.8 = (bf16[32,256]{1,0:T(8,128)(2,1)S(1)}, bf16[32,256]{1,0:T(8,128)(2,1)S(1)}, u32[]{:S(2)}, u32[]{:S(2)}) collective-permute-start(bf16[32,256]{1,0:T(8,128)(2,1)S(1)} %get-tuple-element.80), channel_id=1, source_target_pairs={{0,3},{1,0},{2,1},{3,2},{4,7},{5,4},{6,5},{7,6},{8,11},{9,8},{10,9... | collective-permute-start | bytes 49160 | tf_op jit(solution)/shard_map/ppermute | solution.py:536

commit v6 on v5

--- a/solution.py
+++ b/solution.py
@@ -128,15 +128,13 @@
             below_ref[m, pc] = one_hot((lane == at) & (dr >= 1))
 
 
-def pack_kernel(members, channels, rows, xa_ref, xb_ref, _, down_ref, up_ref, d_scr, u_scr):
-    wide = xa_ref.shape[1]
+def pack_kernel(members, channels, rows, x_ref, _, down_ref, up_ref, d_scr, u_scr):
+    wide = x_ref.shape[1]
     lanes = down_ref.shape[1]
-    cut = xa_ref.shape[0]
     nd, nu = members * channels * UP, members * channels * DOWN
     for t in range(wide // lanes):
         for g in range(members * channels):
-            ref, at = (xa_ref, g * rows) if g * rows < cut else (xb_ref, g * rows - cut)
-            block = ref[at : at + rows, t * lanes : (t + 1) * lanes].astype(F32)
+            block = x_ref[g * rows : (g + 1) * rows, t * lanes : (t + 1) * lanes].astype(F32)
             d_scr[t * nd + g * UP : t * nd + (g + 1) * UP, :] = block[rows - UP : rows]
             u_scr[t * nu + g * DOWN : t * nu + (g + 1) * DOWN, :] = block[0:DOWN]
     down_ref[...] = d_scr[...].astype(BF)
@@ -364,20 +362,20 @@
 
 
 def latent_kernel(nb, quarter, own_ref, *refs):
-    ext_ref, first_ref, second_ref = refs[-3:]
+    line_ref, first_ref, second_ref = refs[-3:]
     total = own_ref[...]
     for ref in refs[:-3]:
         total = total + ref[...].astype(F32)
     latent = silu_of_half(0.5 * total)
     tall = quarter * 32
     turned = jnp.concatenate([latent[tall : tall + 16], jnp.zeros((112, 128), F32)], axis=0).T
-    ext = ext_ref.shape[2]
+    ext = line_ref.shape[1]
     lines = []
     for r in range(quarter):
         rows = slice(r * 32, (r + 1) * 32)
         line = [latent[rows, 0:nb], turned[rows, 1:2], jnp.zeros((32, ext - nb - 2), F32), turned[rows, 0:1]]
         lines.append(jnp.concatenate(line, axis=1))
-        put_latent(ext_ref, r, lines[-1])
+        line_ref[rows, :] = lines[-1].astype(BF)
     first_ref[...] = lines[-1].astype(BF)
     second_ref[...] = lines[0].astype(BF)
 
@@ -448,7 +446,7 @@
 
 
 def decoder_inner(
-    nb, ext_ref, d1_ref, d2_ref,
+    nb, line_ref, d1_ref, d2_ref,
     w_edge, w_field, up_part, field_part, join_ref, turn_ref, part_ref, wd1, wd2, l_ref, u_ref, g_ref,
 ):
     wd1[...] = jnp.zeros_like(wd1)
@@ -462,7 +460,7 @@
                 at = pr * 4 + 2 * q + pc
                 to = rr * 4 + q + cc
                 wd2[at * 16 : (at + 1) * 16, to * 32 : (to + 1) * 32] = d2_ref[tr * 4 + tc]
-    rows, _, wide = ext_ref.shape
+    rows, wide = line_ref.shape[0] // 32, line_ref.shape[1]
     frm = lax.broadcasted_iota(jnp.int32, join_ref.shape, 0)
     to = lax.broadcasted_iota(jnp.int32, join_ref.shape, 1)
     place = frm // nb
@@ -472,7 +470,8 @@
 
     l_ref[0] = jnp.zeros_like(l_ref[0])
     l_ref[1] = jnp.zeros_like(l_ref[0])
-    l_ref[2 : rows + 2] = ext_ref[...]
+    for r in range(rows):
+        put_latent(l_ref, r + 2, line_ref[r * 32 : r * 32 + 32, :].astype(F32))
     l_ref[rows + 2] = jnp.zeros_like(l_ref[0])
     u_ref[...] = jnp.zeros_like(u_ref)
     keep_even, keep_odd = column_keeps(nb, wide)
@@ -486,8 +485,8 @@
     w_edge[0, 64:128, :] = wd1[0:64, 0:96]
     w_edge[1, 0:64, :] = wd1[64:128, 192:288]
     w_edge[1, 64:128, :] = wd1[0:64, 96:192]
-    up_part[0] = dot(w_edge[1], ext_ref[0])
-    up_part[1] = dot(w_edge[0], ext_ref[rows - 1])
+    up_part[0] = dot(w_edge[1], l_ref[2])
+    up_part[1] = dot(w_edge[0], l_ref[rows + 1])
 
     def known(taps, first, count):
         return by_phase(dot(wd2[:, taps : taps + 128 * count], u_ref[(first + 1) * 128 : (first + 1 + count) * 128, :]))
@@ -569,7 +568,6 @@
     total = padded(5 * per[0], 16), padded(5 * per[1], 16)
     pack = functools.partial(pack_kernel, count, channels, rows)
     sizes = [(nd * chunks, lanes), (nu * chunks, lanes)]
-    cut = (count * channels) // 2 * rows
     spreads, own, above, below = call(
         functools.partial(prepare_kernel, count, channels, per),
         [
@@ -579,8 +577,9 @@
             ((count, 2, 48, total[1]), BF),
         ],
         [],
-    )
-    down, up = call(pack, [(s, BF) for s in sizes], [(s, F32) for s in sizes], x[:cut], x[cut:], below, mb=16, us=20)
+        us=20,
+    )
+    down, up = call(pack, [(s, BF) for s in sizes], [(s, F32) for s in sizes], x, below, mb=16, us=20)
     up = shifted(up, -1)
     down = shifted(down, 1)
 
@@ -649,7 +648,7 @@
     ext = padded(nb + 2, 128)
     latent, first, second = call(
         functools.partial(latent_kernel, nb, quarter),
-        [((quarter, 96, ext), BF), ((32, ext), BF), ((32, ext), BF)],
+        [((quarter * 32, ext), BF), ((32, ext), BF), ((32, ext), BF)],
         [],
         mine, *[moved[k] for k in range(slots - 1)],
     )

time: 35.4 us -> 35.2 us (level)
  no operation moved by 1% of the time
where the time goes in v6:
time: 35.2 us; the launch traced here: 35 us
  Pallas kernels  13.7 us (39%)
  starting transfers between devices  13.6 us (39%)
  waiting for transfers between devices  6.49 us (18%)
  local copies, waits for them, and re-layouts  1.17 us (3%)
    pallas_call x11, Pallas kernels, call(): pl.pallas_call(kernel, out_shape=[jax.ShapeDtypeStruct(*o) for o in outs]...  13.7 us
    ppermute x5, starting transfers between devices, shifted(): lax.ppermute(value, 'row', [(i, (i + by) % peers) for i in range(peers)])  9.28 us
    ppermute x4, waiting for transfers between devices, swapped(): lax.ppermute(value, 'mem', [(i, i ^ by) for i in range(lax.axis_size('mem...  5.46 us
    ppermute x4, starting transfers between devices, swapped(): lax.ppermute(value, 'mem', [(i, i ^ by) for i in range(lax.axis_size('mem...  4.3 us
    unnamed x14, local copies, waits for them, and re-layouts  1.11 us
    ppermute x5, waiting for transfers between devices, shifted(): lax.ppermute(value, 'row', [(i, (i + by) % peers) for i in range(peers)])  1.03 us
  transfers between devices with their start and end apart: 9, of which 5 were waited for; matrix products, arithmetic and copies ran while one was open for 0% of the time, Pallas kernels for 31%

profile of v6, /device:TPU:0, one launch (start us, length us, event | category | flops | bytes accessed | tf_op | source)
XLA Modules:
  0.0 35.0 jit_solution(5958858156015783054)
XLA Ops:
  0.0 0.0 copy-start
  0.0 0.2 shard_map.73
  0.2 1.1 %copy-done = bf16[2,5,16,4096]{3,2,1,0:T(8,128)(2,1)S(1)} copy-done((bf16[2,5,16,4096]{3,2,1,0:T(8,128)(2,1)S(1)}, bf16[2,5,16,4096]{3,2,1,0:T(8,128)(2,1)}, u32[]{:S(2)}) %copy-start) | copy-done | bytes 1310744
  1.3 0.0 copy-start.1
  1.3 0.0 copy-start.2
  1.3 0.0 copy-start.3
  1.3 0.0 copy-start.4
  1.3 0.2 shard_map.74
  1.6 3.9 %collective-permute-start.1 = (bf16[160,512]{1,0:T(8,128)(2,1)S(1)}, bf16[160,512]{1,0:T(8,128)(2,1)S(1)}, u32[]{:S(2)}, u32[]{:S(2)}) collective-permute-start(bf16[160,512]{1,0:T(8,128)(2,1)S(1)} %get-tuple-element.58), channel_id=1, source_target_pairs={{0,3},{1,0},{2,1},{3,2},{4,7},{5,4},{6,5},{7,6},{8,11},{9,8},{10,9... | collective-permute-start | bytes 491528 | tf_op jit(solution)/shard_map/ppermute | solution.py:535
  5.5 0.0 collective-permute-start
  5.5 0.0 copy-done.1
  5.5 0.0 copy-done.2
  5.5 0.0 copy-done.3
  5.5 0.0 copy-done.4
  5.6 4.7 %shard_map.75 = (bf16[1792,2048]{1,0:T(8,128)(2,1)S(1)}, f32[128,2048]{1,0:T(8,128)S(1)}, f32[128,2048]{1,0:T(8,128)S(1)}, f32[128,2048]{1,0:T(8,128)S(1)}, f32[...) custom-call(bf16[160,4096]{1,0:T(8,128)(2,1)S(1)} %bitcast.15, ...), custom_call_target="tpu_custom_call" | custom-call | flops 1000000000 | bytes 3000000 | tf_op jit(solution)/shard_map/pallas_call | solution.py:546
  10.2 0.0 collective-permute-done.1.got_ref
  10.2 1.2 %shard_map.76 = (bf16[128,2048]{1,0:T(8,128)(2,1)S(1)}, bf16[32,1024]{1,0:T(8,128)(2,1)S(1)}) custom-call(bf16[160,512]{1,0:T(8,128)(2,1)S(1)} %collective-permute-done.1.got_ref, bf16[2,256,256]{2,1,0:T(8,128)(2,1)S(1)} %get-tuple-element.50.spread_ref, bf16[256,128]{1,0:T(8,128)(2,1)S(1)} %get-tuple-element.59.w1_ref, ...), custom_call_target="tpu_custom_call" | custom-call | flops 1000000000 | bytes 3000000 | tf_op jit(solution)/shard_map/pallas_call | solution.py:546
  11.5 2.3 %collective-permute-start.2 = (bf16[32,1024]{1,0:T(8,128)(2,1)S(1)}, bf16[32,1024]{1,0:T(8,128)(2,1)S(1)}, u32[]{:S(2)}, u32[]{:S(2)}) collective-permute-start(bf16[32,1024]{1,0:T(8,128)(2,1)S(1)} %get-tuple-element.71), channel_id=1, source_target_pairs={{0,1},{1,2},{2,3},{3,0},{4,5},{5,6},{6,7},{7,4},{8,9},{9,10},{10,1... | collective-permute-start | bytes 196616 | tf_op jit(solution)/shard_map/ppermute | solution.py:535
  13.8 2.0 %shard_map.77 = (f32[128,2048]{1,0:T(8,128)S(1)}, f32[128,2048]{1,0:T(8,128)S(1)}, f32[2,32,1024]{2,1,0:T(8,128)S(1)}) custom-call(bf16[1792,2048]{1,0:T(8,128)(2,1)S(1)} %get-tuple-element.56.h1_ref, bf16[128,2048]{1,0:T(8,128)(2,1)S(1)} %get-tuple-element.57.h2_mid, bf16[128,2048]{1,0:T(8,128)(2,1)S(1)} %get-tuple-element.63.h2_low, ...), custom_call_target="tpu_custom_call" | custom-call | flops 1000000000 | bytes 3000000 | tf_op jit(solution)/shard_map/pallas_call | solution.py:546
  15.9 0.0 copy-start.6
  15.9 0.0 copy-start.5
  15.9 0.0 collective-permute-done.got_ref
  15.9 1.8 %shard_map.78 = (f32[2,16,1024]{2,1,0:T(8,128)S(1)}, f32[96,1280]{1,0:T(8,128)S(1)}) custom-call(bf16[240,512]{1,0:T(8,128)(2,1)S(1)} %collective-permute-done.got_ref, bf16[2,256,256]{2,1,0:T(8,128)(2,1)S(1)} %get-tuple-element.50.spread_ref, bf16[512,160]{1,0:T(8,128)(2,1)S(1)} %get-tuple-element.53.w1_ref, f32[128,2048]{1,0:T(8,128)S(1)} %get-tuple-element.54.h_ref, ...), custom_call_target="tpu_custom_call" | custom-call | flops 1000000000 | bytes 3000000 | tf_op jit(solution)/shard_map/pallas_call | solution.py:546
  17.7 0.0 collective-permute-done.2.carry_ref
  17.7 0.4 %shard_map.79 = (bf16[4,144,128]{2,1,0:T(8,128)(2,1)S(1)}, bf16[4,144,128]{2,1,0:T(8,128)(2,1)S(1)}) custom-call(f32[2,16,1024]{2,1,0:T(8,128)S(1)} %get-tuple-element.70.pre_ref, bf16[32,1024]{1,0:T(8,128)(2,1)S(1)} %collective-permute-done.2.carry_ref, bf16[32,32]{1,0:T(8,128)(2,1)S(1)} %get-tuple-element.65.mix_ref, f32[96,1280]{1,0:T(8,128)S(1)} %get-tuple-element.72.tail_ref), custom_call_target="tpu_custom_call" | custom-call | flops 1000000000 | bytes 3000000 | tf_op jit(solution)/shard_map/pallas_call | solution.py:546
  18.0 0.0 collective-permute-start.3
  18.1 1.4 %collective-permute-done.3.got_ref = bf16[4,144,128]{2,1,0:T(8,128)(2,1)S(1)} collective-permute-done((bf16[4,144,128]{2,1,0:T(8,128)(2,1)S(1)}, bf16[4,144,128]{2,1,0:T(8,128)(2,1)S(1)}, u32[]{:S(2)}, u32[]{:S(2)}) %collective-permute-start.3) | collective-permute-done | bytes 147488 | tf_op jit(solution)/shard_map/ppermute | solution.py:539
  19.5 2.7 %collective-permute-start.5 = (bf16[144,128]{1,0:T(8,128)(2,1)S(1)}, bf16[144,128]{1,0:T(8,128)(2,1)S(1)}, u32[]{:S(2)}, u32[]{:S(2)}) collective-permute-start(bf16[144,128]{1,0:T(8,128)(2,1)S(1)} %get-tuple-element.77), channel_id=1, source_target_pairs={{0,16},{4,20},{8,24},{12,28},{16,0},{20,4},{24,8},{28,12},{1,17},{... | collective-permute-start | bytes 110600 | tf_op jit(solution)/shard_map/ppermute | solution.py:539
  22.1 1.3 %collective-permute-start.6 = (bf16[144,128]{1,0:T(8,128)(2,1)S(1)}, bf16[144,128]{1,0:T(8,128)(2,1)S(1)}, u32[]{:S(2)}, u32[]{:S(2)}) collective-permute-start(bf16[144,128]{1,0:T(8,128)(2,1)S(1)} %get-tuple-element.78), channel_id=1, source_target_pairs={{0,24},{4,28},{8,16},{12,20},{16,8},{20,12},{24,0},{28,4},{1,25},{... | collective-permute-start | bytes 110600 | tf_op jit(solution)/shard_map/ppermute | solution.py:539
  23.5 0.3 collective-permute-start.4
  23.7 0.0 copy-done.6
  23.8 0.0 copy-done.5
  23.8 1.0 %collective-permute-done.5.refs_1_ = bf16[144,128]{1,0:T(8,128)(2,1)S(1)} collective-permute-done((bf16[144,128]{1,0:T(8,128)(2,1)S(1)}, bf16[144,128]{1,0:T(8,128)(2,1)S(1)}, u32[]{:S(2)}, u32[]{:S(2)}) %collective-permute-start.5) | collective-permute-done | bytes 36896 | tf_op jit(solution)/shard_map/ppermute | solution.py:539
  24.8 3.1 %collective-permute-done.6.refs_2_ = bf16[144,128]{1,0:T(8,128)(2,1)S(1)} collective-permute-done((bf16[144,128]{1,0:T(8,128)(2,1)S(1)}, bf16[144,128]{1,0:T(8,128)(2,1)S(1)}, u32[]{:S(2)}, u32[]{:S(2)}) %collective-permute-start.6) | collective-permute-done | bytes 36896 | tf_op jit(solution)/shard_map/ppermute | solution.py:539
  27.9 0.0 collective-permute-done.4.refs_0_
  27.9 0.2 shard_map.81
  28.1 1.6 %collective-permute-start.7 = (bf16[32,256]{1,0:T(8,128)(2,1)S(1)}, bf16[32,256]{1,0:T(8,128)(2,1)S(1)}, u32[]{:S(2)}, u32[]{:S(2)}) collective-permute-start(bf16[32,256]{1,0:T(8,128)(2,1)S(1)} %get-tuple-element.79), channel_id=1, source_target_pairs={{0,1},{1,2},{2,3},{3,0},{4,5},{5,6},{6,7},{7,4},{8,9},{9,10},{10,1... | collective-permute-start | bytes 49160 | tf_op jit(solution)/shard_map/ppermute | solution.py:535
  29.7 1.4 %collective-permute-start.8 = (bf16[32,256]{1,0:T(8,128)(2,1)S(1)}, bf16[32,256]{1,0:T(8,128)(2,1)S(1)}, u32[]{:S(2)}, u32[]{:S(2)}) collective-permute-start(bf16[32,256]{1,0:T(8,128)(2,1)S(1)} %get-tuple-element.80), channel_id=1, source_target_pairs={{0,3},{1,0},{2,1},{3,2},{4,7},{5,4},{6,5},{7,6},{8,11},{9,8},{10,9... | collective-permute-start | bytes 49160 | tf_op jit(solution)/shard_map/ppermute | solution.py:535
  31.1 1.3 %shard_map.82 = (bf16[2,128,96]{2,1,0:T(8,128)(2,1)S(1)}, bf16[2,256,256]{2,1,0:T(8,128)(2,1)S(1)}, f32[2,128,256]{2,1,0:T(8,128)S(1)}, f32[2,256,128]{2,1,0:T(8...) custom-call(bf16[128,256]{1,0:T(8,128)(2,1)S(1)} %get-tuple-element.81.line_ref, ...), custom_call_target="tpu_custom_call" | custom-call | flops 1000000000 | bytes 3000000 | tf_op jit(solution)/shard_map/pallas_call | solution.py:546
  32.4 0.4 %collective-permute-done.7.first_ref = bf16[32,256]{1,0:T(8,128)(2,1)S(1)} collective-permute-done((bf16[32,256]{1,0:T(8,128)(2,1)S(1)}, bf16[32,256]{1,0:T(8,128)(2,1)S(1)}, u32[]{:S(2)}, u32[]{:S(2)}) %collective-permute-start.7) | collective-permute-done | bytes 16416 | tf_op jit(solution)/shard_map/ppermute | solution.py:535
  32.8 0.6 %collective-permute-done.8.second_ref = bf16[32,256]{1,0:T(8,128)(2,1)S(1)} collective-permute-done((bf16[32,256]{1,0:T(8,128)(2,1)S(1)}, bf16[32,256]{1,0:T(8,128)(2,1)S(1)}, u32[]{:S(2)}, u32[]{:S(2)}) %collective-permute-start.8) | collective-permute-done | bytes 16416 | tf_op jit(solution)/shard_map/ppermute | solution.py:535
  33.4 1.6 %shard_map.83 = bf16[16,16,512]{2,1,0:T(8,128)(2,1)} custom-call(bf16[32,256]{1,0:T(8,128)(2,1)S(1)} %collective-permute-done.7.first_ref, bf16[32,256]{1,0:T(8,128)(2,1)S(1)} %collective-permute-done.8.second_ref, bf16[2,128,96]{2,1,0:T(8,128)(2,1)S(1)} %get-tuple-element.84.w_edge, bf16[2,256,256]{2,1,0:T(8,128)(2,1)S(1)} %get-tuple-element.85.w_field, ...), custom_call_target="tpu_custom_call" | custom-call | flops 1000000000 | bytes 3000000 | tf_op jit(solution)/shard_map/pallas_call | solution.py:546
  (3 shorter events, 0.1 us)
Async XLA Ops:
  0.0 1.3 %copy-start = (bf16[2,5,16,4096]{3,2,1,0:T(8,128)(2,1)S(1)}, bf16[2,5,16,4096]{3,2,1,0:T(8,128)(2,1)}, u32[]{:S(2)}) copy-start(bf16[2,5,16,4096]{3,2,1,0:T(8,128)(2,1)} %param.7) | copy-start | bytes 3932164
  1.3 4.2 %copy-start.1 = (bf16[64,64,3,3]{1,0,3,2:T(8,128)(2,1)S(1)}, bf16[64,64,3,3]{1,0,3,2:T(8,128)(2,1)}, u32[]{:S(2)}) copy-start(bf16[64,64,3,3]{1,0,3,2:T(8,128)(2,1)} %param.9) | copy-start | bytes 221188
  1.3 4.2 %copy-start.2 = (bf16[16,64,3,3]{1,0,3,2:T(8,128)(2,1)S(1)}, bf16[16,64,3,3]{1,0,3,2:T(8,128)(2,1)}, u32[]{:S(2)}) copy-start(bf16[16,64,3,3]{1,0,3,2:T(8,128)(2,1)} %param.10) | copy-start | bytes 55300
  1.3 4.2 %copy-start.3 = (bf16[32,256]{1,0:T(8,128)(2,1)S(1)}, bf16[32,256]{1,0:T(8,128)(2,1)}, u32[]{:S(2)}) copy-start(bf16[32,256]{1,0:T(8,128)(2,1)} %mix_ref.1) | copy-start | bytes 49156
  1.3 4.2 %copy-start.4 = (bf16[64,5,3,3]{0,3,2,1:T(4,128)(2,1)S(1)}, bf16[64,5,3,3]{0,3,2,1:T(4,128)(2,1)}, u32[]{:S(2)}) copy-start(bf16[64,5,3,3]{0,3,2,1:T(4,128)(2,1)} %param.8) | copy-start | bytes 17284
  1.6 8.7 %collective-permute-start.1 = (bf16[160,512]{1,0:T(8,128)(2,1)S(1)}, bf16[160,512]{1,0:T(8,128)(2,1)S(1)}, u32[]{:S(2)}, u32[]{:S(2)}) collective-permute-start(bf16[160,512]{1,0:T(8,128)(2,1)S(1)} %get-tuple-element.58), channel_id=1, source_target_pairs={{0,3},{1,0},{2,1},{3,2},{4,7},{5,4},{6,5},{7,6},{8,11},{9,8},{10,9... | collective-permute-start | bytes 491528 | tf_op jit(solution)/shard_map/ppermute | solution.py:535
  5.5 10.4 %collective-permute-start = (bf16[240,512]{1,0:T(8,128)(2,1)S(1)}, bf16[240,512]{1,0:T(8,128)(2,1)S(1)}, u32[]{:S(2)}, u32[]{:S(2)}) collective-permute-start(bf16[240,512]{1,0:T(8,128)(2,1)S(1)} %get-tuple-element.49), channel_id=1, source_target_pairs={{0,1},{1,2},{2,3},{3,0},{4,5},{5,6},{6,7},{7,4},{8,9},{9,10},{10,1... | collective-permute-start | bytes 737288 | tf_op jit(solution)/shard_map/ppermute | solution.py:535
  11.5 6.2 %collective-permute-start.2 = (bf16[32,1024]{1,0:T(8,128)(2,1)S(1)}, bf16[32,1024]{1,0:T(8,128)(2,1)S(1)}, u32[]{:S(2)}, u32[]{:S(2)}) collective-permute-start(bf16[32,1024]{1,0:T(8,128)(2,1)S(1)} %get-tuple-element.71), channel_id=1, source_target_pairs={{0,1},{1,2},{2,3},{3,0},{4,5},{5,6},{6,7},{7,4},{8,9},{9,10},{10,1... | collective-permute-start | bytes 196616 | tf_op jit(solution)/shard_map/ppermute | solution.py:535
  15.9 7.9 %copy-start.6 = (bf16[16,32,4,4]{1,3,2,0:T(4,128)(2,1)S(1)}, bf16[16,32,4,4]{1,3,2,0:T(4,128)(2,1)}, u32[]{:S(2)}) copy-start(bf16[16,32,4,4]{1,3,2,0:T(4,128)(2,1)} %param.13) | copy-start | bytes 49156
  15.9 7.9 %copy-start.5 = (bf16[32,32,4,4]{1,3,2,0:T(4,128)(2,1)S(1)}, bf16[32,32,4,4]{1,3,2,0:T(4,128)(2,1)}, u32[]{:S(2)}) copy-start(bf16[32,32,4,4]{1,3,2,0:T(4,128)(2,1)} %param.12) | copy-start | bytes 98308
  18.0 1.4 %collective-permute-start.3 = (bf16[4,144,128]{2,1,0:T(8,128)(2,1)S(1)}, bf16[4,144,128]{2,1,0:T(8,128)(2,1)S(1)}, u32[]{:S(2)}, u32[]{:S(2)}) collective-permute-start(bf16[4,144,128]{2,1,0:T(8,128)(2,1)S(1)} %get-tuple-element.74), channel_id=1, source_target_pairs={{0,4},{4,0},{8,12},{12,8},{16,20},{20,16},{24,28},{28,24},{1,5},{5... | collective-permute-start | bytes 442376 | tf_op jit(solution)/shard_map/ppermute | solution.py:539
  19.5 5.3 %collective-permute-start.5 = (bf16[144,128]{1,0:T(8,128)(2,1)S(1)}, bf16[144,128]{1,0:T(8,128)(2,1)S(1)}, u32[]{:S(2)}, u32[]{:S(2)}) collective-permute-start(bf16[144,128]{1,0:T(8,128)(2,1)S(1)} %get-tuple-element.77), channel_id=1, source_target_pairs={{0,16},{4,20},{8,24},{12,28},{16,0},{20,4},{24,8},{28,12},{1,17},{... | collective-permute-start | bytes 110600 | tf_op jit(solution)/shard_map/ppermute | solution.py:539
  22.1 5.8 %collective-permute-start.6 = (bf16[144,128]{1,0:T(8,128)(2,1)S(1)}, bf16[144,128]{1,0:T(8,128)(2,1)S(1)}, u32[]{:S(2)}, u32[]{:S(2)}) collective-permute-start(bf16[144,128]{1,0:T(8,128)(2,1)S(1)} %get-tuple-element.78), channel_id=1, source_target_pairs={{0,24},{4,28},{8,16},{12,20},{16,8},{20,12},{24,0},{28,4},{1,25},{... | collective-permute-start | bytes 110600 | tf_op jit(solution)/shard_map/ppermute | solution.py:539
  23.5 4.4 %collective-permute-start.4 = (bf16[144,128]{1,0:T(8,128)(2,1)S(1)}, bf16[144,128]{1,0:T(8,128)(2,1)S(1)}, u32[]{:S(2)}, u32[]{:S(2)}) collective-permute-start(bf16[144,128]{1,0:T(8,128)(2,1)S(1)} %get-tuple-element.76), channel_id=1, source_target_pairs={{0,8},{4,12},{8,0},{12,4},{16,24},{20,28},{24,16},{28,20},{1,9},{5... | collective-permute-start | bytes 110600 | tf_op jit(solution)/shard_map/ppermute | solution.py:539
  28.1 4.7 %collective-permute-start.7 = (bf16[32,256]{1,0:T(8,128)(2,1)S(1)}, bf16[32,256]{1,0:T(8,128)(2,1)S(1)}, u32[]{:S(2)}, u32[]{:S(2)}) collective-permute-start(bf16[32,256]{1,0:T(8,128)(2,1)S(1)} %get-tuple-element.79), channel_id=1, source_target_pairs={{0,1},{1,2},{2,3},{3,0},{4,5},{5,6},{6,7},{7,4},{8,9},{9,10},{10,1... | collective-permute-start | bytes 49160 | tf_op jit(solution)/shard_map/ppermute | solution.py:535
  29.7 3.7 %collective-permute-start.8 = (bf16[32,256]{1,0:T(8,128)(2,1)S(1)}, bf16[32,256]{1,0:T(8,128)(2,1)S(1)}, u32[]{:S(2)}, u32[]{:S(2)}) collective-permute-start(bf16[32,256]{1,0:T(8,128)(2,1)S(1)} %get-tuple-element.80), channel_id=1, source_target_pairs={{0,3},{1,0},{2,1},{3,2},{4,7},{5,4},{6,5},{7,6},{8,11},{9,8},{10,9... | collective-permute-start | bytes 49160 | tf_op jit(solution)/shard_map/ppermute | solution.py:535

commit v7 on v6

--- a/solution.py
+++ b/solution.py
@@ -11,6 +11,7 @@
 BF = jnp.bfloat16
 F32 = jnp.float32
 CH_BOT = 16
+EDGES = 8
 UP = 3
 DOWN = 2
 TRANSPOSED = [(p, i, 2 * i - p) for p in range(2) for i in range(3) if 0 <= 2 * i - p < 4]
@@ -59,6 +60,13 @@
     ref[at * 256 + 128 : at * 256 + 192, lanes] = odd
     ref[at * 256 : at * 256 + 64, lanes] = shift_right(odd)
     ref[at * 256 + 192 : at * 256 + 256, lanes] = shift_left(even)
+
+
+def put_line(ref, at, line):
+    rows, cols = slice(at, at + 32), line.shape[1]
+    ref[rows, 0:128] = jnp.zeros((32, 128), F32)
+    ref[rows, 128 : 128 + cols] = line
+    ref[rows, 128 + cols : 256 + cols] = jnp.zeros((32, 128), F32)
 
 
 def bottleneck(w):
@@ -270,13 +278,13 @@
         w = v[0:32, n * wide : (n + 1) * wide] + carry
         carry = v[32:64, n * wide : (n + 1) * wide]
         parts = [bottleneck(w[:, m * cols : (m + 1) * cols]) for m in range(members)]
-        mixed_ref[n] = dot(mix_ref[...], jnp.concatenate(parts, axis=0))
+        put_line(mixed_ref, n * 32, dot(mix_ref[...], jnp.concatenate(parts, axis=0)))
 
 
 def top_kernel(
     members, channels, per,
-    got_ref, spread_ref, w1_ref, h_ref, w2_ref, a_first, a_second, w3_ref, v_ref, mix_ref, mid_ref,
-    pre_ref, tail_ref, y_ref, h1_ref, h2_ref,
+    got_ref, spread_ref, w1_ref, h_ref, w2_ref, a_first, a_second, w3_ref, v_ref, mix_ref,
+    pre_ref, second_ref, y_ref, h1_ref, h2_ref,
 ):
     source = (got_ref[...].astype(F32) * is_row(0)).astype(BF)
     y = place_halo(source, spread_ref, y_ref, members * channels * UP, per)
@@ -294,32 +302,24 @@
         lanes = slice(m * cols, (m + 1) * cols)
         pre_ref[m] = v[0:16, lanes] + shift_right(v[16:32, lanes])
         second.append(bottleneck(v[32:64, lanes] + v_ref[:, lanes]))
-    tall = tail_ref.shape[0]
-    tail_ref[:, 0:128] = jnp.zeros((tall, 128), F32)
-    tail_ref[:, 128 + cols : 256 + cols] = jnp.zeros((tall, 128), F32)
-    inside = slice(128, 128 + cols)
-    tail_ref[0:32, inside] = dot(mix_ref[...], jnp.concatenate(second, axis=0))
-    for r in range(mid_ref.shape[0]):
-        tail_ref[(r + 1) * 32 : (r + 2) * 32, inside] = mid_ref[r]
-
-
-def chunk_kernel(nb, pre_ref, carry_ref, mix_ref, tail_ref, keep_ref, send_ref, head_ref):
-    members, _, cols = pre_ref.shape
+    put_line(second_ref, 0, dot(mix_ref[...], jnp.concatenate(second, axis=0)))
+
+
+def chunk_kernel(nb, pre_ref, carry_ref, mix_ref, second_ref, tail_ref, keep_ref, send_ref, head_ref):
+    members = pre_ref.shape[0]
     carry = carry_ref[...].astype(F32) * is_row(0)
     first = [
         silu_of_half(pre_ref[m] + carry[m * 16 : m * 16 + 16]).astype(BF) for m in range(members)
     ]
-    head_ref[:, 0:128] = jnp.zeros((32, 128), F32)
-    head_ref[:, 128 + cols : 256 + cols] = jnp.zeros((32, 128), F32)
-    head_ref[:, 128 : 128 + cols] = dot(mix_ref[...], jnp.concatenate(first, axis=0))
+    put_line(head_ref, 0, dot(mix_ref[...], jnp.concatenate(first, axis=0)))
 
     me = lax.axis_index("mem")
     slots = lax.axis_size("mem") // 2
-    tall = 32 + tail_ref.shape[0]
+    tall = 64 + tail_ref.shape[0]
 
     def tile_at(base):
         at = pl.ds(pl.multiple_of(base, 128), 128)
-        return jnp.concatenate([head_ref[:, at], tail_ref[:, at]], axis=0)
+        return jnp.concatenate([head_ref[:, at], second_ref[:, at], tail_ref[:, at]], axis=0)
 
     def lanes_from(lane):
         v = tile_at(lane // 128 * 128)
@@ -343,8 +343,8 @@
     for side, ref in enumerate((keep_ref, send_ref)):
         for k in range(slots):
             at = 2 * (side * slots + k)
-            ref[k, tall : tall + 16, :] = jnp.concatenate(
-                [turned[at : at + 2], jnp.zeros((14, 128), F32)], axis=0
+            ref[k, tall : tall + EDGES, :] = jnp.concatenate(
+                [turned[at : at + 2], jnp.zeros((EDGES - 2, 128), F32)], axis=0
             ).astype(BF)
 
 
@@ -368,7 +368,7 @@
         total = total + ref[...].astype(F32)
     latent = silu_of_half(0.5 * total)
     tall = quarter * 32
-    turned = jnp.concatenate([latent[tall : tall + 16], jnp.zeros((112, 128), F32)], axis=0).T
+    turned = jnp.concatenate([latent[tall : tall + EDGES], jnp.zeros((128 - EDGES, 128), F32)], axis=0).T
     ext = line_ref.shape[1]
     lines = []
     for r in range(quarter):
@@ -623,23 +623,23 @@
     carry = shifted(carry, 1)
     a_first, a_second, mid = call(
         functools.partial(middle_kernel, count, half),
-        [row_f32, row_f32, ((quarter - 2, 32, cols), F32)],
+        [row_f32, row_f32, ((quarter * 32 - 64, cols + 256), F32)],
         [((256, (half // 2 - 2) * wide_cols), BF)],
         h1, h2_mid, h2_low, w2_big, w3_big, v_third, mix, mb=12,
     )
-    pre, tail = call(
+    pre, second = call(
         functools.partial(top_kernel, count, channels, per[0]),
-        [((count, CH_BOT, cols), F32), ((quarter * 32 - 32, cols + 256), F32)],
+        [((count, CH_BOT, cols), F32), ((32, cols + 256), F32)],
         [((total[0], cols), F32), ((512, wide_cols), BF), ((256, wide_cols), BF)],
-        down, spreads, w1_down, h_first, w2_big, a_first, a_second, w3_big, v_second, mix, mid, mb=12,
+        down, spreads, w1_down, h_first, w2_big, a_first, a_second, w3_big, v_second, mix, mb=12,
     )
     slots = peers // 2
-    chunk = (quarter * 32 + 16, 128)
+    chunk = (quarter * 32 + EDGES, 128)
     keep, send = call(
         functools.partial(chunk_kernel, nb),
         [((slots,) + chunk, BF)] * 2,
         [((32, cols + 256), F32)],
-        pre, carry, mix, tail,
+        pre, carry, mix, second, mid,
     )
     got = swapped(send, 1)
     mine, *others = call(pair_kernel, [(chunk, F32)] + [(chunk, BF)] * (slots - 1), [], keep, got)

time: 35.2 us -> 35.1 us (level)
  no operation moved by 1% of the time
where the time goes in v7:
time: 35.1 us; the launch traced here: 35 us
  Pallas kernels  13.6 us (39%)
  starting transfers between devices  13.6 us (39%)
  waiting for transfers between devices  6.46 us (18%)
  local copies, waits for them, and re-layouts  1.17 us (3%)
    pallas_call x11, Pallas kernels, call(): pl.pallas_call(kernel, out_shape=[jax.ShapeDtypeStruct(*o) for o in outs]...  13.6 us
    ppermute x5, starting transfers between devices, shifted(): lax.ppermute(value, 'row', [(i, (i + by) % peers) for i in range(peers)])  9.28 us
    ppermute x4, waiting for transfers between devices, swapped(): lax.ppermute(value, 'mem', [(i, i ^ by) for i in range(lax.axis_size('mem...  5.42 us
    ppermute x4, starting transfers between devices, swapped(): lax.ppermute(value, 'mem', [(i, i ^ by) for i in range(lax.axis_size('mem...  4.3 us
    unnamed x14, local copies, waits for them, and re-layouts  1.11 us
    ppermute x5, waiting for transfers between devices, shifted(): lax.ppermute(value, 'row', [(i, (i + by) % peers) for i in range(peers)])  1.04 us
  transfers between devices with their start and end apart: 9, of which 5 were waited for; matrix products, arithmetic and copies ran while one was open for 0% of the time, Pallas kernels for 31%

profile of v7, /device:TPU:0, one launch (start us, length us, event | category | flops | bytes accessed | tf_op | source)
XLA Modules:
  0.0 35.0 jit_solution(8729746499549419939)
XLA Ops:
  0.0 0.0 copy-start
  0.0 0.2 shard_map.73
  0.2 1.1 %copy-done = bf16[2,5,16,4096]{3,2,1,0:T(8,128)(2,1)S(1)} copy-done((bf16[2,5,16,4096]{3,2,1,0:T(8,128)(2,1)S(1)}, bf16[2,5,16,4096]{3,2,1,0:T(8,128)(2,1)}, u32[]{:S(2)}) %copy-start) | copy-done | bytes 1310744
  1.3 0.0 copy-start.1
  1.3 0.0 copy-start.2
  1.3 0.0 copy-start.3
  1.3 0.0 copy-start.4
  1.3 0.2 shard_map.74
  1.6 3.9 %collective-permute-start.1 = (bf16[160,512]{1,0:T(8,128)(2,1)S(1)}, bf16[160,512]{1,0:T(8,128)(2,1)S(1)}, u32[]{:S(2)}, u32[]{:S(2)}) collective-permute-start(bf16[160,512]{1,0:T(8,128)(2,1)S(1)} %get-tuple-element.58), channel_id=1, source_target_pairs={{0,3},{1,0},{2,1},{3,2},{4,7},{5,4},{6,5},{7,6},{8,11},{9,8},{10,9... | collective-permute-start | bytes 491528 | tf_op jit(solution)/shard_map/ppermute | solution.py:535
  5.5 0.0 collective-permute-start
  5.5 0.0 copy-done.1
  5.5 0.0 copy-done.2
  5.5 0.0 copy-done.3
  5.5 0.0 copy-done.4
  5.6 4.7 %shard_map.75 = (bf16[1792,2048]{1,0:T(8,128)(2,1)S(1)}, f32[128,2048]{1,0:T(8,128)S(1)}, f32[128,2048]{1,0:T(8,128)S(1)}, f32[128,2048]{1,0:T(8,128)S(1)}, f32[...) custom-call(bf16[160,4096]{1,0:T(8,128)(2,1)S(1)} %bitcast.15, ...), custom_call_target="tpu_custom_call" | custom-call | flops 1000000000 | bytes 3000000 | tf_op jit(solution)/shard_map/pallas_call | solution.py:546
  10.2 0.0 collective-permute-done.1.got_ref
  10.2 1.2 %shard_map.76 = (bf16[128,2048]{1,0:T(8,128)(2,1)S(1)}, bf16[32,1024]{1,0:T(8,128)(2,1)S(1)}) custom-call(bf16[160,512]{1,0:T(8,128)(2,1)S(1)} %collective-permute-done.1.got_ref, bf16[2,256,256]{2,1,0:T(8,128)(2,1)S(1)} %get-tuple-element.50.spread_ref, bf16[256,128]{1,0:T(8,128)(2,1)S(1)} %get-tuple-element.59.w1_ref, ...), custom_call_target="tpu_custom_call" | custom-call | flops 1000000000 | bytes 3000000 | tf_op jit(solution)/shard_map/pallas_call | solution.py:546
  11.5 2.3 %collective-permute-start.2 = (bf16[32,1024]{1,0:T(8,128)(2,1)S(1)}, bf16[32,1024]{1,0:T(8,128)(2,1)S(1)}, u32[]{:S(2)}, u32[]{:S(2)}) collective-permute-start(bf16[32,1024]{1,0:T(8,128)(2,1)S(1)} %get-tuple-element.70), channel_id=1, source_target_pairs={{0,1},{1,2},{2,3},{3,0},{4,5},{5,6},{6,7},{7,4},{8,9},{9,10},{10,1... | collective-permute-start | bytes 196616 | tf_op jit(solution)/shard_map/ppermute | solution.py:535
  13.8 2.0 %shard_map.77 = (f32[128,2048]{1,0:T(8,128)S(1)}, f32[128,2048]{1,0:T(8,128)S(1)}, f32[64,1280]{1,0:T(8,128)S(1)}) custom-call(bf16[1792,2048]{1,0:T(8,128)(2,1)S(1)} %get-tuple-element.56.h1_ref, bf16[128,2048]{1,0:T(8,128)(2,1)S(1)} %get-tuple-element.57.h2_mid, bf16[128,2048]{1,0:T(8,128)(2,1)S(1)} %get-tuple-element.63.h2_low, ...), custom_call_target="tpu_custom_call" | custom-call | flops 1000000000 | bytes 3000000 | tf_op jit(solution)/shard_map/pallas_call | solution.py:546
  15.9 0.0 copy-start.6
  15.9 0.0 copy-start.5
  15.9 0.0 collective-permute-done.got_ref
  15.9 1.8 %shard_map.78 = (f32[2,16,1024]{2,1,0:T(8,128)S(1)}, f32[32,1280]{1,0:T(8,128)S(1)}) custom-call(bf16[240,512]{1,0:T(8,128)(2,1)S(1)} %collective-permute-done.got_ref, bf16[2,256,256]{2,1,0:T(8,128)(2,1)S(1)} %get-tuple-element.50.spread_ref, bf16[512,160]{1,0:T(8,128)(2,1)S(1)} %get-tuple-element.53.w1_ref, f32[128,2048]{1,0:T(8,128)S(1)} %get-tuple-element.54.h_ref, ...), custom_call_target="tpu_custom_call" | custom-call | flops 1000000000 | bytes 3000000 | tf_op jit(solution)/shard_map/pallas_call | solution.py:546
  17.7 0.0 collective-permute-done.2.carry_ref
  17.7 0.4 %shard_map.79 = (bf16[4,136,128]{2,1,0:T(8,128)(2,1)S(1)}, bf16[4,136,128]{2,1,0:T(8,128)(2,1)S(1)}) custom-call(f32[2,16,1024]{2,1,0:T(8,128)S(1)} %get-tuple-element.69.pre_ref, bf16[32,1024]{1,0:T(8,128)(2,1)S(1)} %collective-permute-done.2.carry_ref, bf16[32,32]{1,0:T(8,128)(2,1)S(1)} %get-tuple-element.65.mix_ref, ...), custom_call_target="tpu_custom_call" | custom-call | flops 1000000000 | bytes 3000000 | tf_op jit(solution)/shard_map/pallas_call | solution.py:546
  18.0 0.0 collective-permute-start.3
  18.1 1.3 %collective-permute-done.3.got_ref = bf16[4,136,128]{2,1,0:T(8,128)(2,1)S(1)} collective-permute-done((bf16[4,136,128]{2,1,0:T(8,128)(2,1)S(1)}, bf16[4,136,128]{2,1,0:T(8,128)(2,1)S(1)}, u32[]{:S(2)}, u32[]{:S(2)}) %collective-permute-start.3) | collective-permute-done | bytes 139296 | tf_op jit(solution)/shard_map/ppermute | solution.py:539
  19.5 2.7 %collective-permute-start.5 = (bf16[136,128]{1,0:T(8,128)(2,1)S(1)}, bf16[136,128]{1,0:T(8,128)(2,1)S(1)}, u32[]{:S(2)}, u32[]{:S(2)}) collective-permute-start(bf16[136,128]{1,0:T(8,128)(2,1)S(1)} %get-tuple-element.77), channel_id=1, source_target_pairs={{0,16},{4,20},{8,24},{12,28},{16,0},{20,4},{24,8},{28,12},{1,17},{... | collective-permute-start | bytes 104456 | tf_op jit(solution)/shard_map/ppermute | solution.py:539
  22.1 1.3 %collective-permute-start.6 = (bf16[136,128]{1,0:T(8,128)(2,1)S(1)}, bf16[136,128]{1,0:T(8,128)(2,1)S(1)}, u32[]{:S(2)}, u32[]{:S(2)}) collective-permute-start(bf16[136,128]{1,0:T(8,128)(2,1)S(1)} %get-tuple-element.78), channel_id=1, source_target_pairs={{0,24},{4,28},{8,16},{12,20},{16,8},{20,12},{24,0},{28,4},{1,25},{... | collective-permute-start | bytes 104456 | tf_op jit(solution)/shard_map/ppermute | solution.py:539
  23.5 0.3 collective-permute-start.4
  23.7 0.0 copy-done.6
  23.7 0.0 copy-done.5
  23.8 0.9 %collective-permute-done.5.refs_1_ = bf16[136,128]{1,0:T(8,128)(2,1)S(1)} collective-permute-done((bf16[136,128]{1,0:T(8,128)(2,1)S(1)}, bf16[136,128]{1,0:T(8,128)(2,1)S(1)}, u32[]{:S(2)}, u32[]{:S(2)}) %collective-permute-start.5) | collective-permute-done | bytes 34848 | tf_op jit(solution)/shard_map/ppermute | solution.py:539
  24.7 3.1 %collective-permute-done.6.refs_2_ = bf16[136,128]{1,0:T(8,128)(2,1)S(1)} collective-permute-done((bf16[136,128]{1,0:T(8,128)(2,1)S(1)}, bf16[136,128]{1,0:T(8,128)(2,1)S(1)}, u32[]{:S(2)}, u32[]{:S(2)}) %collective-permute-start.6) | collective-permute-done | bytes 34848 | tf_op jit(solution)/shard_map/ppermute | solution.py:539
  27.9 0.0 collective-permute-done.4.refs_0_
  27.9 0.2 shard_map.81
  28.1 1.6 %collective-permute-start.7 = (bf16[32,256]{1,0:T(8,128)(2,1)S(1)}, bf16[32,256]{1,0:T(8,128)(2,1)S(1)}, u32[]{:S(2)}, u32[]{:S(2)}) collective-permute-start(bf16[32,256]{1,0:T(8,128)(2,1)S(1)} %get-tuple-element.79), channel_id=1, source_target_pairs={{0,1},{1,2},{2,3},{3,0},{4,5},{5,6},{6,7},{7,4},{8,9},{9,10},{10,1... | collective-permute-start | bytes 49160 | tf_op jit(solution)/shard_map/ppermute | solution.py:535
  29.6 1.4 %collective-permute-start.8 = (bf16[32,256]{1,0:T(8,128)(2,1)S(1)}, bf16[32,256]{1,0:T(8,128)(2,1)S(1)}, u32[]{:S(2)}, u32[]{:S(2)}) collective-permute-start(bf16[32,256]{1,0:T(8,128)(2,1)S(1)} %get-tuple-element.80), channel_id=1, source_target_pairs={{0,3},{1,0},{2,1},{3,2},{4,7},{5,4},{6,5},{7,6},{8,11},{9,8},{10,9... | collective-permute-start | bytes 49160 | tf_op jit(solution)/shard_map/ppermute | solution.py:535
  31.0 1.3 %shard_map.82 = (bf16[2,128,96]{2,1,0:T(8,128)(2,1)S(1)}, bf16[2,256,256]{2,1,0:T(8,128)(2,1)S(1)}, f32[2,128,256]{2,1,0:T(8,128)S(1)}, f32[2,256,128]{2,1,0:T(8...) custom-call(bf16[128,256]{1,0:T(8,128)(2,1)S(1)} %get-tuple-element.81.line_ref, ...), custom_call_target="tpu_custom_call" | custom-call | flops 1000000000 | bytes 3000000 | tf_op jit(solution)/shard_map/pallas_call | solution.py:546
  32.3 0.4 %collective-permute-done.7.first_ref = bf16[32,256]{1,0:T(8,128)(2,1)S(1)} collective-permute-done((bf16[32,256]{1,0:T(8,128)(2,1)S(1)}, bf16[32,256]{1,0:T(8,128)(2,1)S(1)}, u32[]{:S(2)}, u32[]{:S(2)}) %collective-permute-start.7) | collective-permute-done | bytes 16416 | tf_op jit(solution)/shard_map/ppermute | solution.py:535
  32.8 0.6 %collective-permute-done.8.second_ref = bf16[32,256]{1,0:T(8,128)(2,1)S(1)} collective-permute-done((bf16[32,256]{1,0:T(8,128)(2,1)S(1)}, bf16[32,256]{1,0:T(8,128)(2,1)S(1)}, u32[]{:S(2)}, u32[]{:S(2)}) %collective-permute-start.8) | collective-permute-done | bytes 16416 | tf_op jit(solution)/shard_map/ppermute | solution.py:535
  33.4 1.6 %shard_map.83 = bf16[16,16,512]{2,1,0:T(8,128)(2,1)} custom-call(bf16[32,256]{1,0:T(8,128)(2,1)S(1)} %collective-permute-done.7.first_ref, bf16[32,256]{1,0:T(8,128)(2,1)S(1)} %collective-permute-done.8.second_ref, bf16[2,128,96]{2,1,0:T(8,128)(2,1)S(1)} %get-tuple-element.84.w_edge, bf16[2,256,256]{2,1,0:T(8,128)(2,1)S(1)} %get-tuple-element.85.w_field, ...), custom_call_target="tpu_custom_call" | custom-call | flops 1000000000 | bytes 3000000 | tf_op jit(solution)/shard_map/pallas_call | solution.py:546
  (3 shorter events, 0.1 us)
Async XLA Ops:
  0.0 1.3 %copy-start = (bf16[2,5,16,4096]{3,2,1,0:T(8,128)(2,1)S(1)}, bf16[2,5,16,4096]{3,2,1,0:T(8,128)(2,1)}, u32[]{:S(2)}) copy-start(bf16[2,5,16,4096]{3,2,1,0:T(8,128)(2,1)} %param.7) | copy-start | bytes 3932164
  1.3 4.2 %copy-start.1 = (bf16[64,64,3,3]{1,0,3,2:T(8,128)(2,1)S(1)}, bf16[64,64,3,3]{1,0,3,2:T(8,128)(2,1)}, u32[]{:S(2)}) copy-start(bf16[64,64,3,3]{1,0,3,2:T(8,128)(2,1)} %param.9) | copy-start | bytes 221188
  1.3 4.2 %copy-start.2 = (bf16[16,64,3,3]{1,0,3,2:T(8,128)(2,1)S(1)}, bf16[16,64,3,3]{1,0,3,2:T(8,128)(2,1)}, u32[]{:S(2)}) copy-start(bf16[16,64,3,3]{1,0,3,2:T(8,128)(2,1)} %param.10) | copy-start | bytes 55300
  1.3 4.2 %copy-start.3 = (bf16[32,256]{1,0:T(8,128)(2,1)S(1)}, bf16[32,256]{1,0:T(8,128)(2,1)}, u32[]{:S(2)}) copy-start(bf16[32,256]{1,0:T(8,128)(2,1)} %mix_ref.1) | copy-start | bytes 49156
  1.3 4.2 %copy-start.4 = (bf16[64,5,3,3]{0,3,2,1:T(4,128)(2,1)S(1)}, bf16[64,5,3,3]{0,3,2,1:T(4,128)(2,1)}, u32[]{:S(2)}) copy-start(bf16[64,5,3,3]{0,3,2,1:T(4,128)(2,1)} %param.8) | copy-start | bytes 17284
  1.6 8.7 %collective-permute-start.1 = (bf16[160,512]{1,0:T(8,128)(2,1)S(1)}, bf16[160,512]{1,0:T(8,128)(2,1)S(1)}, u32[]{:S(2)}, u32[]{:S(2)}) collective-permute-start(bf16[160,512]{1,0:T(8,128)(2,1)S(1)} %get-tuple-element.58), channel_id=1, source_target_pairs={{0,3},{1,0},{2,1},{3,2},{4,7},{5,4},{6,5},{7,6},{8,11},{9,8},{10,9... | collective-permute-start | bytes 491528 | tf_op jit(solution)/shard_map/ppermute | solution.py:535
  5.5 10.4 %collective-permute-start = (bf16[240,512]{1,0:T(8,128)(2,1)S(1)}, bf16[240,512]{1,0:T(8,128)(2,1)S(1)}, u32[]{:S(2)}, u32[]{:S(2)}) collective-permute-start(bf16[240,512]{1,0:T(8,128)(2,1)S(1)} %get-tuple-element.49), channel_id=1, source_target_pairs={{0,1},{1,2},{2,3},{3,0},{4,5},{5,6},{6,7},{7,4},{8,9},{9,10},{10,1... | collective-permute-start | bytes 737288 | tf_op jit(solution)/shard_map/ppermute | solution.py:535
  11.5 6.2 %collective-permute-start.2 = (bf16[32,1024]{1,0:T(8,128)(2,1)S(1)}, bf16[32,1024]{1,0:T(8,128)(2,1)S(1)}, u32[]{:S(2)}, u32[]{:S(2)}) collective-permute-start(bf16[32,1024]{1,0:T(8,128)(2,1)S(1)} %get-tuple-element.70), channel_id=1, source_target_pairs={{0,1},{1,2},{2,3},{3,0},{4,5},{5,6},{6,7},{7,4},{8,9},{9,10},{10,1... | collective-permute-start | bytes 196616 | tf_op jit(solution)/shard_map/ppermute | solution.py:535
  15.9 7.9 %copy-start.6 = (bf16[16,32,4,4]{1,3,2,0:T(4,128)(2,1)S(1)}, bf16[16,32,4,4]{1,3,2,0:T(4,128)(2,1)}, u32[]{:S(2)}) copy-start(bf16[16,32,4,4]{1,3,2,0:T(4,128)(2,1)} %param.13) | copy-start | bytes 49156
  15.9 7.9 %copy-start.5 = (bf16[32,32,4,4]{1,3,2,0:T(4,128)(2,1)S(1)}, bf16[32,32,4,4]{1,3,2,0:T(4,128)(2,1)}, u32[]{:S(2)}) copy-start(bf16[32,32,4,4]{1,3,2,0:T(4,128)(2,1)} %param.12) | copy-start | bytes 98308
  18.0 1.4 %collective-permute-start.3 = (bf16[4,136,128]{2,1,0:T(8,128)(2,1)S(1)}, bf16[4,136,128]{2,1,0:T(8,128)(2,1)S(1)}, u32[]{:S(2)}, u32[]{:S(2)}) collective-permute-start(bf16[4,136,128]{2,1,0:T(8,128)(2,1)S(1)} %get-tuple-element.74), channel_id=1, source_target_pairs={{0,4},{4,0},{8,12},{12,8},{16,20},{20,16},{24,28},{28,24},{1,5},{5... | collective-permute-start | bytes 417800 | tf_op jit(solution)/shard_map/ppermute | solution.py:539
  19.5 5.3 %collective-permute-start.5 = (bf16[136,128]{1,0:T(8,128)(2,1)S(1)}, bf16[136,128]{1,0:T(8,128)(2,1)S(1)}, u32[]{:S(2)}, u32[]{:S(2)}) collective-permute-start(bf16[136,128]{1,0:T(8,128)(2,1)S(1)} %get-tuple-element.77), channel_id=1, source_target_pairs={{0,16},{4,20},{8,24},{12,28},{16,0},{20,4},{24,8},{28,12},{1,17},{... | collective-permute-start | bytes 104456 | tf_op jit(solution)/shard_map/ppermute | solution.py:539
  22.1 5.7 %collective-permute-start.6 = (bf16[136,128]{1,0:T(8,128)(2,1)S(1)}, bf16[136,128]{1,0:T(8,128)(2,1)S(1)}, u32[]{:S(2)}, u32[]{:S(2)}) collective-permute-start(bf16[136,128]{1,0:T(8,128)(2,1)S(1)} %get-tuple-element.78), channel_id=1, source_target_pairs={{0,24},{4,28},{8,16},{12,20},{16,8},{20,12},{24,0},{28,4},{1,25},{... | collective-permute-start | bytes 104456 | tf_op jit(solution)/shard_map/ppermute | solution.py:539
  23.5 4.4 %collective-permute-start.4 = (bf16[136,128]{1,0:T(8,128)(2,1)S(1)}, bf16[136,128]{1,0:T(8,128)(2,1)S(1)}, u32[]{:S(2)}, u32[]{:S(2)}) collective-permute-start(bf16[136,128]{1,0:T(8,128)(2,1)S(1)} %get-tuple-element.76), channel_id=1, source_target_pairs={{0,8},{4,12},{8,0},{12,4},{16,24},{20,28},{24,16},{28,20},{1,9},{5... | collective-permute-start | bytes 104456 | tf_op jit(solution)/shard_map/ppermute | solution.py:539
  28.1 4.7 %collective-permute-start.7 = (bf16[32,256]{1,0:T(8,128)(2,1)S(1)}, bf16[32,256]{1,0:T(8,128)(2,1)S(1)}, u32[]{:S(2)}, u32[]{:S(2)}) collective-permute-start(bf16[32,256]{1,0:T(8,128)(2,1)S(1)} %get-tuple-element.79), channel_id=1, source_target_pairs={{0,1},{1,2},{2,3},{3,0},{4,5},{5,6},{6,7},{7,4},{8,9},{9,10},{10,1... | collective-permute-start | bytes 49160 | tf_op jit(solution)/shard_map/ppermute | solution.py:535
  29.6 3.7 %collective-permute-start.8 = (bf16[32,256]{1,0:T(8,128)(2,1)S(1)}, bf16[32,256]{1,0:T(8,128)(2,1)S(1)}, u32[]{:S(2)}, u32[]{:S(2)}) collective-permute-start(bf16[32,256]{1,0:T(8,128)(2,1)S(1)} %get-tuple-element.80), channel_id=1, source_target_pairs={{0,3},{1,0},{2,1},{3,2},{4,7},{5,4},{6,5},{7,6},{8,11},{9,8},{10,9... | collective-permute-start | bytes 49160 | tf_op jit(solution)/shard_map/ppermute | solution.py:535

commit v8 on v7

--- a/solution.py
+++ b/solution.py
@@ -152,7 +152,7 @@
 def inner_kernel(
     members, channels, rows,
     x_ref, w1_ref, w2_ref, w3_ref, mix_ref, spread_ref, own_ref, above_ref, below_ref,
-    h1_ref, h_first, h_last, a_last, v_second, v_third, h2_mid,
+    h1_ref, h_first, h_last, a_last, a_first, a_second, v_second, v_third, h2_mid,
     w2_big, w3_big, w1_down, w1_up, mix_own,
     w1_flat, w1_own, y_ref, out1_ref, h2_ref,
 ):
@@ -227,6 +227,8 @@
     v = dot(w3_big[...], h2_ref[...])
     v_second[...] = v[0:32]
     v_third[...] = v[32:64]
+    a_first[...] = dot(w2_big[:, 512:768], h1_ref[0:256, :])
+    a_second[...] = dot(w2_big[:, 256:768], h1_ref[0:512, :])
     h2_mid[...] = silu_of_half(dot(w2_big[...], h1_ref[512:1280, :])).astype(BF)
 
 
@@ -253,12 +255,10 @@
 def middle_kernel(
     members, half,
     h1_ref, h2_mid, h2_low, w2_ref, w3_ref, v_ref, mix_ref,
-    a_first, a_second, mixed_ref, h2_ref,
+    mixed_ref, h2_ref,
 ):
     wide = h1_ref.shape[1]
     cols = wide // members
-    a_first[...] = dot(w2_ref[:, 512:768], h1_ref[0:256, :])
-    a_second[...] = dot(w2_ref[:, 256:768], h1_ref[0:512, :])
     pairs = range(4, half, 2)
     for n, a in enumerate(pairs):
         lanes = slice(n * wide, (n + 1) * wide)
@@ -590,12 +590,12 @@
     row_f32 = ((128, wide_cols), F32)
     third_f32 = ((32, wide_cols), F32)
     (
-        h1, h_first, h_last, a_last, v_second, v_third, h2_mid,
+        h1, h_first, h_last, a_last, a_first, a_second, v_second, v_third, h2_mid,
         w2_big, w3_big, w1_down, w1_up, mix,
     ) = call(
         functools.partial(inner_kernel, count, channels, rows),
         [((256 * (half - 1), wide_cols), BF)]
-        + [row_f32] * 3
+        + [row_f32] * 5
         + [third_f32] * 2
         + [
             ((128, wide_cols), BF),
@@ -621,9 +621,9 @@
         up, spreads, w1_up, h_last, w2_big, a_last, w3_big, mb=12,
     )
     carry = shifted(carry, 1)
-    a_first, a_second, mid = call(
+    (mid,) = call(
         functools.partial(middle_kernel, count, half),
-        [row_f32, row_f32, ((quarter * 32 - 64, cols + 256), F32)],
+        [((quarter * 32 - 64, cols + 256), F32)],
         [((256, (half // 2 - 2) * wide_cols), BF)],
         h1, h2_mid, h2_low, w2_big, w3_big, v_third, mix, mb=12,
     )

time: 35.1 us -> 35.2 us (level)
  starting transfers between devices: 13.6 us -> 13.2 us
  waiting for transfers between devices: 6.46 us -> 6.85 us
    ppermute x5, waiting for transfers between devices: 1.04 us -> 1.41 us  [shifted(): lax.ppermute(value, 'row', [(i, (i + by) % peers) for i in range(peers)])]
where the time goes in v8:
time: 35.2 us; the launch traced here: 35 us
  Pallas kernels  13.7 us (39%)
  starting transfers between devices  13.2 us (38%)
  waiting for transfers between devices  6.85 us (19%)
  local copies, waits for them, and re-layouts  1.17 us (3%)
    pallas_call x11, Pallas kernels, call(): pl.pallas_call(kernel, out_shape=[jax.ShapeDtypeStruct(*o) for o in outs]...  13.7 us
    ppermute x5, starting transfers between devices, shifted(): lax.ppermute(value, 'row', [(i, (i + by) % peers) for i in range(peers)])  8.93 us
    ppermute x4, waiting for transfers between devices, swapped(): lax.ppermute(value, 'mem', [(i, i ^ by) for i in range(lax.axis_size('mem...  5.44 us
    ppermute x4, starting transfers between devices, swapped(): lax.ppermute(value, 'mem', [(i, i ^ by) for i in range(lax.axis_size('mem...  4.28 us
    ppermute x5, waiting for transfers between devices, shifted(): lax.ppermute(value, 'row', [(i, (i + by) % peers) for i in range(peers)])  1.41 us
    unnamed x14, local copies, waits for them, and re-layouts  1.11 us
  transfers between devices with their start and end apart: 9, of which 5 were waited for; matrix products, arithmetic and copies ran while one was open for 0% of the time, Pallas kernels for 31%

profile of v8, /device:TPU:0, one launch (start us, length us, event | category | flops | bytes accessed | tf_op | source)
XLA Modules:
  0.0 35.0 jit_solution(6739654094400111452)
XLA Ops:
  0.0 0.0 copy-start
  0.0 0.2 shard_map.73
  0.2 1.1 %copy-done = bf16[2,5,16,4096]{3,2,1,0:T(8,128)(2,1)S(1)} copy-done((bf16[2,5,16,4096]{3,2,1,0:T(8,128)(2,1)S(1)}, bf16[2,5,16,4096]{3,2,1,0:T(8,128)(2,1)}, u32[]{:S(2)}) %copy-start) | copy-done | bytes 1310744
  1.3 0.0 copy-start.1
  1.3 0.0 copy-start.2
  1.3 0.0 copy-start.3
  1.3 0.0 copy-start.4
  1.3 0.2 shard_map.74
  1.6 3.9 %collective-permute-start.1 = (bf16[160,512]{1,0:T(8,128)(2,1)S(1)}, bf16[160,512]{1,0:T(8,128)(2,1)S(1)}, u32[]{:S(2)}, u32[]{:S(2)}) collective-permute-start(bf16[160,512]{1,0:T(8,128)(2,1)S(1)} %get-tuple-element.61), channel_id=1, source_target_pairs={{0,3},{1,0},{2,1},{3,2},{4,7},{5,4},{6,5},{7,6},{8,11},{9,8},{10,9... | collective-permute-start | bytes 491528 | tf_op jit(solution)/shard_map/ppermute | solution.py:535
  5.5 0.0 collective-permute-start
  5.5 0.0 copy-done.1
  5.5 0.0 copy-done.2
  5.5 0.0 copy-done.3
  5.5 0.0 copy-done.4
  5.6 5.1 %shard_map.75 = (bf16[1792,2048]{1,0:T(8,128)(2,1)S(1)}, f32[128,2048]{1,0:T(8,128)S(1)}, f32[128,2048]{1,0:T(8,128)S(1)}, f32[128,2048]{1,0:T(8,128)S(1)}, f32[...) custom-call(bf16[160,4096]{1,0:T(8,128)(2,1)S(1)} %bitcast.15, ...), custom_call_target="tpu_custom_call" | custom-call | flops 1000000000 | bytes 3000000 | tf_op jit(solution)/shard_map/pallas_call | solution.py:546
  10.6 0.0 collective-permute-done.1.got_ref
  10.6 1.2 %shard_map.77 = (bf16[128,2048]{1,0:T(8,128)(2,1)S(1)}, bf16[32,1024]{1,0:T(8,128)(2,1)S(1)}) custom-call(bf16[160,512]{1,0:T(8,128)(2,1)S(1)} %collective-permute-done.1.got_ref, bf16[2,256,256]{2,1,0:T(8,128)(2,1)S(1)} %get-tuple-element.49.spread_ref, bf16[256,128]{1,0:T(8,128)(2,1)S(1)} %get-tuple-element.62.w1_ref, ...), custom_call_target="tpu_custom_call" | custom-call | flops 1000000000 | bytes 3000000 | tf_op jit(solution)/shard_map/pallas_call | solution.py:546
  11.9 2.0 %collective-permute-start.2 = (bf16[32,1024]{1,0:T(8,128)(2,1)S(1)}, bf16[32,1024]{1,0:T(8,128)(2,1)S(1)}, u32[]{:S(2)}, u32[]{:S(2)}) collective-permute-start(bf16[32,1024]{1,0:T(8,128)(2,1)S(1)} %get-tuple-element.65), channel_id=1, source_target_pairs={{0,1},{1,2},{2,3},{3,0},{4,5},{5,6},{6,7},{7,4},{8,9},{9,10},{10,1... | collective-permute-start | bytes 196616 | tf_op jit(solution)/shard_map/ppermute | solution.py:535
  13.9 1.6 %shard_map.78.tail_ref = f32[64,1280]{1,0:T(8,128)S(1)} custom-call(bf16[1792,2048]{1,0:T(8,128)(2,1)S(1)} %get-tuple-element.67.h1_ref, bf16[128,2048]{1,0:T(8,128)(2,1)S(1)} %get-tuple-element.68.h2_mid, bf16[128,2048]{1,0:T(8,128)(2,1)S(1)} %get-tuple-element.69.h2_low, bf16[128,768]{1,0:T(8,128)(2,1)S(1)} %get-tuple-element.54.w2_ref, ...), custom_call_target="tpu_custom_call" | custom-call | flops 1000000000 | bytes 3000000 | tf_op jit(solution)/shard_map/pallas_call | solution.py:546
  15.5 0.0 copy-start.6
  15.5 0.0 copy-start.5
  15.5 0.0 collective-permute-done.got_ref
  15.5 1.8 %shard_map.76 = (f32[2,16,1024]{2,1,0:T(8,128)S(1)}, f32[32,1280]{1,0:T(8,128)S(1)}) custom-call(bf16[240,512]{1,0:T(8,128)(2,1)S(1)} %collective-permute-done.got_ref, bf16[2,256,256]{2,1,0:T(8,128)(2,1)S(1)} %get-tuple-element.49.spread_ref, bf16[512,160]{1,0:T(8,128)(2,1)S(1)} %get-tuple-element.52.w1_ref, f32[128,2048]{1,0:T(8,128)S(1)} %get-tuple-element.53.h_ref, ...), custom_call_target="tpu_custom_call" | custom-call | flops 1000000000 | bytes 3000000 | tf_op jit(solution)/shard_map/pallas_call | solution.py:546
  17.3 0.0 collective-permute-done.2.carry_ref
  17.3 0.4 %shard_map.79 = (bf16[4,136,128]{2,1,0:T(8,128)(2,1)S(1)}, bf16[4,136,128]{2,1,0:T(8,128)(2,1)S(1)}) custom-call(f32[2,16,1024]{2,1,0:T(8,128)S(1)} %get-tuple-element.60.pre_ref, bf16[32,1024]{1,0:T(8,128)(2,1)S(1)} %collective-permute-done.2.carry_ref, bf16[32,32]{1,0:T(8,128)(2,1)S(1)} %get-tuple-element.59.mix_ref, ...), custom_call_target="tpu_custom_call" | custom-call | flops 1000000000 | bytes 3000000 | tf_op jit(solution)/shard_map/pallas_call | solution.py:546
  17.7 0.0 collective-permute-start.3
  17.7 1.3 %collective-permute-done.3.got_ref = bf16[4,136,128]{2,1,0:T(8,128)(2,1)S(1)} collective-permute-done((bf16[4,136,128]{2,1,0:T(8,128)(2,1)S(1)}, bf16[4,136,128]{2,1,0:T(8,128)(2,1)S(1)}, u32[]{:S(2)}, u32[]{:S(2)}) %collective-permute-start.3) | collective-permute-done | bytes 139296 | tf_op jit(solution)/shard_map/ppermute | solution.py:539
  19.1 2.7 %collective-permute-start.5 = (bf16[136,128]{1,0:T(8,128)(2,1)S(1)}, bf16[136,128]{1,0:T(8,128)(2,1)S(1)}, u32[]{:S(2)}, u32[]{:S(2)}) collective-permute-start(bf16[136,128]{1,0:T(8,128)(2,1)S(1)} %get-tuple-element.75), channel_id=1, source_target_pairs={{0,16},{4,20},{8,24},{12,28},{16,0},{20,4},{24,8},{28,12},{1,17},{... | collective-permute-start | bytes 104456 | tf_op jit(solution)/shard_map/ppermute | solution.py:539
  21.8 1.4 %collective-permute-start.6 = (bf16[136,128]{1,0:T(8,128)(2,1)S(1)}, bf16[136,128]{1,0:T(8,128)(2,1)S(1)}, u32[]{:S(2)}, u32[]{:S(2)}) collective-permute-start(bf16[136,128]{1,0:T(8,128)(2,1)S(1)} %get-tuple-element.76), channel_id=1, source_target_pairs={{0,24},{4,28},{8,16},{12,20},{16,8},{20,12},{24,0},{28,4},{1,25},{... | collective-permute-start | bytes 104456 | tf_op jit(solution)/shard_map/ppermute | solution.py:539
  23.2 0.2 collective-permute-start.4
  23.4 0.0 copy-done.6
  23.4 0.0 copy-done.5
  23.4 1.0 %collective-permute-done.5.refs_1_ = bf16[136,128]{1,0:T(8,128)(2,1)S(1)} collective-permute-done((bf16[136,128]{1,0:T(8,128)(2,1)S(1)}, bf16[136,128]{1,0:T(8,128)(2,1)S(1)}, u32[]{:S(2)}, u32[]{:S(2)}) %collective-permute-start.5) | collective-permute-done | bytes 34848 | tf_op jit(solution)/shard_map/ppermute | solution.py:539
  24.4 3.1 %collective-permute-done.6.refs_2_ = bf16[136,128]{1,0:T(8,128)(2,1)S(1)} collective-permute-done((bf16[136,128]{1,0:T(8,128)(2,1)S(1)}, bf16[136,128]{1,0:T(8,128)(2,1)S(1)}, u32[]{:S(2)}, u32[]{:S(2)}) %collective-permute-start.6) | collective-permute-done | bytes 34848 | tf_op jit(solution)/shard_map/ppermute | solution.py:539
  27.5 0.0 collective-permute-done.4.refs_0_
  27.5 0.2 shard_map.81
  27.7 1.9 %collective-permute-start.7 = (bf16[32,256]{1,0:T(8,128)(2,1)S(1)}, bf16[32,256]{1,0:T(8,128)(2,1)S(1)}, u32[]{:S(2)}, u32[]{:S(2)}) collective-permute-start(bf16[32,256]{1,0:T(8,128)(2,1)S(1)} %get-tuple-element.77), channel_id=1, source_target_pairs={{0,1},{1,2},{2,3},{3,0},{4,5},{5,6},{6,7},{7,4},{8,9},{9,10},{10,1... | collective-permute-start | bytes 49160 | tf_op jit(solution)/shard_map/ppermute | solution.py:535
  29.7 1.0 %collective-permute-start.8 = (bf16[32,256]{1,0:T(8,128)(2,1)S(1)}, bf16[32,256]{1,0:T(8,128)(2,1)S(1)}, u32[]{:S(2)}, u32[]{:S(2)}) collective-permute-start(bf16[32,256]{1,0:T(8,128)(2,1)S(1)} %get-tuple-element.78), channel_id=1, source_target_pairs={{0,3},{1,0},{2,1},{3,2},{4,7},{5,4},{6,5},{7,6},{8,11},{9,8},{10,9... | collective-permute-start | bytes 49160 | tf_op jit(solution)/shard_map/ppermute | solution.py:535
  30.7 1.3 %shard_map.82 = (bf16[2,128,96]{2,1,0:T(8,128)(2,1)S(1)}, bf16[2,256,256]{2,1,0:T(8,128)(2,1)S(1)}, f32[2,128,256]{2,1,0:T(8,128)S(1)}, f32[2,256,128]{2,1,0:T(8...) custom-call(bf16[128,256]{1,0:T(8,128)(2,1)S(1)} %get-tuple-element.79.line_ref, ...), custom_call_target="tpu_custom_call" | custom-call | flops 1000000000 | bytes 3000000 | tf_op jit(solution)/shard_map/pallas_call | solution.py:546
  32.0 0.4 %collective-permute-done.7.first_ref = bf16[32,256]{1,0:T(8,128)(2,1)S(1)} collective-permute-done((bf16[32,256]{1,0:T(8,128)(2,1)S(1)}, bf16[32,256]{1,0:T(8,128)(2,1)S(1)}, u32[]{:S(2)}, u32[]{:S(2)}) %collective-permute-start.7) | collective-permute-done | bytes 16416 | tf_op jit(solution)/shard_map/ppermute | solution.py:535
  32.4 1.0 %collective-permute-done.8.second_ref = bf16[32,256]{1,0:T(8,128)(2,1)S(1)} collective-permute-done((bf16[32,256]{1,0:T(8,128)(2,1)S(1)}, bf16[32,256]{1,0:T(8,128)(2,1)S(1)}, u32[]{:S(2)}, u32[]{:S(2)}) %collective-permute-start.8) | collective-permute-done | bytes 16416 | tf_op jit(solution)/shard_map/ppermute | solution.py:535
  33.4 1.6 %shard_map.83 = bf16[16,16,512]{2,1,0:T(8,128)(2,1)} custom-call(bf16[32,256]{1,0:T(8,128)(2,1)S(1)} %collective-permute-done.7.first_ref, bf16[32,256]{1,0:T(8,128)(2,1)S(1)} %collective-permute-done.8.second_ref, bf16[2,128,96]{2,1,0:T(8,128)(2,1)S(1)} %get-tuple-element.82.w_edge, bf16[2,256,256]{2,1,0:T(8,128)(2,1)S(1)} %get-tuple-element.83.w_field, ...), custom_call_target="tpu_custom_call" | custom-call | flops 1000000000 | bytes 3000000 | tf_op jit(solution)/shard_map/pallas_call | solution.py:546
  (3 shorter events, 0.1 us)
Async XLA Ops:
  0.0 1.3 %copy-start = (bf16[2,5,16,4096]{3,2,1,0:T(8,128)(2,1)S(1)}, bf16[2,5,16,4096]{3,2,1,0:T(8,128)(2,1)}, u32[]{:S(2)}) copy-start(bf16[2,5,16,4096]{3,2,1,0:T(8,128)(2,1)} %param.7) | copy-start | bytes 3932164
  1.3 4.2 %copy-start.1 = (bf16[64,64,3,3]{1,0,3,2:T(8,128)(2,1)S(1)}, bf16[64,64,3,3]{1,0,3,2:T(8,128)(2,1)}, u32[]{:S(2)}) copy-start(bf16[64,64,3,3]{1,0,3,2:T(8,128)(2,1)} %param.9) | copy-start | bytes 221188
  1.3 4.2 %copy-start.2 = (bf16[16,64,3,3]{1,0,3,2:T(8,128)(2,1)S(1)}, bf16[16,64,3,3]{1,0,3,2:T(8,128)(2,1)}, u32[]{:S(2)}) copy-start(bf16[16,64,3,3]{1,0,3,2:T(8,128)(2,1)} %param.10) | copy-start | bytes 55300
  1.3 4.2 %copy-start.3 = (bf16[32,256]{1,0:T(8,128)(2,1)S(1)}, bf16[32,256]{1,0:T(8,128)(2,1)}, u32[]{:S(2)}) copy-start(bf16[32,256]{1,0:T(8,128)(2,1)} %mix_ref.1) | copy-start | bytes 49156
  1.3 4.2 %copy-start.4 = (bf16[64,5,3,3]{0,3,2,1:T(4,128)(2,1)S(1)}, bf16[64,5,3,3]{0,3,2,1:T(4,128)(2,1)}, u32[]{:S(2)}) copy-start(bf16[64,5,3,3]{0,3,2,1:T(4,128)(2,1)} %param.8) | copy-start | bytes 17284
  1.6 9.1 %collective-permute-start.1 = (bf16[160,512]{1,0:T(8,128)(2,1)S(1)}, bf16[160,512]{1,0:T(8,128)(2,1)S(1)}, u32[]{:S(2)}, u32[]{:S(2)}) collective-permute-start(bf16[160,512]{1,0:T(8,128)(2,1)S(1)} %get-tuple-element.61), channel_id=1, source_target_pairs={{0,3},{1,0},{2,1},{3,2},{4,7},{5,4},{6,5},{7,6},{8,11},{9,8},{10,9... | collective-permute-start | bytes 491528 | tf_op jit(solution)/shard_map/ppermute | solution.py:535
  5.5 10.0 %collective-permute-start = (bf16[240,512]{1,0:T(8,128)(2,1)S(1)}, bf16[240,512]{1,0:T(8,128)(2,1)S(1)}, u32[]{:S(2)}, u32[]{:S(2)}) collective-permute-start(bf16[240,512]{1,0:T(8,128)(2,1)S(1)} %get-tuple-element.48), channel_id=1, source_target_pairs={{0,1},{1,2},{2,3},{3,0},{4,5},{5,6},{6,7},{7,4},{8,9},{9,10},{10,1... | collective-permute-start | bytes 737288 | tf_op jit(solution)/shard_map/ppermute | solution.py:535
  11.9 5.4 %collective-permute-start.2 = (bf16[32,1024]{1,0:T(8,128)(2,1)S(1)}, bf16[32,1024]{1,0:T(8,128)(2,1)S(1)}, u32[]{:S(2)}, u32[]{:S(2)}) collective-permute-start(bf16[32,1024]{1,0:T(8,128)(2,1)S(1)} %get-tuple-element.65), channel_id=1, source_target_pairs={{0,1},{1,2},{2,3},{3,0},{4,5},{5,6},{6,7},{7,4},{8,9},{9,10},{10,1... | collective-permute-start | bytes 196616 | tf_op jit(solution)/shard_map/ppermute | solution.py:535
  15.5 7.9 %copy-start.6 = (bf16[16,32,4,4]{1,3,2,0:T(4,128)(2,1)S(1)}, bf16[16,32,4,4]{1,3,2,0:T(4,128)(2,1)}, u32[]{:S(2)}) copy-start(bf16[16,32,4,4]{1,3,2,0:T(4,128)(2,1)} %param.13) | copy-start | bytes 49156
  15.5 7.9 %copy-start.5 = (bf16[32,32,4,4]{1,3,2,0:T(4,128)(2,1)S(1)}, bf16[32,32,4,4]{1,3,2,0:T(4,128)(2,1)}, u32[]{:S(2)}) copy-start(bf16[32,32,4,4]{1,3,2,0:T(4,128)(2,1)} %param.12) | copy-start | bytes 98308
  17.7 1.4 %collective-permute-start.3 = (bf16[4,136,128]{2,1,0:T(8,128)(2,1)S(1)}, bf16[4,136,128]{2,1,0:T(8,128)(2,1)S(1)}, u32[]{:S(2)}, u32[]{:S(2)}) collective-permute-start(bf16[4,136,128]{2,1,0:T(8,128)(2,1)S(1)} %get-tuple-element.72), channel_id=1, source_target_pairs={{0,4},{4,0},{8,12},{12,8},{16,20},{20,16},{24,28},{28,24},{1,5},{5... | collective-permute-start | bytes 417800 | tf_op jit(solution)/shard_map/ppermute | solution.py:539
  19.1 5.3 %collective-permute-start.5 = (bf16[136,128]{1,0:T(8,128)(2,1)S(1)}, bf16[136,128]{1,0:T(8,128)(2,1)S(1)}, u32[]{:S(2)}, u32[]{:S(2)}) collective-permute-start(bf16[136,128]{1,0:T(8,128)(2,1)S(1)} %get-tuple-element.75), channel_id=1, source_target_pairs={{0,16},{4,20},{8,24},{12,28},{16,0},{20,4},{24,8},{28,12},{1,17},{... | collective-permute-start | bytes 104456 | tf_op jit(solution)/shard_map/ppermute | solution.py:539
  21.8 5.7 %collective-permute-start.6 = (bf16[136,128]{1,0:T(8,128)(2,1)S(1)}, bf16[136,128]{1,0:T(8,128)(2,1)S(1)}, u32[]{:S(2)}, u32[]{:S(2)}) collective-permute-start(bf16[136,128]{1,0:T(8,128)(2,1)S(1)} %get-tuple-element.76), channel_id=1, source_target_pairs={{0,24},{4,28},{8,16},{12,20},{16,8},{20,12},{24,0},{28,4},{1,25},{... | collective-permute-start | bytes 104456 | tf_op jit(solution)/shard_map/ppermute | solution.py:539
  23.2 4.4 %collective-permute-start.4 = (bf16[136,128]{1,0:T(8,128)(2,1)S(1)}, bf16[136,128]{1,0:T(8,128)(2,1)S(1)}, u32[]{:S(2)}, u32[]{:S(2)}) collective-permute-start(bf16[136,128]{1,0:T(8,128)(2,1)S(1)} %get-tuple-element.74), channel_id=1, source_target_pairs={{0,8},{4,12},{8,0},{12,4},{16,24},{20,28},{24,16},{28,20},{1,9},{5... | collective-permute-start | bytes 104456 | tf_op jit(solution)/shard_map/ppermute | solution.py:539
  27.7 4.7 %collective-permute-start.7 = (bf16[32,256]{1,0:T(8,128)(2,1)S(1)}, bf16[32,256]{1,0:T(8,128)(2,1)S(1)}, u32[]{:S(2)}, u32[]{:S(2)}) collective-permute-start(bf16[32,256]{1,0:T(8,128)(2,1)S(1)} %get-tuple-element.77), channel_id=1, source_target_pairs={{0,1},{1,2},{2,3},{3,0},{4,5},{5,6},{6,7},{7,4},{8,9},{9,10},{10,1... | collective-permute-start | bytes 49160 | tf_op jit(solution)/shard_map/ppermute | solution.py:535
  29.7 3.7 %collective-permute-start.8 = (bf16[32,256]{1,0:T(8,128)(2,1)S(1)}, bf16[32,256]{1,0:T(8,128)(2,1)S(1)}, u32[]{:S(2)}, u32[]{:S(2)}) collective-permute-start(bf16[32,256]{1,0:T(8,128)(2,1)S(1)} %get-tuple-element.78), channel_id=1, source_target_pairs={{0,3},{1,0},{2,1},{3,2},{4,7},{5,4},{6,5},{7,6},{8,11},{9,8},{10,9... | collective-permute-start | bytes 49160 | tf_op jit(solution)/shard_map/ppermute | solution.py:535

commit v9 on v8

--- a/solution.py
+++ b/solution.py
@@ -306,7 +306,7 @@
 
 
 def chunk_kernel(nb, pre_ref, carry_ref, mix_ref, second_ref, tail_ref, keep_ref, send_ref, head_ref):
-    members = pre_ref.shape[0]
+    members, _, cols = pre_ref.shape
     carry = carry_ref[...].astype(F32) * is_row(0)
     first = [
         silu_of_half(pre_ref[m] + carry[m * 16 : m * 16 + 16]).astype(BF) for m in range(members)
@@ -325,23 +325,17 @@
         v = tile_at(lane // 128 * 128)
         return v if nb % 128 == 0 else pltpu.roll(v, (128 - lane % 128) % 128, 1)
 
-    lane_at = lax.broadcasted_iota(jnp.int32, (tall, 128), 1)
-    edges = jnp.zeros((tall, 128), F32)
+    count = 4 * slots
+    which = lax.broadcasted_iota(jnp.int32, (count, cols + 256), 0)
+    lane = lax.broadcasted_iota(jnp.int32, (count, cols + 256), 1)
+    block = me ^ (2 * (lax.rem(which, 2 * slots) // 2) + which // (2 * slots))
+    edge = 128 + block * nb + jnp.where(lax.rem(which, 2) == 0, -1, nb)
+    pick = jnp.where(lane == edge, 1.0, 0.0).astype(BF)
+    whole = jnp.concatenate([head_ref[...], second_ref[...], tail_ref[...]], axis=0).astype(BF)
+    turned = lax.dot_general(pick, whole, (((1,), (1,)), ((), ())), preferred_element_type=F32)
     for side, ref in enumerate((keep_ref, send_ref)):
         for k in range(slots):
-            start = 128 + (me ^ (2 * k + side)) * nb
-            ref[k, 0:tall, :] = lanes_from(start).astype(BF)
-            if nb % 128 == 0:
-                left = tile_at(start - 128)[:, 127:128]
-            else:
-                left = lanes_from(start - 1)[:, 0:1]
-            right = lanes_from(start + nb)[:, 0:1]
-            at = 2 * (side * slots + k)
-            edges = jnp.where(lane_at == at, left, edges)
-            edges = jnp.where(lane_at == at + 1, right, edges)
-    turned = edges.T
-    for side, ref in enumerate((keep_ref, send_ref)):
-        for k in range(slots):
+            ref[k, 0:tall, :] = lanes_from(128 + (me ^ (2 * k + side)) * nb).astype(BF)
             at = 2 * (side * slots + k)
             ref[k, tall : tall + EDGES, :] = jnp.concatenate(
                 [turned[at : at + 2], jnp.zeros((EDGES - 2, 128), F32)], axis=0

time: 35.2 us -> 35.2 us (level)
  no operation moved by 1% of the time
where the time goes in v9:
time: 35.2 us; the launch traced here: 35 us
  Pallas kernels  13.6 us (39%)
  starting transfers between devices  13.2 us (38%)
  waiting for transfers between devices  6.86 us (19%)
  local copies, waits for them, and re-layouts  1.17 us (3%)
    pallas_call x11, Pallas kernels, call(): pl.pallas_call(kernel, out_shape=[jax.ShapeDtypeStruct(*o) for o in outs]...  13.6 us
    ppermute x5, starting transfers between devices, shifted(): lax.ppermute(value, 'row', [(i, (i + by) % peers) for i in range(peers)])  8.93 us
    ppermute x4, waiting for transfers between devices, swapped(): lax.ppermute(value, 'mem', [(i, i ^ by) for i in range(lax.axis_size('mem...  5.44 us
    ppermute x4, starting transfers between devices, swapped(): lax.ppermute(value, 'mem', [(i, i ^ by) for i in range(lax.axis_size('mem...  4.29 us
    ppermute x5, waiting for transfers between devices, shifted(): lax.ppermute(value, 'row', [(i, (i + by) % peers) for i in range(peers)])  1.41 us
    unnamed x14, local copies, waits for them, and re-layouts  1.11 us
  transfers between devices with their start and end apart: 9, of which 5 were waited for; matrix products, arithmetic and copies ran while one was open for 0% of the time, Pallas kernels for 31%

profile of v9, /device:TPU:0, one launch (start us, length us, event | category | flops | bytes accessed | tf_op | source)
XLA Modules:
  0.0 35.0 jit_solution(17076984002347934540)
XLA Ops:
  0.0 0.0 copy-start
  0.0 0.2 shard_map.73
  0.2 1.1 %copy-done = bf16[2,5,16,4096]{3,2,1,0:T(8,128)(2,1)S(1)} copy-done((bf16[2,5,16,4096]{3,2,1,0:T(8,128)(2,1)S(1)}, bf16[2,5,16,4096]{3,2,1,0:T(8,128)(2,1)}, u32[]{:S(2)}) %copy-start) | copy-done | bytes 1310744
  1.3 0.0 copy-start.1
  1.3 0.0 copy-start.2
  1.3 0.0 copy-start.3
  1.3 0.0 copy-start.4
  1.3 0.2 shard_map.74
  1.6 3.9 %collective-permute-start.1 = (bf16[160,512]{1,0:T(8,128)(2,1)S(1)}, bf16[160,512]{1,0:T(8,128)(2,1)S(1)}, u32[]{:S(2)}, u32[]{:S(2)}) collective-permute-start(bf16[160,512]{1,0:T(8,128)(2,1)S(1)} %get-tuple-element.61), channel_id=1, source_target_pairs={{0,3},{1,0},{2,1},{3,2},{4,7},{5,4},{6,5},{7,6},{8,11},{9,8},{10,9... | collective-permute-start | bytes 491528 | tf_op jit(solution)/shard_map/ppermute | solution.py:529
  5.5 0.0 collective-permute-start
  5.5 0.0 copy-done.1
  5.5 0.0 copy-done.2
  5.5 0.0 copy-done.3
  5.5 0.0 copy-done.4
  5.6 5.1 %shard_map.75 = (bf16[1792,2048]{1,0:T(8,128)(2,1)S(1)}, f32[128,2048]{1,0:T(8,128)S(1)}, f32[128,2048]{1,0:T(8,128)S(1)}, f32[128,2048]{1,0:T(8,128)S(1)}, f32[...) custom-call(bf16[160,4096]{1,0:T(8,128)(2,1)S(1)} %bitcast.15, ...), custom_call_target="tpu_custom_call" | custom-call | flops 1000000000 | bytes 3000000 | tf_op jit(solution)/shard_map/pallas_call | solution.py:540
  10.6 0.0 collective-permute-done.1.got_ref
  10.6 1.2 %shard_map.77 = (bf16[128,2048]{1,0:T(8,128)(2,1)S(1)}, bf16[32,1024]{1,0:T(8,128)(2,1)S(1)}) custom-call(bf16[160,512]{1,0:T(8,128)(2,1)S(1)} %collective-permute-done.1.got_ref, bf16[2,256,256]{2,1,0:T(8,128)(2,1)S(1)} %get-tuple-element.49.spread_ref, bf16[256,128]{1,0:T(8,128)(2,1)S(1)} %get-tuple-element.62.w1_ref, ...), custom_call_target="tpu_custom_call" | custom-call | flops 1000000000 | bytes 3000000 | tf_op jit(solution)/shard_map/pallas_call | solution.py:540
  11.9 2.0 %collective-permute-start.2 = (bf16[32,1024]{1,0:T(8,128)(2,1)S(1)}, bf16[32,1024]{1,0:T(8,128)(2,1)S(1)}, u32[]{:S(2)}, u32[]{:S(2)}) collective-permute-start(bf16[32,1024]{1,0:T(8,128)(2,1)S(1)} %get-tuple-element.65), channel_id=1, source_target_pairs={{0,1},{1,2},{2,3},{3,0},{4,5},{5,6},{6,7},{7,4},{8,9},{9,10},{10,1... | collective-permute-start | bytes 196616 | tf_op jit(solution)/shard_map/ppermute | solution.py:529
  13.9 1.6 %shard_map.78.tail_ref = f32[64,1280]{1,0:T(8,128)S(1)} custom-call(bf16[1792,2048]{1,0:T(8,128)(2,1)S(1)} %get-tuple-element.67.h1_ref, bf16[128,2048]{1,0:T(8,128)(2,1)S(1)} %get-tuple-element.68.h2_mid, bf16[128,2048]{1,0:T(8,128)(2,1)S(1)} %get-tuple-element.69.h2_low, bf16[128,768]{1,0:T(8,128)(2,1)S(1)} %get-tuple-element.54.w2_ref, ...), custom_call_target="tpu_custom_call" | custom-call | flops 1000000000 | bytes 3000000 | tf_op jit(solution)/shard_map/pallas_call | solution.py:540
  15.5 0.0 copy-start.6
  15.5 0.0 copy-start.5
  15.5 0.0 collective-permute-done.got_ref
  15.5 1.8 %shard_map.76 = (f32[2,16,1024]{2,1,0:T(8,128)S(1)}, f32[32,1280]{1,0:T(8,128)S(1)}) custom-call(bf16[240,512]{1,0:T(8,128)(2,1)S(1)} %collective-permute-done.got_ref, bf16[2,256,256]{2,1,0:T(8,128)(2,1)S(1)} %get-tuple-element.49.spread_ref, bf16[512,160]{1,0:T(8,128)(2,1)S(1)} %get-tuple-element.52.w1_ref, f32[128,2048]{1,0:T(8,128)S(1)} %get-tuple-element.53.h_ref, ...), custom_call_target="tpu_custom_call" | custom-call | flops 1000000000 | bytes 3000000 | tf_op jit(solution)/shard_map/pallas_call | solution.py:540
  17.3 0.0 collective-permute-done.2.carry_ref
  17.3 0.3 shard_map.79
  17.7 0.1 collective-permute-start.3
  17.7 1.3 %collective-permute-done.3.got_ref = bf16[4,136,128]{2,1,0:T(8,128)(2,1)S(1)} collective-permute-done((bf16[4,136,128]{2,1,0:T(8,128)(2,1)S(1)}, bf16[4,136,128]{2,1,0:T(8,128)(2,1)S(1)}, u32[]{:S(2)}, u32[]{:S(2)}) %collective-permute-start.3) | collective-permute-done | bytes 139296 | tf_op jit(solution)/shard_map/ppermute | solution.py:533
  19.1 2.7 %collective-permute-start.5 = (bf16[136,128]{1,0:T(8,128)(2,1)S(1)}, bf16[136,128]{1,0:T(8,128)(2,1)S(1)}, u32[]{:S(2)}, u32[]{:S(2)}) collective-permute-start(bf16[136,128]{1,0:T(8,128)(2,1)S(1)} %get-tuple-element.75), channel_id=1, source_target_pairs={{0,16},{4,20},{8,24},{12,28},{16,0},{20,4},{24,8},{28,12},{1,17},{... | collective-permute-start | bytes 104456 | tf_op jit(solution)/shard_map/ppermute | solution.py:533
  21.8 1.4 %collective-permute-start.6 = (bf16[136,128]{1,0:T(8,128)(2,1)S(1)}, bf16[136,128]{1,0:T(8,128)(2,1)S(1)}, u32[]{:S(2)}, u32[]{:S(2)}) collective-permute-start(bf16[136,128]{1,0:T(8,128)(2,1)S(1)} %get-tuple-element.76), channel_id=1, source_target_pairs={{0,24},{4,28},{8,16},{12,20},{16,8},{20,12},{24,0},{28,4},{1,25},{... | collective-permute-start | bytes 104456 | tf_op jit(solution)/shard_map/ppermute | solution.py:533
  23.2 0.2 collective-permute-start.4
  23.4 0.0 copy-done.6
  23.4 0.0 copy-done.5
  23.4 1.0 %collective-permute-done.5.refs_1_ = bf16[136,128]{1,0:T(8,128)(2,1)S(1)} collective-permute-done((bf16[136,128]{1,0:T(8,128)(2,1)S(1)}, bf16[136,128]{1,0:T(8,128)(2,1)S(1)}, u32[]{:S(2)}, u32[]{:S(2)}) %collective-permute-start.5) | collective-permute-done | bytes 34848 | tf_op jit(solution)/shard_map/ppermute | solution.py:533
  24.4 3.1 %collective-permute-done.6.refs_2_ = bf16[136,128]{1,0:T(8,128)(2,1)S(1)} collective-permute-done((bf16[136,128]{1,0:T(8,128)(2,1)S(1)}, bf16[136,128]{1,0:T(8,128)(2,1)S(1)}, u32[]{:S(2)}, u32[]{:S(2)}) %collective-permute-start.6) | collective-permute-done | bytes 34848 | tf_op jit(solution)/shard_map/ppermute | solution.py:533
  27.5 0.0 collective-permute-done.4.refs_0_
  27.5 0.2 shard_map.81
  27.7 1.9 %collective-permute-start.7 = (bf16[32,256]{1,0:T(8,128)(2,1)S(1)}, bf16[32,256]{1,0:T(8,128)(2,1)S(1)}, u32[]{:S(2)}, u32[]{:S(2)}) collective-permute-start(bf16[32,256]{1,0:T(8,128)(2,1)S(1)} %get-tuple-element.77), channel_id=1, source_target_pairs={{0,1},{1,2},{2,3},{3,0},{4,5},{5,6},{6,7},{7,4},{8,9},{9,10},{10,1... | collective-permute-start | bytes 49160 | tf_op jit(solution)/shard_map/ppermute | solution.py:529
  29.7 1.0 %collective-permute-start.8 = (bf16[32,256]{1,0:T(8,128)(2,1)S(1)}, bf16[32,256]{1,0:T(8,128)(2,1)S(1)}, u32[]{:S(2)}, u32[]{:S(2)}) collective-permute-start(bf16[32,256]{1,0:T(8,128)(2,1)S(1)} %get-tuple-element.78), channel_id=1, source_target_pairs={{0,3},{1,0},{2,1},{3,2},{4,7},{5,4},{6,5},{7,6},{8,11},{9,8},{10,9... | collective-permute-start | bytes 49160 | tf_op jit(solution)/shard_map/ppermute | solution.py:529
  30.7 1.3 %shard_map.82 = (bf16[2,128,96]{2,1,0:T(8,128)(2,1)S(1)}, bf16[2,256,256]{2,1,0:T(8,128)(2,1)S(1)}, f32[2,128,256]{2,1,0:T(8,128)S(1)}, f32[2,256,128]{2,1,0:T(8...) custom-call(bf16[128,256]{1,0:T(8,128)(2,1)S(1)} %get-tuple-element.79.line_ref, ...), custom_call_target="tpu_custom_call" | custom-call | flops 1000000000 | bytes 3000000 | tf_op jit(solution)/shard_map/pallas_call | solution.py:540
  32.0 0.4 %collective-permute-done.7.first_ref = bf16[32,256]{1,0:T(8,128)(2,1)S(1)} collective-permute-done((bf16[32,256]{1,0:T(8,128)(2,1)S(1)}, bf16[32,256]{1,0:T(8,128)(2,1)S(1)}, u32[]{:S(2)}, u32[]{:S(2)}) %collective-permute-start.7) | collective-permute-done | bytes 16416 | tf_op jit(solution)/shard_map/ppermute | solution.py:529
  32.4 1.0 %collective-permute-done.8.second_ref = bf16[32,256]{1,0:T(8,128)(2,1)S(1)} collective-permute-done((bf16[32,256]{1,0:T(8,128)(2,1)S(1)}, bf16[32,256]{1,0:T(8,128)(2,1)S(1)}, u32[]{:S(2)}, u32[]{:S(2)}) %collective-permute-start.8) | collective-permute-done | bytes 16416 | tf_op jit(solution)/shard_map/ppermute | solution.py:529
  33.4 1.6 %shard_map.83 = bf16[16,16,512]{2,1,0:T(8,128)(2,1)} custom-call(bf16[32,256]{1,0:T(8,128)(2,1)S(1)} %collective-permute-done.7.first_ref, bf16[32,256]{1,0:T(8,128)(2,1)S(1)} %collective-permute-done.8.second_ref, bf16[2,128,96]{2,1,0:T(8,128)(2,1)S(1)} %get-tuple-element.82.w_edge, bf16[2,256,256]{2,1,0:T(8,128)(2,1)S(1)} %get-tuple-element.83.w_field, ...), custom_call_target="tpu_custom_call" | custom-call | flops 1000000000 | bytes 3000000 | tf_op jit(solution)/shard_map/pallas_call | solution.py:540
  (3 shorter events, 0.1 us)
Async XLA Ops:
  0.0 1.3 %copy-start = (bf16[2,5,16,4096]{3,2,1,0:T(8,128)(2,1)S(1)}, bf16[2,5,16,4096]{3,2,1,0:T(8,128)(2,1)}, u32[]{:S(2)}) copy-start(bf16[2,5,16,4096]{3,2,1,0:T(8,128)(2,1)} %param.7) | copy-start | bytes 3932164
  1.3 4.2 %copy-start.1 = (bf16[64,64,3,3]{1,0,3,2:T(8,128)(2,1)S(1)}, bf16[64,64,3,3]{1,0,3,2:T(8,128)(2,1)}, u32[]{:S(2)}) copy-start(bf16[64,64,3,3]{1,0,3,2:T(8,128)(2,1)} %param.9) | copy-start | bytes 221188
  1.3 4.2 %copy-start.2 = (bf16[16,64,3,3]{1,0,3,2:T(8,128)(2,1)S(1)}, bf16[16,64,3,3]{1,0,3,2:T(8,128)(2,1)}, u32[]{:S(2)}) copy-start(bf16[16,64,3,3]{1,0,3,2:T(8,128)(2,1)} %param.10) | copy-start | bytes 55300
  1.3 4.2 %copy-start.3 = (bf16[32,256]{1,0:T(8,128)(2,1)S(1)}, bf16[32,256]{1,0:T(8,128)(2,1)}, u32[]{:S(2)}) copy-start(bf16[32,256]{1,0:T(8,128)(2,1)} %mix_ref.1) | copy-start | bytes 49156
  1.3 4.2 %copy-start.4 = (bf16[64,5,3,3]{0,3,2,1:T(4,128)(2,1)S(1)}, bf16[64,5,3,3]{0,3,2,1:T(4,128)(2,1)}, u32[]{:S(2)}) copy-start(bf16[64,5,3,3]{0,3,2,1:T(4,128)(2,1)} %param.8) | copy-start | bytes 17284
  1.6 9.1 %collective-permute-start.1 = (bf16[160,512]{1,0:T(8,128)(2,1)S(1)}, bf16[160,512]{1,0:T(8,128)(2,1)S(1)}, u32[]{:S(2)}, u32[]{:S(2)}) collective-permute-start(bf16[160,512]{1,0:T(8,128)(2,1)S(1)} %get-tuple-element.61), channel_id=1, source_target_pairs={{0,3},{1,0},{2,1},{3,2},{4,7},{5,4},{6,5},{7,6},{8,11},{9,8},{10,9... | collective-permute-start | bytes 491528 | tf_op jit(solution)/shard_map/ppermute | solution.py:529
  5.5 10.0 %collective-permute-start = (bf16[240,512]{1,0:T(8,128)(2,1)S(1)}, bf16[240,512]{1,0:T(8,128)(2,1)S(1)}, u32[]{:S(2)}, u32[]{:S(2)}) collective-permute-start(bf16[240,512]{1,0:T(8,128)(2,1)S(1)} %get-tuple-element.48), channel_id=1, source_target_pairs={{0,1},{1,2},{2,3},{3,0},{4,5},{5,6},{6,7},{7,4},{8,9},{9,10},{10,1... | collective-permute-start | bytes 737288 | tf_op jit(solution)/shard_map/ppermute | solution.py:529
  11.9 5.4 %collective-permute-start.2 = (bf16[32,1024]{1,0:T(8,128)(2,1)S(1)}, bf16[32,1024]{1,0:T(8,128)(2,1)S(1)}, u32[]{:S(2)}, u32[]{:S(2)}) collective-permute-start(bf16[32,1024]{1,0:T(8,128)(2,1)S(1)} %get-tuple-element.65), channel_id=1, source_target_pairs={{0,1},{1,2},{2,3},{3,0},{4,5},{5,6},{6,7},{7,4},{8,9},{9,10},{10,1... | collective-permute-start | bytes 196616 | tf_op jit(solution)/shard_map/ppermute | solution.py:529
  15.5 7.9 %copy-start.6 = (bf16[16,32,4,4]{1,3,2,0:T(4,128)(2,1)S(1)}, bf16[16,32,4,4]{1,3,2,0:T(4,128)(2,1)}, u32[]{:S(2)}) copy-start(bf16[16,32,4,4]{1,3,2,0:T(4,128)(2,1)} %param.13) | copy-start | bytes 49156
  15.5 7.9 %copy-start.5 = (bf16[32,32,4,4]{1,3,2,0:T(4,128)(2,1)S(1)}, bf16[32,32,4,4]{1,3,2,0:T(4,128)(2,1)}, u32[]{:S(2)}) copy-start(bf16[32,32,4,4]{1,3,2,0:T(4,128)(2,1)} %param.12) | copy-start | bytes 98308
  17.7 1.4 %collective-permute-start.3 = (bf16[4,136,128]{2,1,0:T(8,128)(2,1)S(1)}, bf16[4,136,128]{2,1,0:T(8,128)(2,1)S(1)}, u32[]{:S(2)}, u32[]{:S(2)}) collective-permute-start(bf16[4,136,128]{2,1,0:T(8,128)(2,1)S(1)} %get-tuple-element.72), channel_id=1, source_target_pairs={{0,4},{4,0},{8,12},{12,8},{16,20},{20,16},{24,28},{28,24},{1,5},{5... | collective-permute-start | bytes 417800 | tf_op jit(solution)/shard_map/ppermute | solution.py:533
  19.1 5.3 %collective-permute-start.5 = (bf16[136,128]{1,0:T(8,128)(2,1)S(1)}, bf16[136,128]{1,0:T(8,128)(2,1)S(1)}, u32[]{:S(2)}, u32[]{:S(2)}) collective-permute-start(bf16[136,128]{1,0:T(8,128)(2,1)S(1)} %get-tuple-element.75), channel_id=1, source_target_pairs={{0,16},{4,20},{8,24},{12,28},{16,0},{20,4},{24,8},{28,12},{1,17},{... | collective-permute-start | bytes 104456 | tf_op jit(solution)/shard_map/ppermute | solution.py:533
  21.8 5.7 %collective-permute-start.6 = (bf16[136,128]{1,0:T(8,128)(2,1)S(1)}, bf16[136,128]{1,0:T(8,128)(2,1)S(1)}, u32[]{:S(2)}, u32[]{:S(2)}) collective-permute-start(bf16[136,128]{1,0:T(8,128)(2,1)S(1)} %get-tuple-element.76), channel_id=1, source_target_pairs={{0,24},{4,28},{8,16},{12,20},{16,8},{20,12},{24,0},{28,4},{1,25},{... | collective-permute-start | bytes 104456 | tf_op jit(solution)/shard_map/ppermute | solution.py:533
  23.2 4.4 %collective-permute-start.4 = (bf16[136,128]{1,0:T(8,128)(2,1)S(1)}, bf16[136,128]{1,0:T(8,128)(2,1)S(1)}, u32[]{:S(2)}, u32[]{:S(2)}) collective-permute-start(bf16[136,128]{1,0:T(8,128)(2,1)S(1)} %get-tuple-element.74), channel_id=1, source_target_pairs={{0,8},{4,12},{8,0},{12,4},{16,24},{20,28},{24,16},{28,20},{1,9},{5... | collective-permute-start | bytes 104456 | tf_op jit(solution)/shard_map/ppermute | solution.py:533
  27.7 4.7 %collective-permute-start.7 = (bf16[32,256]{1,0:T(8,128)(2,1)S(1)}, bf16[32,256]{1,0:T(8,128)(2,1)S(1)}, u32[]{:S(2)}, u32[]{:S(2)}) collective-permute-start(bf16[32,256]{1,0:T(8,128)(2,1)S(1)} %get-tuple-element.77), channel_id=1, source_target_pairs={{0,1},{1,2},{2,3},{3,0},{4,5},{5,6},{6,7},{7,4},{8,9},{9,10},{10,1... | collective-permute-start | bytes 49160 | tf_op jit(solution)/shard_map/ppermute | solution.py:529
  29.7 3.7 %collective-permute-start.8 = (bf16[32,256]{1,0:T(8,128)(2,1)S(1)}, bf16[32,256]{1,0:T(8,128)(2,1)S(1)}, u32[]{:S(2)}, u32[]{:S(2)}) collective-permute-start(bf16[32,256]{1,0:T(8,128)(2,1)S(1)} %get-tuple-element.78), channel_id=1, source_target_pairs={{0,3},{1,0},{2,1},{3,2},{4,7},{5,4},{6,5},{7,6},{8,11},{9,8},{10,9... | collective-permute-start | bytes 49160 | tf_op jit(solution)/shard_map/ppermute | solution.py:529
